TPU v7x, 128 devices: a whole 4x4x4 slice. The times are simulated.
128 devices in a mesh: row: 8 (over z, core), col: 16 (over y, x).
Axes of the slice: x: 4, y: 4, z: 4, core: 2. Of those that a mesh axis runs over, the one named last changes fastest.
Arguments:
- amplitudes: float32 [4096, 8192], P(('row', 'col')), may hold values from -6 to 6
- intermediates: float32 [4096, 8192], P(('row', 'col')), may hold values from -0.09375 to 0.09375
Outputs:
- sigma: float32 [8192, 8192], P('row', 'col')
All inputs are finite; a program needn't handle non-finite values.
Results may differ from a plain program's by a relative error of at most 0.00007.
Values sent between devices are 32-bit elements; how exact they have to be, the bound alone decides.
No kernel may reach another device: no remote copies, remote signals or barrier semaphores. Data moves between devices by JAX's collectives and lax.ppermute only.
A program may use at most 128 MiB of HBM per device.

v0:
```python
import jax
import jax.numpy as jnp
from jax import lax
from jax.sharding import PartitionSpec as P


def broadcast(block, axis, holder):
    block = jnp.where(lax.axis_index(axis) == holder, block, jnp.zeros_like(block))
    return lax.psum(block, axis)


def contract(first, second):
    return lax.dot_general(
        first,
        second,
        (((0,), (0,)), ((), ())),
        precision=lax.Precision.HIGHEST,
        preferred_element_type=jnp.float32,
    )


def shards(amplitudes, intermediates):
    amp_grid = lax.all_to_all(amplitudes, "row", split_axis=1, concat_axis=0, tiled=True)
    inter_grid = lax.all_to_all(intermediates, "col", split_axis=1, concat_axis=0, tiled=True)
    rows_count = lax.axis_size("row")
    slab_rows = amp_grid.shape[0] // rows_count
    width_left = amp_grid.shape[1]
    width_right = inter_grid.shape[1]
    initial = jnp.zeros((width_left, width_right), jnp.float32)

    def advance(phase, running):
        section = lax.dynamic_slice_in_dim(amp_grid, phase * slab_rows, slab_rows, 0)
        panel_left = lax.all_gather(section, "col", axis=0, tiled=True)
        panel_right = broadcast(inter_grid, "row", phase)
        return running + contract(panel_left, panel_right)

    result = lax.fori_loop(0, rows_count, advance, initial)
    return result


def solution(mesh):
    in_specs = (P(("row", "col"), None), P(("row", "col"), None))
    out_specs = P("row", "col")
    return jax.shard_map(shards, mesh=mesh, in_specs=in_specs, out_specs=out_specs, check_vma=False)
```

profile of v0, /device:TPU:6, one launch (start us, length us, event | category | flops | bytes accessed | tf_op | source)
XLA Modules:
  0.0 994.6 jit_solution(6099595492000357475)
XLA Ops:
  6.5 2.4 copy.10
  8.9 5.3 all-to-all-start
  14.3 1.1 copy.9
  15.3 14.9 %all-to-all-done = f32[32,8,1024]{2,0,1:T(8,128)S(1)} async-done(((f32[32,8,1024]{2,0,1:T(8,128)}), f32[32,8,1024]{2,0,1:T(8,128)S(1)}, u32[]{:S(2)}, u32[]{:S(2)}) %all-to-all-start) | async-done | bytes 1048608 | tf_op jit(solution)/shard_map/all_to_all | solution.py:23
  30.2 1.0 copy-done.1
  31.2 7.4 all-to-all-start.1
  38.6 14.3 %all-to-all-done.1 = f32[32,16,512]{2,0,1:T(8,128)S(1)} async-done(((f32[32,16,512]{2,0,1:T(8,128)}), f32[32,16,512]{2,0,1:T(8,128)S(1)}, u32[]{:S(2)}, u32[]{:S(2)}) %all-to-all-start.1) | async-done | bytes 1048608 | tf_op jit(solution)/shard_map/all_to_all | solution.py:24
  52.9 933.8 %while.14 = (s32[]{:T(128)}, f32[1024,512]{1,0:T(8,128)S(1)}, f32[256,1024]{1,0:T(8,128)}, f32[512,512]{1,0:T(8,128)S(1)}, s32[]{:T(128)}, /*index=5*/s32[]{:T(128)}, s32[]{:T(128)}, s32[]{:T(128)}, u32[]{:T(128)}, u32[]{:T(128)}) while((s32[]{:T(128)}, f32[1024,512]{1,0:T(8,128)S(1)}, f32[256,1024]{1,0:T(8,128)}, ...), condition=%wide.region_2.3_spmd.clone, body=%wide.region_0.2_spmd.clone.sunk | while | flops 3222798336 | bytes 22675740 | solution.py:37
  52.9 1.1 broadcast_select_fusion.2
  54.1 0.0 all-gather.2.cloned.1.call-start
  54.1 1.6 constant_dynamic-slice_fusion.2
  55.7 60.7 %all-reduce.2.cloned.1.call-done = f32[512,512]{1,0:T(8,128)} async-done(((f32[512,512]{1,0:T(8,128)}), f32[512,512]{1,0:T(8,128)}) %all-reduce.2.cloned.1.call-update) | async-done | bytes 1048592 | tf_op jit(solution)/shard_map/while/body/eval_jaxpr/psum | solution.py:9
  116.5 45.8 %all-gather.2.cloned.1.call-done = f32[512,1024]{1,0:T(8,128)} async-done(((f32[32,1024]{1,0:T(8,128)}), f32[512,1024]{1,0:T(8,128)}) %all-gather.2.cloned.1.call-update) | async-done | bytes 2097168 | tf_op jit(solution)/shard_map/while/body/eval_jaxpr/all_gather | solution.py:33
  162.3 5.7 select_add_fusion.2
  168.0 0.0 all-reduce.2.cloned.1.call-start
  168.1 1.1 broadcast_select_fusion.2
  169.2 0.0 all-gather.2.cloned.1.call-start
  169.3 1.6 constant_dynamic-slice_fusion.2
  170.9 62.8 %all-reduce.2.cloned.1.call-done = f32[512,512]{1,0:T(8,128)} async-done(((f32[512,512]{1,0:T(8,128)}), f32[512,512]{1,0:T(8,128)}) %all-reduce.2.cloned.1.call-update) | async-done | bytes 1048592 | tf_op jit(solution)/shard_map/while/body/eval_jaxpr/psum | solution.py:9
  233.6 45.7 %all-gather.2.cloned.1.call-done = f32[512,1024]{1,0:T(8,128)} async-done(((f32[32,1024]{1,0:T(8,128)}), f32[512,1024]{1,0:T(8,128)}) %all-gather.2.cloned.1.call-update) | async-done | bytes 2097168 | tf_op jit(solution)/shard_map/while/body/eval_jaxpr/all_gather | solution.py:33
  279.3 5.7 select_add_fusion.2
  285.1 0.0 all-reduce.2.cloned.1.call-start
  285.1 1.1 broadcast_select_fusion.2
  286.3 0.0 all-gather.2.cloned.1.call-start
  286.3 1.6 constant_dynamic-slice_fusion.2
  287.9 62.5 %all-reduce.2.cloned.1.call-done = f32[512,512]{1,0:T(8,128)} async-done(((f32[512,512]{1,0:T(8,128)}), f32[512,512]{1,0:T(8,128)}) %all-reduce.2.cloned.1.call-update) | async-done | bytes 1048592 | tf_op jit(solution)/shard_map/while/body/eval_jaxpr/psum | solution.py:9
  350.4 45.7 %all-gather.2.cloned.1.call-done = f32[512,1024]{1,0:T(8,128)} async-done(((f32[32,1024]{1,0:T(8,128)}), f32[512,1024]{1,0:T(8,128)}) %all-gather.2.cloned.1.call-update) | async-done | bytes 2097168 | tf_op jit(solution)/shard_map/while/body/eval_jaxpr/all_gather | solution.py:33
  396.0 5.7 select_add_fusion.2
  401.8 0.0 all-reduce.2.cloned.1.call-start
  401.9 1.1 broadcast_select_fusion.2
  403.0 0.0 all-gather.2.cloned.1.call-start
  403.0 1.6 constant_dynamic-slice_fusion.2
  404.6 62.8 %all-reduce.2.cloned.1.call-done = f32[512,512]{1,0:T(8,128)} async-done(((f32[512,512]{1,0:T(8,128)}), f32[512,512]{1,0:T(8,128)}) %all-reduce.2.cloned.1.call-update) | async-done | bytes 1048592 | tf_op jit(solution)/shard_map/while/body/eval_jaxpr/psum | solution.py:9
  467.4 45.8 %all-gather.2.cloned.1.call-done = f32[512,1024]{1,0:T(8,128)} async-done(((f32[32,1024]{1,0:T(8,128)}), f32[512,1024]{1,0:T(8,128)}) %all-gather.2.cloned.1.call-update) | async-done | bytes 2097168 | tf_op jit(solution)/shard_map/while/body/eval_jaxpr/all_gather | solution.py:33
  513.2 5.7 select_add_fusion.2
  519.0 0.0 all-reduce.2.cloned.1.call-start
  519.0 1.1 broadcast_select_fusion.2
  520.2 0.0 all-gather.2.cloned.1.call-start
  520.2 1.6 constant_dynamic-slice_fusion.2
  521.8 62.8 %all-reduce.2.cloned.1.call-done = f32[512,512]{1,0:T(8,128)} async-done(((f32[512,512]{1,0:T(8,128)}), f32[512,512]{1,0:T(8,128)}) %all-reduce.2.cloned.1.call-update) | async-done | bytes 1048592 | tf_op jit(solution)/shard_map/while/body/eval_jaxpr/psum | solution.py:9
  584.6 45.7 %all-gather.2.cloned.1.call-done = f32[512,1024]{1,0:T(8,128)} async-done(((f32[32,1024]{1,0:T(8,128)}), f32[512,1024]{1,0:T(8,128)}) %all-gather.2.cloned.1.call-update) | async-done | bytes 2097168 | tf_op jit(solution)/shard_map/while/body/eval_jaxpr/all_gather | solution.py:33
  630.2 5.7 select_add_fusion.2
  636.0 0.0 all-reduce.2.cloned.1.call-start
  636.1 1.1 broadcast_select_fusion.2
  637.2 0.0 all-gather.2.cloned.1.call-start
  637.2 1.6 constant_dynamic-slice_fusion.2
  638.8 62.8 %all-reduce.2.cloned.1.call-done = f32[512,512]{1,0:T(8,128)} async-done(((f32[512,512]{1,0:T(8,128)}), f32[512,512]{1,0:T(8,128)}) %all-reduce.2.cloned.1.call-update) | async-done | bytes 1048592 | tf_op jit(solution)/shard_map/while/body/eval_jaxpr/psum | solution.py:9
  701.6 45.7 %all-gather.2.cloned.1.call-done = f32[512,1024]{1,0:T(8,128)} async-done(((f32[32,1024]{1,0:T(8,128)}), f32[512,1024]{1,0:T(8,128)}) %all-gather.2.cloned.1.call-update) | async-done | bytes 2097168 | tf_op jit(solution)/shard_map/while/body/eval_jaxpr/all_gather | solution.py:33
  747.3 5.7 select_add_fusion.2
  753.0 0.0 all-reduce.2.cloned.1.call-start
  753.1 1.1 broadcast_select_fusion.2
  754.2 0.0 all-gather.2.cloned.1.call-start
  754.3 1.6 constant_dynamic-slice_fusion.2
  755.9 62.8 %all-reduce.2.cloned.1.call-done = f32[512,512]{1,0:T(8,128)} async-done(((f32[512,512]{1,0:T(8,128)}), f32[512,512]{1,0:T(8,128)}) %all-reduce.2.cloned.1.call-update) | async-done | bytes 1048592 | tf_op jit(solution)/shard_map/while/body/eval_jaxpr/psum | solution.py:9
  818.6 45.7 %all-gather.2.cloned.1.call-done = f32[512,1024]{1,0:T(8,128)} async-done(((f32[32,1024]{1,0:T(8,128)}), f32[512,1024]{1,0:T(8,128)}) %all-gather.2.cloned.1.call-update) | async-done | bytes 2097168 | tf_op jit(solution)/shard_map/while/body/eval_jaxpr/all_gather | solution.py:33
  864.3 5.7 select_add_fusion.2
  870.1 0.0 all-reduce.2.cloned.1.call-start
  870.1 1.1 broadcast_select_fusion.2
  871.2 0.0 all-gather.2.cloned.1.call-start
  871.3 1.6 constant_dynamic-slice_fusion.2
  872.9 62.5 %all-reduce.2.cloned.1.call-done = f32[512,512]{1,0:T(8,128)} async-done(((f32[512,512]{1,0:T(8,128)}), f32[512,512]{1,0:T(8,128)}) %all-reduce.2.cloned.1.call-update) | async-done | bytes 1048592 | tf_op jit(solution)/shard_map/while/body/eval_jaxpr/psum | solution.py:9
  935.3 45.7 %all-gather.2.cloned.1.call-done = f32[512,1024]{1,0:T(8,128)} async-done(((f32[32,1024]{1,0:T(8,128)}), f32[512,1024]{1,0:T(8,128)}) %all-gather.2.cloned.1.call-update) | async-done | bytes 2097168 | tf_op jit(solution)/shard_map/while/body/eval_jaxpr/all_gather | solution.py:33
  981.0 5.7 select_add_fusion.2
  986.8 1.3 copy-done
  (22 shorter events, 0.3 us)
Async XLA Ops:
  6.5 7.7 copy-start.2
  8.9 21.3 %all-to-all-start = ((f32[32,8,1024]{2,0,1:T(8,128)}), f32[32,8,1024]{2,0,1:T(8,128)S(1)}, u32[]{:S(2)}, u32[]{:S(2)}) async-start(f32[32,8,1024]{2,0,1:T(8,128)} %bitcast.15), calls=%async_computation | async-start | bytes 2097152 | tf_op jit(solution)/shard_map/all_to_all | solution.py:23
  30.2 1.0 copy-start.1
  31.2 21.8 %all-to-all-start.1 = ((f32[32,16,512]{2,0,1:T(8,128)}), f32[32,16,512]{2,0,1:T(8,128)S(1)}, u32[]{:S(2)}, u32[]{:S(2)}) async-start(f32[32,16,512]{2,0,1:T(8,128)} %bitcast.14), calls=%async_computation.1 | async-start | bytes 2097152 | tf_op jit(solution)/shard_map/all_to_all | solution.py:24
  52.9 63.5 %all-reduce.2.cloned.1.call-start = ((), (), s32[]{:S(2)}) async-start(), calls=%async_computation.3 | async-start | bytes 2097152 | tf_op jit(solution)/shard_map/while/body/eval_jaxpr/psum | solution.py:9
  54.1 108.2 %all-gather.2.cloned.1.call-start = ((), (), s32[]{:S(2)}) async-start(), calls=%async_computation.2 | async-start | bytes 2228224 | tf_op jit(solution)/shard_map/while/body/eval_jaxpr/all_gather | solution.py:33
  168.0 65.6 %all-reduce.2.cloned.1.call-start = ((), (), s32[]{:S(2)}) async-start(), calls=%async_computation.3 | async-start | bytes 2097152 | tf_op jit(solution)/shard_map/while/body/eval_jaxpr/psum | solution.py:9
  169.2 110.1 %all-gather.2.cloned.1.call-start = ((), (), s32[]{:S(2)}) async-start(), calls=%async_computation.2 | async-start | bytes 2228224 | tf_op jit(solution)/shard_map/while/body/eval_jaxpr/all_gather | solution.py:33
  285.1 65.3 %all-reduce.2.cloned.1.call-start = ((), (), s32[]{:S(2)}) async-start(), calls=%async_computation.3 | async-start | bytes 2097152 | tf_op jit(solution)/shard_map/while/body/eval_jaxpr/psum | solution.py:9
  286.3 109.8 %all-gather.2.cloned.1.call-start = ((), (), s32[]{:S(2)}) async-start(), calls=%async_computation.2 | async-start | bytes 2228224 | tf_op jit(solution)/shard_map/while/body/eval_jaxpr/all_gather | solution.py:33
  401.8 65.6 %all-reduce.2.cloned.1.call-start = ((), (), s32[]{:S(2)}) async-start(), calls=%async_computation.3 | async-start | bytes 2097152 | tf_op jit(solution)/shard_map/while/body/eval_jaxpr/psum | solution.py:9
  403.0 110.2 %all-gather.2.cloned.1.call-start = ((), (), s32[]{:S(2)}) async-start(), calls=%async_computation.2 | async-start | bytes 2228224 | tf_op jit(solution)/shard_map/while/body/eval_jaxpr/all_gather | solution.py:33
  519.0 65.6 %all-reduce.2.cloned.1.call-start = ((), (), s32[]{:S(2)}) async-start(), calls=%async_computation.3 | async-start | bytes 2097152 | tf_op jit(solution)/shard_map/while/body/eval_jaxpr/psum | solution.py:9
  520.2 110.1 %all-gather.2.cloned.1.call-start = ((), (), s32[]{:S(2)}) async-start(), calls=%async_computation.2 | async-start | bytes 2228224 | tf_op jit(solution)/shard_map/while/body/eval_jaxpr/all_gather | solution.py:33
  636.0 65.6 %all-reduce.2.cloned.1.call-start = ((), (), s32[]{:S(2)}) async-start(), calls=%async_computation.3 | async-start | bytes 2097152 | tf_op jit(solution)/shard_map/while/body/eval_jaxpr/psum | solution.py:9
  637.2 110.1 %all-gather.2.cloned.1.call-start = ((), (), s32[]{:S(2)}) async-start(), calls=%async_computation.2 | async-start | bytes 2228224 | tf_op jit(solution)/shard_map/while/body/eval_jaxpr/all_gather | solution.py:33
  753.0 65.6 %all-reduce.2.cloned.1.call-start = ((), (), s32[]{:S(2)}) async-start(), calls=%async_computation.3 | async-start | bytes 2097152 | tf_op jit(solution)/shard_map/while/body/eval_jaxpr/psum | solution.py:9
  754.2 110.1 %all-gather.2.cloned.1.call-start = ((), (), s32[]{:S(2)}) async-start(), calls=%async_computation.2 | async-start | bytes 2228224 | tf_op jit(solution)/shard_map/while/body/eval_jaxpr/all_gather | solution.py:33
  870.1 65.3 %all-reduce.2.cloned.1.call-start = ((), (), s32[]{:S(2)}) async-start(), calls=%async_computation.3 | async-start | bytes 2097152 | tf_op jit(solution)/shard_map/while/body/eval_jaxpr/psum | solution.py:9
  871.2 109.8 %all-gather.2.cloned.1.call-start = ((), (), s32[]{:S(2)}) async-start(), calls=%async_computation.2 | async-start | bytes 2228224 | tf_op jit(solution)/shard_map/while/body/eval_jaxpr/all_gather | solution.py:33
  986.8 1.3 copy-start
Sparse Core Ops, SparseCore 0:
  56.1 60.3 all-reduce.1
  118.6 43.6 all-gather.1
  171.2 62.3 all-reduce.1
  235.6 43.6 all-gather.1
  288.0 62.3 all-reduce.1
  352.4 43.6 all-gather.1
  405.0 62.3 all-reduce.1
  469.5 43.6 all-gather.1
  522.2 62.3 all-reduce.1
  586.6 43.6 all-gather.1
  639.2 62.3 all-reduce.1
  703.6 43.6 all-gather.1
  756.2 62.3 all-reduce.1
  820.6 43.6 all-gather.1
  872.9 62.3 all-reduce.1
  937.3 43.6 all-gather.1
where the time goes:
time: 996 us; the launch traced here: 995 us
  waiting for transfers between devices  895 us (90%)
  matrix products  46 us (5%)
  local copies, waits for them, and re-layouts  18.3 us (2%)
  starting transfers between devices  13.4 us (1%)
  between operations  13.1 us (1%)
    psum x8, waiting for transfers between devices, broadcast(): return lax.psum(block, axis)  499 us
    all_gather x8, waiting for transfers between devices, advance(): panel_left = lax.all_gather(section, 'col', axis=0, tiled=True)  366 us
    dot_general x8, matrix products, contract(): lax.dot_general(first, second, (((0,), (0,)), ((), ())), precision=lax.Pr...  46 us
  transfers between devices with their start and end apart: 18, of which 18 were waited for; matrix products, arithmetic and copies ran while one was open for 1% of the time, Pallas kernels for 0%

commit v1 on v0

v1 whole, which is shorter than its diff:
```python
import functools

import jax
import jax.numpy as jnp
from jax import lax
from jax.experimental import pallas as pl
from jax.experimental.pallas import tpu as pltpu
from jax.sharding import Mesh, PartitionSpec as P

N = 4
ALL = ("z", "c", "y", "x")
VMEM_LIMIT = 48 * 1024 * 1024


def shift(value, axis, step):
    return lax.ppermute(value, axis, [(i, (i + step) % N) for i in range(N)])


def split(value):
    high = value.astype(jnp.bfloat16)
    low = (value - high.astype(jnp.float32)).astype(jnp.bfloat16)
    return high, low


def dot(first, second):
    return lax.dot_general(
        first, second, (((1,), (0,)), ((), ())), preferred_element_type=jnp.float32
    )


def arrange_kernel(place, b_ref, x_ref, y_ref):
    half = x_ref.shape[2] // N
    for dy in range(N):
        for dx in range(N):
            block = lax.rem(place[0] + dy, N) * N + lax.rem(place[1] + dx, N)
            first = pl.multiple_of(block * 2 * half, 2 * half)
            x_ref[dy, :, dx * half : (dx + 1) * half] = b_ref[:, pl.ds(first, half)]
            second = pl.multiple_of(first + half, half)
            y_ref[dx, :, dy * half : (dy + 1) * half] = b_ref[:, pl.ds(second, half)]


def arrange(b, place):
    rows, columns = b.shape
    out = jax.ShapeDtypeStruct((N, rows, columns // (2 * N)), b.dtype)
    return pl.pallas_call(
        arrange_kernel,
        out_shape=(out, out),
        in_specs=[
            pl.BlockSpec(memory_space=pltpu.SMEM),
            pl.BlockSpec(memory_space=pltpu.VMEM),
        ],
        out_specs=(pl.BlockSpec(memory_space=pltpu.VMEM),) * 2,
        compiler_params=pltpu.CompilerParams(vmem_limit_bytes=VMEM_LIMIT),
        name="arrange",
    )(place, b)


def product_kernel(steps, has_start, *refs):
    count = len(steps)
    a_refs, refs = refs[:count], refs[count:]
    b_ref, refs = refs[0], refs[1:]
    start_ref, refs = (refs[0], refs[1:]) if has_start else (None, refs)
    out_ref, high_ref, low_ref = refs

    @pl.when(pl.program_id(0) == 0)
    def _():
        for i in range(count):
            high_ref[i], low_ref[i] = split(a_refs[i][...])

    depth = a_refs[0].shape[1]
    total = start_ref[0] if has_start else None
    for i, step in enumerate(steps):
        block = b_ref[:, step].reshape(depth, b_ref.shape[3])
        high, low = split(block)
        term = dot(high_ref[i], high) + dot(high_ref[i], low) + dot(low_ref[i], high)
        total = term if total is None else total + term
    out_ref[0] = total


def product(blocks, steps, b, start=None):
    rows, depth = blocks[0].shape
    ranks, _, slab, columns = b.shape
    width = columns // N
    operands = list(blocks) + [b]
    in_specs = [pl.BlockSpec((rows, depth), lambda r: (0, 0)) for _ in blocks]
    in_specs.append(pl.BlockSpec((ranks, N, slab, width), lambda r: (0, 0, 0, r)))
    if start is not None:
        operands.append(start)
        in_specs.append(pl.BlockSpec((1, rows, width), lambda r: (r, 0, 0)))
    flops = 6 * rows * depth * len(blocks) * columns
    return pl.pallas_call(
        functools.partial(product_kernel, tuple(steps), start is not None),
        grid=(N,),
        out_shape=jax.ShapeDtypeStruct((N, rows, width), jnp.float32),
        in_specs=in_specs,
        out_specs=pl.BlockSpec((1, rows, width), lambda r: (r, 0, 0)),
        scratch_shapes=[pltpu.VMEM((len(blocks), rows, depth), jnp.bfloat16)] * 2,
        compiler_params=pltpu.CompilerParams(vmem_limit_bytes=VMEM_LIMIT),
        cost_estimate=pl.CostEstimate(
            flops=flops, bytes_accessed=4 * rows * columns * 2, transcendentals=0
        ),
        name="product",
    )(*operands)


def gather_a(own, axis):
    half = own.shape[0] // 2
    behind = shift(own, axis, 1)
    ahead = shift(own, axis, -1)
    top = shift(behind[:half], axis, 1)
    bottom = shift(ahead[half:], axis, -1)
    return behind, ahead, jnp.concatenate([top, bottom], 0)


def reduce_c(part, axis):
    half = part.shape[1] // 2
    top = shift(part[2, :half], axis, 1)
    bottom = shift(part[2, half:], axis, -1)
    forward = jnp.concatenate([part[1, :half] + top, part[1, half:]], 0)
    backward = jnp.concatenate([part[3, :half], part[3, half:] + bottom], 0)
    return part[0] + (shift(forward, axis, 1) + shift(backward, axis, -1))


def scatter_b(blocks, axis):
    return [blocks[0]] + [shift(blocks[d], axis, d) for d in range(1, N)]


def gather_b(blocks):
    block = jnp.stack(blocks, 0)
    return lax.all_gather(block, ("z", "c"), axis=0, tiled=False)


def shards(a, b):
    place = jnp.stack([lax.axis_index("y"), lax.axis_index("x")]).astype(jnp.int32)
    bx, by = arrange(b, place)
    bx = scatter_b(bx, "y")
    by = scatter_b(by, "x")
    az = lax.all_to_all(a, ("z", "c"), split_axis=1, concat_axis=0, tiled=True)
    own = az.T
    panel_x = gather_b(bx)
    panel_y = gather_b(by)
    outs = []
    for axis, along, panel in (("y", "x", panel_x), ("x", "y", panel_y)):
        behind, ahead, far = gather_a(own, axis)
        part = product([own, behind, ahead], (0, 1, 3), panel)
        part = product([far], (2,), panel, part)
        outs.append(reduce_c(part, along))
    return jnp.concatenate(outs, 1)


def solution(mesh):
    fine = Mesh(mesh.devices.reshape(N, 2, N, N), ALL)
    return jax.shard_map(
        shards,
        mesh=fine,
        in_specs=(P(ALL, None), P(ALL, None)),
        out_specs=P(("z", "c"), ("y", "x")),
        check_vma=False,
    )
```

time: 996 us -> 192 us (0.19)
  waiting for transfers between devices: 895 us -> 71.2 us
  matrix products: 46 us -> 0 us
  blocking collectives: 0 us -> 31.5 us
  Pallas kernels: 0 us -> 28.1 us
  starting transfers between devices: 13.4 us -> 31.1 us
    psum x8 -> x0, waiting for transfers between devices: 499 us -> none  [broadcast(): return lax.psum(block, axis)]
    all_gather x8 -> x2, waiting for transfers between devices: 366 us -> 0.02 us  [gather_b(): return lax.all_gather(block, ('z', 'c'), axis=0, tiled=False)]
    ppermute x0 -> x22, waiting for transfers between devices: none -> 71.2 us  [shift(): return lax.ppermute(value, axis, [(i, (i + step) % N) for i in range(N)])]
    dot_general x8 -> x0, matrix products: 46 us -> none  [contract(): lax.dot_general(first, second, (((0,), (0,)), ((), ())), precision=lax.Pr...]
    all_to_all x0 -> x1, blocking collectives: none -> 31.5 us  [shards(): az = lax.all_to_all(a, ('z', 'c'), split_axis=1, concat_axis=0, tiled=True)]
    ppermute x0 -> x22, starting transfers between devices: none -> 31.1 us  [shift(): return lax.ppermute(value, axis, [(i, (i + step) % N) for i in range(N)])]
    all_to_all x2 -> x0, waiting for transfers between devices: 29.2 us -> none  [the longest x1 14.9 us: shards(): lax.all_to_all(amplitudes, 'row', split_axis=1, concat_axis=0, tiled=True)]
    pallas_call x0 -> x5, Pallas kernels: none -> 28.1 us  [the longest x4 27.5 us: product(): pl.pallas_call(functools.partial(product_kernel, tuple(steps), start is n...]
  transfers between devices with their start and end apart: 18 -> 24, of which waited for: 18 -> 13; matrix products, arithmetic and copies ran while one was open for 1% -> 3% of each run, Pallas kernels for 0% -> 14%
where the time goes in v1:
time: 192 us; the launch traced here: 190 us
  waiting for transfers between devices  71.2 us (37%)
  blocking collectives  31.5 us (16%)
  starting transfers between devices  31.1 us (16%)
  Pallas kernels  28.1 us (15%)
  between operations  13.7 us (7%)
  local copies, waits for them, and re-layouts  9.06 us (5%)
  other arithmetic  5.64 us (3%)
    ppermute x22, waiting for transfers between devices, shift(): return lax.ppermute(value, axis, [(i, (i + step) % N) for i in range(N)])  71.2 us
    all_to_all x1, blocking collectives, shards(): az = lax.all_to_all(a, ('z', 'c'), split_axis=1, concat_axis=0, tiled=True)  31.5 us
    ppermute x22, starting transfers between devices, shift(): return lax.ppermute(value, axis, [(i, (i + step) % N) for i in range(N)])  31.1 us
    pallas_call x4, Pallas kernels, product(): pl.pallas_call(functools.partial(product_kernel, tuple(steps), start is n...  27.5 us
    unnamed x28, local copies, waits for them, and re-layouts  6.94 us
  transfers between devices with their start and end apart: 24, of which 13 were waited for; matrix products, arithmetic and copies ran while one was open for 3% of the time, Pallas kernels for 14%

profile of v1, /device:TPU:6, one launch (start us, length us, event | category | flops | bytes accessed | tf_op | source)
XLA Modules:
  0.0 190.3 jit_solution(13126584195020102105)
XLA Ops:
  6.5 0.1 pad_add_fusion.place
  6.6 1.2 copy-done.2
  7.8 0.6 arrange.1
  8.5 3.1 %collective-permute-start.6 = (f32[32,1024]{1,0:T(8,128)S(1)}, f32[32,1024]{1,0:T(8,128)S(1)}, u32[]{:S(2)}, u32[]{:S(2)}) collective-permute-start(f32[32,1024]{1,0:T(8,128)S(1)} %get-tuple-element.22), channel_id=1, source_target_pairs={{0,12},{4,0},{8,4},{12,8},{1,13},{5,1},{9,5},{13,9},{2,14},{6,2},{... | collective-permute-start | bytes 393224 | tf_op jit(solution)/shard_map/ppermute | solution.py:16
  11.6 2.2 %collective-permute-start.5 = (f32[32,1024]{1,0:T(8,128)S(1)}, f32[32,1024]{1,0:T(8,128)S(1)}, u32[]{:S(2)}, u32[]{:S(2)}) collective-permute-start(f32[32,1024]{1,0:T(8,128)S(1)} %get-tuple-element.23), channel_id=1, source_target_pairs={{0,8},{4,12},{8,0},{12,4},{1,9},{5,13},{9,1},{13,5},{2,10},{6,14},... | collective-permute-start | bytes 393224 | tf_op jit(solution)/shard_map/ppermute | solution.py:16
  13.8 0.5 collective-permute-done.6
  14.4 6.2 %collective-permute-done.4 = f32[32,1024]{1,0:T(8,128)S(1)} collective-permute-done((f32[32,1024]{1,0:T(8,128)S(1)}, f32[32,1024]{1,0:T(8,128)S(1)}, u32[]{:S(2)}, u32[]{:S(2)}) %collective-permute-start.4) | collective-permute-done | bytes 131104 | tf_op jit(solution)/shard_map/ppermute | solution.py:16
  20.6 0.8 pad_maximum_fusion.7
  21.4 0.0 all-gather.7.cloned.1.call-start
  21.5 0.5 collective-permute-start.15
  22.1 2.4 %collective-permute-start.16 = (f32[32,1024]{1,0:T(8,128)S(1)}, f32[32,1024]{1,0:T(8,128)S(1)}, u32[]{:S(2)}, u32[]{:S(2)}) collective-permute-start(f32[32,1024]{1,0:T(8,128)S(1)} %get-tuple-element.27), channel_id=1, source_target_pairs={{0,2},{1,3},{2,0},{3,1},{4,6},{5,7},{6,4},{7,5},{8,10},{9,11},{10,... | collective-permute-start | bytes 393224 | tf_op jit(solution)/shard_map/ppermute | solution.py:16
  24.5 3.1 %collective-permute-done.15 = f32[32,1024]{1,0:T(8,128)S(1)} collective-permute-done((f32[32,1024]{1,0:T(8,128)S(1)}, f32[32,1024]{1,0:T(8,128)S(1)}, u32[]{:S(2)}, u32[]{:S(2)}) %collective-permute-start.15) | collective-permute-done | bytes 131104 | tf_op jit(solution)/shard_map/ppermute | solution.py:16
  27.6 2.3 %collective-permute-done.16 = f32[32,1024]{1,0:T(8,128)S(1)} collective-permute-done((f32[32,1024]{1,0:T(8,128)S(1)}, f32[32,1024]{1,0:T(8,128)S(1)}, u32[]{:S(2)}, u32[]{:S(2)}) %collective-permute-start.16) | collective-permute-done | bytes 131104 | tf_op jit(solution)/shard_map/ppermute | solution.py:16
  29.9 1.3 collective-permute-done.17
  31.2 0.8 pad_maximum_fusion.8
  32.0 0.1 copy.11
  32.1 31.5 %all_to_all.19 = f32[32,8,1024]{2,0,1:T(8,128)S(1)} all-to-all(f32[32,8,1024]{2,0,1:T(8,128)S(1)} %bitcast.81), channel_id=1, replica_groups=mesh['z'=4,'c'=2,'y'=4,'x'=4] {'z','c'}, dimensions={1} | all-to-all | bytes 2097152 | tf_op jit(solution)/shard_map/all_to_all | solution.py:138
  63.6 0.3 copy.8
  63.9 0.1 collective-permute-start
  64.0 3.2 %collective-permute-start.2 = (f32[1024,256]{1,0:T(8,128)S(1)}, f32[1024,256]{1,0:T(8,128)S(1)}, u32[]{:S(2)}, u32[]{:S(2)}) collective-permute-start(f32[1024,256]{1,0:T(8,128)S(1)} %bitcast.71), channel_id=1, source_target_pairs={{0,12},{4,0},{8,4},{12,8},{1,13},{5,1},{9,5},{13,9},{2,14},{6,2},{... | collective-permute-start | bytes 3145736 | tf_op jit(solution)/shard_map/ppermute | solution.py:16
  67.2 0.5 collective-permute-start.11
  67.7 1.5 collective-permute-start.13
  69.2 20.9 %collective-permute-done.refs_1_ = f32[1024,256]{1,0:T(8,128)S(1)} collective-permute-done((f32[1024,256]{1,0:T(8,128)S(1)}, f32[1024,256]{1,0:T(8,128)S(1)}, u32[]{:S(2)}, u32[]{:S(2)}) %collective-permute-start) | collective-permute-done | bytes 1048608 | tf_op jit(solution)/shard_map/ppermute | solution.py:16
  90.2 0.1 collective-permute-start.1
  90.4 3.3 %collective-permute-start.3 = (f32[512,256]{1,0:T(8,128)S(1)}, f32[512,256]{1,0:T(8,128)S(1)}, u32[]{:S(2)}, u32[]{:S(2)}) collective-permute-start(f32[512,256]{1,0:T(8,128)S(1)} %slice.105), channel_id=1, source_target_pairs={{0,12},{4,0},{8,4},{12,8},{1,13},{5,1},{9,5},{13,9},{2,14},{6,2},{... | collective-permute-start | bytes 1572872 | tf_op jit(solution)/shard_map/ppermute | solution.py:16
  93.7 0.6 collective-permute-start.12
  94.3 1.5 collective-permute-start.14
  95.9 8.6 %collective-permute-done.1 = f32[512,256]{1,0:T(8,128)S(1)} collective-permute-done((f32[512,256]{1,0:T(8,128)S(1)}, f32[512,256]{1,0:T(8,128)S(1)}, u32[]{:S(2)}, u32[]{:S(2)}) %collective-permute-start.1) | collective-permute-done | bytes 524320 | tf_op jit(solution)/shard_map/ppermute | solution.py:16
  104.5 0.1 pad_maximum_fusion.1.refs_0_
  104.6 1.6 collective-permute-done.12
  106.2 1.6 collective-permute-done.14
  107.8 0.1 pad_maximum_fusion.4.refs_0_
  107.9 0.0 all-gather.5.cloned.1.call-done
  107.9 1.2 copy-done.8
  109.1 1.2 copy-done.10
  110.3 8.5 %product.4.refs_2_ = f32[4,1024,256]{2,1,0:T(8,128)} custom-call(f32[1024,256]{1,0:T(8,128)S(1)} %bitcast.74, f32[1024,256]{1,0:T(8,128)S(1)} %copy-done.8, f32[1024,256]{1,0:T(8,128)S(1)} %copy-done.10, f32[8,4,32,1024]{3,2,1,0:T(8,128)} %bitcast.76), custom_call_target="tpu_custom_call" | custom-call | flops 4831838208 | bytes 8388608 | tf_op jit(solution)/shard_map/product/pallas_call | solution.py:91
  118.9 5.2 %product.5 = f32[4,1024,256]{2,1,0:T(8,128)S(1)} custom-call(f32[1024,256]{1,0:T(8,128)S(1)} %pad_maximum_fusion.1.refs_0_, f32[8,4,32,1024]{3,2,1,0:T(8,128)} %bitcast.77, f32[4,1024,256]{2,1,0:T(8,128)} %product.4.refs_2_), custom_call_target="tpu_custom_call" | custom-call | flops 1610612736 | bytes 8388608 | tf_op jit(solution)/shard_map/product/pallas_call | solution.py:91
  124.1 2.0 %copy-done = f32[4,1024,256]{2,1,0:T(8,128)} copy-done((f32[4,1024,256]{2,1,0:T(8,128)}, f32[4,1024,256]{2,1,0:T(8,128)S(1)}, u32[]{:S(2)}) %copy-start) | copy-done | bytes 4194328
  126.1 1.4 slice_bitcast_fusion.10
  127.5 0.3 collective-permute-start.7
  127.7 1.8 collective-permute-start.9
  129.5 1.2 copy-done.6
  130.7 8.5 %product.6.refs_2_ = f32[4,1024,256]{2,1,0:T(8,128)} custom-call(f32[1024,256]{1,0:T(8,128)S(1)} %bitcast.75, f32[1024,256]{1,0:T(8,128)S(1)} %copy-done.4, f32[1024,256]{1,0:T(8,128)S(1)} %copy-done.6, f32[8,4,32,1024]{3,2,1,0:T(8,128)} %bitcast.78), custom_call_target="tpu_custom_call" | custom-call | flops 4831838208 | bytes 8388608 | tf_op jit(solution)/shard_map/product/pallas_call | solution.py:91
  139.3 5.2 %product.7 = f32[4,1024,256]{2,1,0:T(8,128)S(1)} custom-call(f32[1024,256]{1,0:T(8,128)S(1)} %pad_maximum_fusion.4.refs_0_, f32[8,4,32,1024]{3,2,1,0:T(8,128)} %bitcast.79, f32[4,1024,256]{2,1,0:T(8,128)} %product.6.refs_2_), custom_call_target="tpu_custom_call" | custom-call | flops 1610612736 | bytes 8388608 | tf_op jit(solution)/shard_map/product/pallas_call | solution.py:91
  144.5 0.1 slice_bitcast_fusion.4
  144.7 0.1 collective-permute-start.18
  144.7 3.2 %collective-permute-start.20 = (f32[512,256]{1,0:T(8,128)S(1)}, f32[512,256]{1,0:T(8,128)S(1)}, u32[]{:S(2)}, u32[]{:S(2)}) collective-permute-start(f32[512,256]{1,0:T(8,128)S(1)} %get-tuple-element.16), channel_id=1, source_target_pairs={{0,12},{4,0},{8,4},{12,8},{1,13},{5,1},{9,5},{13,9},{2,14},{6,2},{... | collective-permute-start | bytes 1572872 | tf_op jit(solution)/shard_map/ppermute | solution.py:16
  148.0 1.3 fusion.4
  149.3 0.1 pad_maximum_fusion.3
  149.4 0.3 collective-permute-start.10
  149.7 0.1 pad_maximum_fusion.2
  149.8 3.0 %collective-permute-start.8 = (f32[1024,256]{1,0:T(8,128)S(1)}, f32[1024,256]{1,0:T(8,128)S(1)}, u32[]{:S(2)}, u32[]{:S(2)}) collective-permute-start(f32[1024,256]{1,0:T(8,128)S(1)} %pad_maximum_fusion.2), channel_id=1, source_target_pairs={{0,1},{1,2},{2,3},{3,0},{4,5},{5,6},{6,7},{7,4},{8,9},{9,10},{10,1... | collective-permute-start | bytes 3145736 | tf_op jit(solution)/shard_map/ppermute | solution.py:16
  152.8 3.8 %collective-permute-done.18 = f32[512,256]{1,0:T(8,128)S(1)} collective-permute-done((f32[512,256]{1,0:T(8,128)S(1)}, f32[512,256]{1,0:T(8,128)S(1)}, u32[]{:S(2)}, u32[]{:S(2)}) %collective-permute-start.18) | collective-permute-done | bytes 524320 | tf_op jit(solution)/shard_map/ppermute | solution.py:16
  156.6 0.1 fusion.2
  156.8 0.1 pad_maximum_fusion.6
  156.8 3.2 %collective-permute-start.21 = (f32[1024,256]{1,0:T(8,128)S(1)}, f32[1024,256]{1,0:T(8,128)S(1)}, u32[]{:S(2)}, u32[]{:S(2)}) collective-permute-start(f32[1024,256]{1,0:T(8,128)S(1)} %pad_maximum_fusion.6), channel_id=1, source_target_pairs={{0,12},{4,0},{8,4},{12,8},{1,13},{5,1},{9,5},{13,9},{2,14},{6,2},{... | collective-permute-start | bytes 3145736 | tf_op jit(solution)/shard_map/ppermute | solution.py:16
  160.1 0.1 pad_maximum_fusion.5
  160.1 0.1 collective-permute-start.19
  160.2 11.8 %collective-permute-done.10 = f32[1024,256]{1,0:T(8,128)S(1)} collective-permute-done((f32[1024,256]{1,0:T(8,128)S(1)}, f32[1024,256]{1,0:T(8,128)S(1)}, u32[]{:S(2)}, u32[]{:S(2)}) %collective-permute-start.10) | collective-permute-done | bytes 1048608 | tf_op jit(solution)/shard_map/ppermute | solution.py:16
  172.0 0.2 fusion.1
  172.3 6.1 %collective-permute-done.21 = f32[1024,256]{1,0:T(8,128)S(1)} collective-permute-done((f32[1024,256]{1,0:T(8,128)S(1)}, f32[1024,256]{1,0:T(8,128)S(1)}, u32[]{:S(2)}, u32[]{:S(2)}) %collective-permute-start.21) | collective-permute-done | bytes 1048608 | tf_op jit(solution)/shard_map/ppermute | solution.py:16
  178.4 3.3 %collective-permute-done.19 = f32[1024,256]{1,0:T(8,128)S(1)} collective-permute-done((f32[1024,256]{1,0:T(8,128)S(1)}, f32[1024,256]{1,0:T(8,128)S(1)}, u32[]{:S(2)}, u32[]{:S(2)}) %collective-permute-start.19) | collective-permute-done | bytes 1048608 | tf_op jit(solution)/shard_map/ppermute | solution.py:16
  181.7 0.2 fusion
  181.9 1.6 pad_maximum_fusion
  (44 shorter events, 0.3 us)
Async XLA Ops:
  6.5 101.3 %all-gather.5.cloned.1.call-start = ((), (), s32[]{:S(2)}) async-start(), calls=%async_computation.1 | async-start | bytes 4718592 | tf_op jit(solution)/shard_map/all_gather | solution.py:130
  6.6 1.2 copy-start.2
  7.8 24.2 %copy-start.13 = (f32[32,8192]{1,0:T(8,128)S(1)}, f32[32,8192]{1,0:T(8,128)}, u32[]{:S(2)}) copy-start(f32[32,8192]{1,0:T(8,128)} %param.2) | copy-start | bytes 3145732
  8.5 5.8 %collective-permute-start.6 = (f32[32,1024]{1,0:T(8,128)S(1)}, f32[32,1024]{1,0:T(8,128)S(1)}, u32[]{:S(2)}, u32[]{:S(2)}) collective-permute-start(f32[32,1024]{1,0:T(8,128)S(1)} %get-tuple-element.22), channel_id=1, source_target_pairs={{0,12},{4,0},{8,4},{12,8},{1,13},{5,1},{9,5},{13,9},{2,14},{6,2},{... | collective-permute-start | bytes 393224 | tf_op jit(solution)/shard_map/ppermute | solution.py:16
  11.6 9.0 %collective-permute-start.4 = (f32[32,1024]{1,0:T(8,128)S(1)}, f32[32,1024]{1,0:T(8,128)S(1)}, u32[]{:S(2)}, u32[]{:S(2)}) collective-permute-start(f32[32,1024]{1,0:T(8,128)S(1)} %get-tuple-element.24), channel_id=1, source_target_pairs={{0,4},{4,8},{8,12},{12,0},{1,5},{5,9},{9,13},{13,1},{2,6},{6,10},{... | collective-permute-start | bytes 393224 | tf_op jit(solution)/shard_map/ppermute | solution.py:16
  11.6 9.0 %collective-permute-start.5 = (f32[32,1024]{1,0:T(8,128)S(1)}, f32[32,1024]{1,0:T(8,128)S(1)}, u32[]{:S(2)}, u32[]{:S(2)}) collective-permute-start(f32[32,1024]{1,0:T(8,128)S(1)} %get-tuple-element.23), channel_id=1, source_target_pairs={{0,8},{4,12},{8,0},{12,4},{1,9},{5,13},{9,1},{13,5},{2,10},{6,14},... | collective-permute-start | bytes 393224 | tf_op jit(solution)/shard_map/ppermute | solution.py:16
  21.4 108.1 %all-gather.7.cloned.1.call-start = ((), (), s32[]{:S(2)}) async-start(), calls=%async_computation.2 | async-start | bytes 4718592 | tf_op jit(solution)/shard_map/all_gather | solution.py:130
  21.5 6.1 %collective-permute-start.15 = (f32[32,1024]{1,0:T(8,128)S(1)}, f32[32,1024]{1,0:T(8,128)S(1)}, u32[]{:S(2)}, u32[]{:S(2)}) collective-permute-start(f32[32,1024]{1,0:T(8,128)S(1)} %get-tuple-element.28), channel_id=1, source_target_pairs={{0,1},{1,2},{2,3},{3,0},{4,5},{5,6},{6,7},{7,4},{8,9},{9,10},{10,1... | collective-permute-start | bytes 393224 | tf_op jit(solution)/shard_map/ppermute | solution.py:16
  22.1 7.8 %collective-permute-start.16 = (f32[32,1024]{1,0:T(8,128)S(1)}, f32[32,1024]{1,0:T(8,128)S(1)}, u32[]{:S(2)}, u32[]{:S(2)}) collective-permute-start(f32[32,1024]{1,0:T(8,128)S(1)} %get-tuple-element.27), channel_id=1, source_target_pairs={{0,2},{1,3},{2,0},{3,1},{4,6},{5,7},{6,4},{7,5},{8,10},{9,11},{10,... | collective-permute-start | bytes 393224 | tf_op jit(solution)/shard_map/ppermute | solution.py:16
  24.5 6.7 %collective-permute-start.17 = (f32[32,1024]{1,0:T(8,128)S(1)}, f32[32,1024]{1,0:T(8,128)S(1)}, u32[]{:S(2)}, u32[]{:S(2)}) collective-permute-start(f32[32,1024]{1,0:T(8,128)S(1)} %get-tuple-element.26), channel_id=1, source_target_pairs={{0,3},{1,0},{2,1},{3,2},{4,7},{5,4},{6,5},{7,6},{8,11},{9,8},{10,9... | collective-permute-start | bytes 393224 | tf_op jit(solution)/shard_map/ppermute | solution.py:16
  63.9 26.3 %collective-permute-start = (f32[1024,256]{1,0:T(8,128)S(1)}, f32[1024,256]{1,0:T(8,128)S(1)}, u32[]{:S(2)}, u32[]{:S(2)}) collective-permute-start(f32[1024,256]{1,0:T(8,128)S(1)} %bitcast.70), channel_id=1, source_target_pairs={{0,4},{4,8},{8,12},{12,0},{1,5},{5,9},{9,13},{13,1},{2,6},{6,10},{... | collective-permute-start | bytes 3145736 | tf_op jit(solution)/shard_map/ppermute | solution.py:16
  64.0 26.3 %collective-permute-start.2 = (f32[1024,256]{1,0:T(8,128)S(1)}, f32[1024,256]{1,0:T(8,128)S(1)}, u32[]{:S(2)}, u32[]{:S(2)}) collective-permute-start(f32[1024,256]{1,0:T(8,128)S(1)} %bitcast.71), channel_id=1, source_target_pairs={{0,12},{4,0},{8,4},{12,8},{1,13},{5,1},{9,5},{13,9},{2,14},{6,2},{... | collective-permute-start | bytes 3145736 | tf_op jit(solution)/shard_map/ppermute | solution.py:16
  67.2 26.4 %collective-permute-start.11 = (f32[1024,256]{1,0:T(8,128)S(1)}, f32[1024,256]{1,0:T(8,128)S(1)}, u32[]{:S(2)}, u32[]{:S(2)}) collective-permute-start(f32[1024,256]{1,0:T(8,128)S(1)} %bitcast.72), channel_id=1, source_target_pairs={{0,1},{1,2},{2,3},{3,0},{4,5},{5,6},{6,7},{7,4},{8,9},{9,10},{10,1... | collective-permute-start | bytes 3145736 | tf_op jit(solution)/shard_map/ppermute | solution.py:16
  67.7 26.5 %collective-permute-start.13 = (f32[1024,256]{1,0:T(8,128)S(1)}, f32[1024,256]{1,0:T(8,128)S(1)}, u32[]{:S(2)}, u32[]{:S(2)}) collective-permute-start(f32[1024,256]{1,0:T(8,128)S(1)} %bitcast.73), channel_id=1, source_target_pairs={{0,3},{1,0},{2,1},{3,2},{4,7},{5,4},{6,5},{7,6},{8,11},{9,8},{10,9... | collective-permute-start | bytes 3145736 | tf_op jit(solution)/shard_map/ppermute | solution.py:16
  90.2 14.3 %copy-start.7 = (f32[1024,256]{1,0:T(8,128)}, f32[1024,256]{1,0:T(8,128)S(1)}, u32[]{:S(2)}) copy-start(f32[1024,256]{1,0:T(8,128)S(1)} %collective-permute-done.refs_1_) | copy-start | bytes 3145732
  90.2 14.3 %collective-permute-start.1 = (f32[512,256]{1,0:T(8,128)S(1)}, f32[512,256]{1,0:T(8,128)S(1)}, u32[]{:S(2)}, u32[]{:S(2)}) collective-permute-start(f32[512,256]{1,0:T(8,128)S(1)} %slice.104), channel_id=1, source_target_pairs={{0,4},{4,8},{8,12},{12,0},{1,5},{5,9},{9,13},{13,1},{2,6},{6,10},{... | collective-permute-start | bytes 1572872 | tf_op jit(solution)/shard_map/ppermute | solution.py:16
  90.3 14.2 %copy-start.9 = (f32[1024,256]{1,0:T(8,128)}, f32[1024,256]{1,0:T(8,128)S(1)}, u32[]{:S(2)}) copy-start(f32[1024,256]{1,0:T(8,128)S(1)} %collective-permute-done.2.refs_2_) | copy-start | bytes 3145732
  90.4 14.2 %collective-permute-start.3 = (f32[512,256]{1,0:T(8,128)S(1)}, f32[512,256]{1,0:T(8,128)S(1)}, u32[]{:S(2)}, u32[]{:S(2)}) collective-permute-start(f32[512,256]{1,0:T(8,128)S(1)} %slice.105), channel_id=1, source_target_pairs={{0,12},{4,0},{8,4},{12,8},{1,13},{5,1},{9,5},{13,9},{2,14},{6,2},{... | collective-permute-start | bytes 1572872 | tf_op jit(solution)/shard_map/ppermute | solution.py:16
  93.6 10.9 %copy-start.3 = (f32[1024,256]{1,0:T(8,128)}, f32[1024,256]{1,0:T(8,128)S(1)}, u32[]{:S(2)}) copy-start(f32[1024,256]{1,0:T(8,128)S(1)} %collective-permute-done.11.refs_1_) | copy-start | bytes 3145732
  93.7 12.5 %collective-permute-start.12 = (f32[512,256]{1,0:T(8,128)S(1)}, f32[512,256]{1,0:T(8,128)S(1)}, u32[]{:S(2)}, u32[]{:S(2)}) collective-permute-start(f32[512,256]{1,0:T(8,128)S(1)} %slice.113), channel_id=1, source_target_pairs={{0,1},{1,2},{2,3},{3,0},{4,5},{5,6},{6,7},{7,4},{8,9},{9,10},{10,1... | collective-permute-start | bytes 1572872 | tf_op jit(solution)/shard_map/ppermute | solution.py:16
  94.3 10.2 %copy-start.5 = (f32[1024,256]{1,0:T(8,128)}, f32[1024,256]{1,0:T(8,128)S(1)}, u32[]{:S(2)}) copy-start(f32[1024,256]{1,0:T(8,128)S(1)} %collective-permute-done.13.refs_2_) | copy-start | bytes 3145732
  94.3 13.5 %collective-permute-start.14 = (f32[512,256]{1,0:T(8,128)S(1)}, f32[512,256]{1,0:T(8,128)S(1)}, u32[]{:S(2)}, u32[]{:S(2)}) collective-permute-start(f32[512,256]{1,0:T(8,128)S(1)} %slice.114), channel_id=1, source_target_pairs={{0,3},{1,0},{2,1},{3,2},{4,7},{5,4},{6,5},{7,6},{8,11},{9,8},{10,9... | collective-permute-start | bytes 1572872 | tf_op jit(solution)/shard_map/ppermute | solution.py:16
  107.9 1.2 copy-start.8
  109.1 1.2 copy-start.10
  124.1 2.0 %copy-start = (f32[4,1024,256]{2,1,0:T(8,128)}, f32[4,1024,256]{2,1,0:T(8,128)S(1)}, u32[]{:S(2)}) copy-start(f32[4,1024,256]{2,1,0:T(8,128)S(1)} %product.5) | copy-start | bytes 12582916
  126.1 3.4 %copy-start.4 = (f32[1024,256]{1,0:T(8,128)S(1)}, f32[1024,256]{1,0:T(8,128)}, u32[]{:S(2)}) copy-start(f32[1024,256]{1,0:T(8,128)} %copy-done.3) | copy-start | bytes 3145732
  127.5 20.5 %collective-permute-start.7 = (f32[512,256]{1,0:T(8,128)}, f32[512,256]{1,0:T(8,128)}, u32[]{:S(2)}, u32[]{:S(2)}) collective-permute-start(f32[512,256]{1,0:T(8,128)} %get-tuple-element.12), channel_id=1, source_target_pairs={{0,1},{1,2},{2,3},{3,0},{4,5},{5,6},{6,7},{7,4},{8,9},{9,10},{10,1... | collective-permute-start | bytes 1572872 | tf_op jit(solution)/shard_map/ppermute | solution.py:16
  127.7 20.2 %collective-permute-start.9 = (f32[512,256]{1,0:T(8,128)}, f32[512,256]{1,0:T(8,128)}, u32[]{:S(2)}, u32[]{:S(2)}) collective-permute-start(f32[512,256]{1,0:T(8,128)} %get-tuple-element.10), channel_id=1, source_target_pairs={{0,3},{1,0},{2,1},{3,2},{4,7},{5,4},{6,5},{7,6},{8,11},{9,8},{10,9... | collective-permute-start | bytes 1572872 | tf_op jit(solution)/shard_map/ppermute | solution.py:16
  129.5 1.2 copy-start.6
  144.5 3.5 %copy-start.1 = (f32[4,1024,256]{2,1,0:T(8,128)S(1)}, f32[4,1024,256]{2,1,0:T(8,128)}, u32[]{:S(2)}) copy-start(f32[4,1024,256]{2,1,0:T(8,128)} %copy-done) | copy-start | bytes 12582916
  144.5 4.8 %copy-start.12 = (f32[512,256]{1,0:T(8,128)S(1)}, f32[512,256]{1,0:T(8,128)}, u32[]{:S(2)}) copy-start(f32[512,256]{1,0:T(8,128)} %get-tuple-element.9) | copy-start | bytes 1572868
  144.5 5.2 %copy-start.11 = (f32[512,256]{1,0:T(8,128)S(1)}, f32[512,256]{1,0:T(8,128)}, u32[]{:S(2)}) copy-start(f32[512,256]{1,0:T(8,128)} %get-tuple-element.11) | copy-start | bytes 1572868
  144.7 12.0 %collective-permute-start.18 = (f32[512,256]{1,0:T(8,128)S(1)}, f32[512,256]{1,0:T(8,128)S(1)}, u32[]{:S(2)}, u32[]{:S(2)}) collective-permute-start(f32[512,256]{1,0:T(8,128)S(1)} %get-tuple-element.18), channel_id=1, source_target_pairs={{0,4},{4,8},{8,12},{12,0},{1,5},{5,9},{9,13},{13,1},{2,6},{6,10},{... | collective-permute-start | bytes 1572872 | tf_op jit(solution)/shard_map/ppermute | solution.py:16
  144.7 11.9 %collective-permute-start.20 = (f32[512,256]{1,0:T(8,128)S(1)}, f32[512,256]{1,0:T(8,128)S(1)}, u32[]{:S(2)}, u32[]{:S(2)}) collective-permute-start(f32[512,256]{1,0:T(8,128)S(1)} %get-tuple-element.16), channel_id=1, source_target_pairs={{0,12},{4,0},{8,4},{12,8},{1,13},{5,1},{9,5},{13,9},{2,14},{6,2},{... | collective-permute-start | bytes 1572872 | tf_op jit(solution)/shard_map/ppermute | solution.py:16
  149.4 22.6 %collective-permute-start.10 = (f32[1024,256]{1,0:T(8,128)S(1)}, f32[1024,256]{1,0:T(8,128)S(1)}, u32[]{:S(2)}, u32[]{:S(2)}) collective-permute-start(f32[1024,256]{1,0:T(8,128)S(1)} %pad_maximum_fusion.3), channel_id=1, source_target_pairs={{0,3},{1,0},{2,1},{3,2},{4,7},{5,4},{6,5},{7,6},{8,11},{9,8},{10,9... | collective-permute-start | bytes 3145736 | tf_op jit(solution)/shard_map/ppermute | solution.py:16
  149.8 22.2 %collective-permute-start.8 = (f32[1024,256]{1,0:T(8,128)S(1)}, f32[1024,256]{1,0:T(8,128)S(1)}, u32[]{:S(2)}, u32[]{:S(2)}) collective-permute-start(f32[1024,256]{1,0:T(8,128)S(1)} %pad_maximum_fusion.2), channel_id=1, source_target_pairs={{0,1},{1,2},{2,3},{3,0},{4,5},{5,6},{6,7},{7,4},{8,9},{9,10},{10,1... | collective-permute-start | bytes 3145736 | tf_op jit(solution)/shard_map/ppermute | solution.py:16
  156.8 21.5 %collective-permute-start.21 = (f32[1024,256]{1,0:T(8,128)S(1)}, f32[1024,256]{1,0:T(8,128)S(1)}, u32[]{:S(2)}, u32[]{:S(2)}) collective-permute-start(f32[1024,256]{1,0:T(8,128)S(1)} %pad_maximum_fusion.6), channel_id=1, source_target_pairs={{0,12},{4,0},{8,4},{12,8},{1,13},{5,1},{9,5},{13,9},{2,14},{6,2},{... | collective-permute-start | bytes 3145736 | tf_op jit(solution)/shard_map/ppermute | solution.py:16
  160.1 21.5 %collective-permute-start.19 = (f32[1024,256]{1,0:T(8,128)S(1)}, f32[1024,256]{1,0:T(8,128)S(1)}, u32[]{:S(2)}, u32[]{:S(2)}) collective-permute-start(f32[1024,256]{1,0:T(8,128)S(1)} %pad_maximum_fusion.5), channel_id=1, source_target_pairs={{0,4},{4,8},{8,12},{12,0},{1,5},{5,9},{9,13},{13,1},{2,6},{6,10},{... | collective-permute-start | bytes 3145736 | tf_op jit(solution)/shard_map/ppermute | solution.py:16
Sparse Core Ops, SparseCore 0:
  21.6 42.4 all-gather.4
  65.8 33.0 all-gather.6

commit v2 on v0

v2 whole, which is shorter than its diff:
```python
import functools
import itertools

import jax
import jax.numpy as jnp
from jax import lax
from jax.experimental import pallas as pl
from jax.experimental.pallas import tpu as pltpu
from jax.sharding import Mesh, PartitionSpec as P

N = 4
ALL = ("z", "c", "y", "x")
VMEM_LIMIT = 16 * 1024 * 1024


def permute(value, target):
    pairs = []
    for z, c, y, x in itertools.product(range(N), range(2), range(N), range(N)):
        tz, tc, ty, tx = target(z, c, y, x)
        place = ((tz % N * 2 + tc % 2) * N + ty % N) * N + tx % N
        pairs.append((((z * 2 + c) * N + y) * N + x, place))
    return lax.ppermute(value, ALL, pairs)


def swap(value):
    return permute(value, lambda z, c, y, x: (z, 1 - c, y, x))


def along_z(value, step):
    return permute(value, lambda z, c, y, x: (z + step * (1 - 2 * c), c, y, x))


def along_gather(value, step):
    return permute(value, lambda z, c, y, x: (z, c, y + step * (1 - c), x + step * c))


def along_reduce(value, step):
    return permute(value, lambda z, c, y, x: (z, c, y + step * c, x + step * (1 - c)))


def split(value):
    high = value.astype(jnp.bfloat16)
    low = (value - high.astype(jnp.float32)).astype(jnp.bfloat16)
    return high, low


def dot(first, second):
    return lax.dot_general(
        first, second, (((1,), (0,)), ((), ())), preferred_element_type=jnp.float32
    )


SMEM = pl.BlockSpec(memory_space=pltpu.SMEM)
VMEM = pl.BlockSpec(memory_space=pltpu.VMEM)
ANY = pl.BlockSpec(memory_space=pl.ANY)
HBM = pl.BlockSpec(memory_space=pltpu.HBM)
PARAMS = pltpu.CompilerParams(vmem_limit_bytes=VMEM_LIMIT)


def prepare_a_kernel(place, a_ref, own_ref, two_ref, side_ref, pass_ref):
    z, c = place[0], place[1]
    wide = own_ref.shape[1]
    half = wide // 2

    def piece(step, part=0, width=wide):
        start = lax.rem(z + step, N) * wide + part * half
        return a_ref[:, pl.ds(pl.multiple_of(start, half), width)]

    own_ref[...] = piece(0)
    two_ref[...] = piece(2)
    side_ref[...] = piece(1 + 2 * c)
    for part in range(2):
        pass_ref[part] = piece(0, part, half)
        pass_ref[2 + part] = piece(3 - 2 * c, part, half)


def prepare_a(a, place):
    rows, columns = a.shape
    piece = jax.ShapeDtypeStruct((rows, columns // N), a.dtype)
    passed = jax.ShapeDtypeStruct((N, rows, columns // (2 * N)), a.dtype)
    return pl.pallas_call(
        prepare_a_kernel,
        out_shape=(piece, piece, piece, passed),
        in_specs=[SMEM, VMEM],
        out_specs=(VMEM,) * 4,
        compiler_params=PARAMS,
        name="prepare_a",
    )(place, a)


def prepare_b_kernel(place, b_ref, keep_ref, pass_ref):
    c, y, x = place[1], place[2], place[3]
    width = keep_ref.shape[2] // N
    for core, ref in ((c, keep_ref), (1 - c, pass_ref)):
        for g in range(N):
            for h in range(N):
                ty = lax.rem(y + g * (1 - core) + h * core, N)
                tx = lax.rem(x + g * core + h * (1 - core), N)
                start = pl.multiple_of(((ty * N + tx) * 2 + core) * width, width)
                ref[g, :, h * width : (h + 1) * width] = b_ref[:, pl.ds(start, width)]


def prepare_b(b, place):
    rows, columns = b.shape
    part = jax.ShapeDtypeStruct((N, rows, columns // (2 * N)), b.dtype)
    return pl.pallas_call(
        prepare_b_kernel,
        out_shape=(part, part),
        in_specs=[SMEM, VMEM],
        out_specs=(VMEM, VMEM),
        compiler_params=PARAMS,
        name="prepare_b",
    )(place, b)


def join_a_kernel(side, got, out_ref):
    rows, wide = side.shape
    half = wide // 2
    out_ref[:rows] = side[...]
    for part in range(2):
        out_ref[rows:, part * half : (part + 1) * half] = got[2 + part]


def join_a(side, got):
    rows, wide = side.shape
    return pl.pallas_call(
        join_a_kernel,
        out_shape=jax.ShapeDtypeStruct((2 * rows, wide), side.dtype),
        in_specs=[VMEM] * 2,
        out_specs=VMEM,
        compiler_params=PARAMS,
        name="join_a",
    )(side, got)


def join_b_kernel(keep, got, *refs):
    rows = keep.shape[1]
    for g in range(N):
        refs[g][:rows] = keep[g]
        refs[g][rows:] = got[g]


def join_b(keep, got):
    _, rows, columns = keep.shape
    return pl.pallas_call(
        join_b_kernel,
        out_shape=(jax.ShapeDtypeStruct((2 * rows, columns), keep.dtype),) * N,
        in_specs=[VMEM] * 2,
        out_specs=(VMEM,) * N,
        compiler_params=PARAMS,
        name="join_b",
    )(keep, got)


def turn_kernel(place, own, got, side, two, two_got, side_got, *refs):
    out_ref = refs[-1]
    half = out_ref.shape[1]
    rows = own.shape[0]
    for part in range(2):
        which = lax.rem(place[1] + part, 2)
        columns = pl.ds(pl.multiple_of(which * half, half), half)
        blocks = [
            own[:, columns],
            got[which],
            side[:, columns],
            two[:, columns],
            two_got[:, columns],
            side_got[rows:, columns],
            side_got[:rows, columns],
        ]
        out_ref[part] = jnp.concatenate(blocks, 0).T


def turn(place, parts, after):
    rows, columns = parts[0].shape
    return pl.pallas_call(
        turn_kernel,
        out_shape=jax.ShapeDtypeStruct((2, columns // 2, 2 * N * rows), jnp.float32),
        in_specs=[SMEM] + [VMEM] * 6 + [ANY] * len(after),
        out_specs=VMEM,
        compiler_params=PARAMS,
        name="turn",
    )(place, *parts, *after)


GATHERED = (0, 1, 3)


def split_a_kernel(a0, a1, a3, high_ref, low_ref):
    depth = a0.shape[2]
    for half in range(2):
        for i, ref in enumerate((a0, a1, a3)):
            place = slice(i * depth, (i + 1) * depth)
            high_ref[half, :, place], low_ref[half, :, place] = split(ref[half])


def split_a(blocks):
    _, rows, depth = blocks[0].shape
    out = jax.ShapeDtypeStruct((2, rows, 3 * depth), jnp.bfloat16)
    return pl.pallas_call(
        split_a_kernel,
        out_shape=(out, out),
        in_specs=[VMEM] * 3,
        out_specs=(VMEM, VMEM),
        compiler_params=PARAMS,
        name="split_a",
    )(*blocks)


def split_b_kernel(*refs):
    high_ref, low_ref = refs[N:]
    slab = refs[0].shape[1]
    for i, g in enumerate(GATHERED + (2,)):
        for s in range(N):
            place = slice((i * N + s) * slab, (i * N + s + 1) * slab)
            high_ref[place], low_ref[place] = split(refs[s][g])


def split_b(panels):
    _, slab, columns = panels[0].shape
    out = jax.ShapeDtypeStruct((N * N * slab, columns), jnp.bfloat16)
    return pl.pallas_call(
        split_b_kernel,
        out_shape=(out, out),
        in_specs=[VMEM] * N,
        out_specs=(VMEM, VMEM),
        compiler_params=PARAMS,
        name="split_b",
    )(*panels)


TILE = 512


def one_product(half, r, high, low, far_high, far_low, bh, bl, out_ref):
    near = high.shape[2]
    rows, width = out_ref.shape
    columns = slice(r * width, (r + 1) * width)
    for start in range(0, rows, TILE):
        tile = slice(start, start + TILE)
        total = dot(high[half, tile], bh[:near, columns])
        total += dot(high[half, tile], bl[:near, columns])
        total += dot(low[half, tile], bh[:near, columns])
        total += dot(far_high[half, tile], bh[near:, columns])
        total += dot(far_high[half, tile], bl[near:, columns])
        total += dot(far_low[half, tile], bh[near:, columns])
        out_ref[tile] = total


def first_kernel(high, low, top, bottom, bh, bl, far_high, far_low, *out_refs):
    far_high[0], far_low[0] = split(top[...])
    far_high[1], far_low[1] = split(bottom[...])
    for half, ref in enumerate(out_refs):
        one_product(half, 2, high, low, far_high, far_low, bh, bl, ref)


def product_kernel(tasks, high, low, far_high, far_low, bh, bl, *out_refs):
    for (half, r), ref in zip(tasks, out_refs):
        one_product(half, r, high, low, far_high, far_low, bh, bl, ref)


def cost(rows, depth, width, count):
    return pl.CostEstimate(
        flops=6 * rows * depth * width * count,
        bytes_accessed=4 * rows * width * count,
        transcendentals=0,
    )


def first_product(high, low, top, bottom, bh, bl):
    rows, depth = top.shape
    width = bh.shape[1] // N
    far = jax.ShapeDtypeStruct((2, rows, depth), jnp.bfloat16)
    out = jax.ShapeDtypeStruct((rows, width), jnp.float32)
    return pl.pallas_call(
        first_kernel,
        out_shape=(far, far, out, out),
        in_specs=[VMEM] * 6,
        out_specs=(VMEM,) * 4,
        compiler_params=PARAMS,
        cost_estimate=cost(rows, N * depth, width, 2),
        name="first_product",
    )(high, low, top, bottom, bh, bl)


def product(tasks, high, low, far_high, far_low, bh, bl):
    _, rows, depth = far_high.shape
    width = bh.shape[1] // N
    out = jax.ShapeDtypeStruct((rows, width), jnp.float32)
    return pl.pallas_call(
        functools.partial(product_kernel, tasks),
        out_shape=(out,) * len(tasks),
        in_specs=[VMEM] * 6,
        out_specs=(VMEM,) * len(tasks),
        compiler_params=PARAMS,
        cost_estimate=cost(rows, N * depth, width, len(tasks)),
        name="product",
    )(high, low, far_high, far_low, bh, bl)


def finish_kernel(place, top0, top3, top1, got, out_ref):
    tile, width = out_ref.shape
    rows = pl.ds(pl.multiple_of(pl.program_id(0) * tile, tile), tile)
    mine = top0[rows] + top3[rows] + top1[rows]
    theirs = got[rows]
    width //= 2

    @pl.when(place[1] == 0)
    def _():
        out_ref[:, :width] = mine
        out_ref[:, width:] = theirs

    @pl.when(place[1] == 1)
    def _():
        out_ref[:, :width] = theirs
        out_ref[:, width:] = mine


def finish(place, top0, top3, top1, got):
    rows, width = top0.shape
    tile = rows // 4
    return pl.pallas_call(
        finish_kernel,
        grid=(4,),
        out_shape=jax.ShapeDtypeStruct((rows, 2 * width), jnp.float32),
        in_specs=[SMEM] + [VMEM] * 4,
        out_specs=pl.BlockSpec((tile, 2 * width), lambda m: (m, 0)),
        compiler_params=PARAMS,
        name="finish",
    )(place, top0, top3, top1, got)


TOP, BOTTOM = 0, 1


def shards(a, b):
    place = jnp.stack([lax.axis_index(name) for name in ALL]).astype(jnp.int32)
    own, two, side, handed = prepare_a(a, place)
    two = along_z(two, 2)
    got = swap(handed)
    side = along_z(join_a(side, got), 1)
    keep, give = prepare_b(b, place)
    pieces = join_b(keep, swap(give))

    panel = [pieces[0]] + [along_gather(pieces[g], g) for g in range(1, N)]
    two, side, panel = lax.optimization_barrier((two, side, panel))
    near = turn(place, (own, got, side, two, swap(two), swap(side)), ())

    panels = [jnp.stack(panel, 0)]
    for _ in range(N - 1):
        panels.append(along_z(panels[-1], 1))

    behind = along_gather(near, 1)
    ahead = along_gather(near, -1)
    top = along_gather(behind[TOP], 1)
    bottom = along_gather(ahead[BOTTOM], -1)

    high, low = split_a((near, behind, ahead))
    bh, bl = split_b(panels)
    far_high, far_low, top2, bottom2 = first_product(high, low, top, bottom, bh, bl)
    operands = (high, low, far_high, far_low, bh, bl)
    bottom1, top3 = product(((BOTTOM, 1), (TOP, 3)), *operands)
    top1, bottom3 = product(((TOP, 1), (BOTTOM, 3)), *operands)
    top0, bottom0 = product(((TOP, 0), (BOTTOM, 0)), *operands)

    top2 = along_reduce(top2, 1)
    bottom2 = along_reduce(bottom2, -1)
    bottom1 = along_reduce(bottom1, 1)
    top3 = along_reduce(top3, -1)
    top1 = along_reduce(top1 + top2, 1)
    bottom3 = along_reduce(bottom3 + bottom2, -1)
    got = swap(bottom0 + bottom1 + bottom3)
    return finish(place, top0, top3, top1, got)


def solution(mesh):
    fine = Mesh(mesh.devices.reshape(N, 2, N, N), ALL)
    return jax.shard_map(
        shards,
        mesh=fine,
        in_specs=(P(ALL, None), P(ALL, None)),
        out_specs=P(("z", "c"), ("y", "x")),
        check_vma=False,
    )
```

time: 996 us -> 125 us (0.13)
  waiting for transfers between devices: 895 us -> 74.9 us
  matrix products: 46 us -> 0 us
  Pallas kernels: 0 us -> 20.2 us
  local copies, waits for them, and re-layouts: 18.3 us -> 2.58 us
  between operations: 13.1 us -> 0.2 us
  starting transfers between devices: 13.4 us -> 25.9 us
    psum x8 -> x0, waiting for transfers between devices: 499 us -> none  [broadcast(): return lax.psum(block, axis)]
    all_gather x8 -> x0, waiting for transfers between devices: 366 us -> none  [advance(): panel_left = lax.all_gather(section, 'col', axis=0, tiled=True)]
    ppermute x0 -> x23, waiting for transfers between devices: none -> 74.9 us  [permute(): return lax.ppermute(value, ALL, pairs)]
    dot_general x8 -> x0, matrix products: 46 us -> none  [contract(): lax.dot_general(first, second, (((0,), (0,)), ((), ())), precision=lax.Pr...]
    all_to_all x2 -> x0, waiting for transfers between devices: 29.2 us -> none  [the longest x1 14.9 us: shards(): lax.all_to_all(amplitudes, 'row', split_axis=1, concat_axis=0, tiled=True)]
    ppermute x0 -> x23, starting transfers between devices: none -> 25.9 us  [permute(): return lax.ppermute(value, ALL, pairs)]
    pallas_call x0 -> x12, Pallas kernels: none -> 20.2 us  [the longest x3 10.2 us: product(): pl.pallas_call(functools.partial(product_kernel, tasks), out_shape=(out,)...]
    all_to_all x2 -> x0, starting transfers between devices: 12.7 us -> none  [the longest x1 7.42 us: shards(): lax.all_to_all(intermediates, 'col', split_axis=1, concat_axis=0, tiled=T...]
  transfers between devices with their start and end apart: 18 -> 23, of which waited for: 18 -> 10; matrix products, arithmetic and copies ran while one was open for 1% -> 1% of each run, Pallas kernels for 0% -> 11%
where the time goes in v2:
time: 125 us
  waiting for transfers between devices  74.9 us (60%)
  starting transfers between devices  25.9 us (21%)
  Pallas kernels  20.2 us (16%)
  local copies, waits for them, and re-layouts  2.58 us (2%)
    ppermute x23, waiting for transfers between devices, permute(): return lax.ppermute(value, ALL, pairs)  74.9 us
    ppermute x23, starting transfers between devices, permute(): return lax.ppermute(value, ALL, pairs)  25.9 us
    pallas_call x3, Pallas kernels, product(): pl.pallas_call(functools.partial(product_kernel, tasks), out_shape=(out,)...  10.2 us
    pallas_call x1, Pallas kernels, first_product(): pl.pallas_call(first_kernel, out_shape=(far, far, out, out), in_specs=[VM...  3.41 us
    pallas_call x1, Pallas kernels, finish(): pl.pallas_call(finish_kernel, grid=(4,), out_shape=jax.ShapeDtypeStruct((...  2.53 us
  transfers between devices with their start and end apart: 23, of which 10 were waited for; matrix products, arithmetic and copies ran while one was open for 1% of the time, Pallas kernels for 11%

profile of v2, /device:TPU:6, one launch (start us, length us, event | category | flops | bytes accessed | tf_op | source)
XLA Modules:
  0.0 124.5 jit_solution(5414760766748799629)
XLA Ops:
  0.0 0.1 pad_add_fusion.place
  0.1 1.2 copy-done
  1.3 0.6 prepare_a.1
  1.9 0.1 collective-permute-start
  2.0 0.0 copy-start.1
  2.0 1.2 copy-done.1
  3.3 0.7 prepare_b.1
  4.0 0.6 collective-permute-start.3
  4.6 0.0 collective-permute-done.got
  4.6 2.0 %collective-permute-start.2 = (f32[64,2048]{1,0:T(8,128)S(1)}, f32[64,2048]{1,0:T(8,128)S(1)}, u32[]{:S(2)}, u32[]{:S(2)}) collective-permute-start(f32[64,2048]{1,0:T(8,128)S(1)} %join_a.1), channel_id=1, source_target_pairs={{0,32},{1,33},{2,34},{3,35},{4,36},{5,37},{6,38},{7,39},{8,40},{9,... | collective-permute-start | bytes 1572872 | tf_op jit(solution)/shard_map/ppermute | solution.py:22
  6.6 3.6 %collective-permute-start.1 = (f32[32,2048]{1,0:T(8,128)S(1)}, f32[32,2048]{1,0:T(8,128)S(1)}, u32[]{:S(2)}, u32[]{:S(2)}) collective-permute-start(f32[32,2048]{1,0:T(8,128)S(1)} %get-tuple-element.37), channel_id=1, source_target_pairs={{0,64},{1,65},{2,66},{3,67},{4,68},{5,69},{6,70},{7,71},{8,72},{9,... | collective-permute-start | bytes 786440 | tf_op jit(solution)/shard_map/ppermute | solution.py:22
  10.2 0.0 collective-permute-done.3.got
  10.2 0.1 join_b.1
  10.2 1.6 %collective-permute-start.4 = (f32[64,1024]{1,0:T(8,128)S(1)}, f32[64,1024]{1,0:T(8,128)S(1)}, u32[]{:S(2)}, u32[]{:S(2)}) collective-permute-start(f32[64,1024]{1,0:T(8,128)S(1)} %get-tuple-element.42), channel_id=1, source_target_pairs={{0,4},{1,5},{2,6},{3,7},{4,8},{5,9},{6,10},{7,11},{8,12},{9,13},{1... | collective-permute-start | bytes 786440 | tf_op jit(solution)/shard_map/ppermute | solution.py:22
  11.9 2.9 %collective-permute-start.5 = (f32[64,1024]{1,0:T(8,128)S(1)}, f32[64,1024]{1,0:T(8,128)S(1)}, u32[]{:S(2)}, u32[]{:S(2)}) collective-permute-start(f32[64,1024]{1,0:T(8,128)S(1)} %get-tuple-element.43), channel_id=1, source_target_pairs={{0,8},{1,9},{2,10},{3,11},{4,12},{5,13},{6,14},{7,15},{8,0},{9,1},... | collective-permute-start | bytes 786440 | tf_op jit(solution)/shard_map/ppermute | solution.py:22
  14.8 1.3 %collective-permute-start.6 = (f32[64,1024]{1,0:T(8,128)S(1)}, f32[64,1024]{1,0:T(8,128)S(1)}, u32[]{:S(2)}, u32[]{:S(2)}) collective-permute-start(f32[64,1024]{1,0:T(8,128)S(1)} %get-tuple-element.44), channel_id=1, source_target_pairs={{0,12},{1,13},{2,14},{3,15},{4,0},{5,1},{6,2},{7,3},{8,4},{9,5},{1... | collective-permute-start | bytes 786440 | tf_op jit(solution)/shard_map/ppermute | solution.py:22
  16.1 6.8 %collective-permute-done.1.two = f32[32,2048]{1,0:T(8,128)S(1)} collective-permute-done((f32[32,2048]{1,0:T(8,128)S(1)}, f32[32,2048]{1,0:T(8,128)S(1)}, u32[]{:S(2)}, u32[]{:S(2)}) %collective-permute-start.1) | collective-permute-done | bytes 262176 | tf_op jit(solution)/shard_map/ppermute | solution.py:22
  22.9 0.0 collective-permute-done.4
  22.9 0.0 collective-permute-done.5
  23.0 0.0 collective-permute-done.6
  23.0 0.0 collective-permute-done.2.side
  23.0 0.1 collective-permute-start.8
  23.1 0.5 collective-permute-start.7
  23.6 0.1 pad_maximum_fusion.refs_0_
  23.7 0.1 collective-permute-start.13
  23.7 1.6 %collective-permute-done.7.two_got = f32[32,2048]{1,0:T(8,128)S(1)} collective-permute-done((f32[32,2048]{1,0:T(8,128)S(1)}, f32[32,2048]{1,0:T(8,128)S(1)}, u32[]{:S(2)}, u32[]{:S(2)}) %collective-permute-start.7) | collective-permute-done | bytes 262176 | tf_op jit(solution)/shard_map/ppermute | solution.py:22
  25.3 0.0 collective-permute-done.8.side_got
  25.3 1.1 turn.1.a0
  26.5 3.1 %collective-permute-start.10 = (f32[2,1024,256]{2,1,0:T(8,128)S(1)}, f32[2,1024,256]{2,1,0:T(8,128)S(1)}, u32[]{:S(2)}, u32[]{:S(2)}) collective-permute-start(f32[2,1024,256]{2,1,0:T(8,128)S(1)} %turn.1.a0), channel_id=1, source_target_pairs={{0,12},{1,13},{2,14},{3,15},{4,0},{5,1},{6,2},{7,3},{8,4},{9,5},{1... | collective-permute-start | bytes 6291464 | tf_op jit(solution)/shard_map/ppermute | solution.py:22
  29.6 0.0 collective-permute-start.9
  29.6 10.2 %collective-permute-done.13.refs_1_ = f32[4,64,1024]{2,1,0:T(8,128)S(1)} collective-permute-done((f32[4,64,1024]{2,1,0:T(8,128)S(1)}, f32[4,64,1024]{2,1,0:T(8,128)S(1)}, u32[]{:S(2)}, u32[]{:S(2)}) %collective-permute-start.13) | collective-permute-done | bytes 1048608 | tf_op jit(solution)/shard_map/ppermute | solution.py:22
  39.7 0.0 collective-permute-start.14
  39.7 16.0 %collective-permute-done.14.refs_2_ = f32[4,64,1024]{2,1,0:T(8,128)S(1)} collective-permute-done((f32[4,64,1024]{2,1,0:T(8,128)S(1)}, f32[4,64,1024]{2,1,0:T(8,128)S(1)}, u32[]{:S(2)}, u32[]{:S(2)}) %collective-permute-start.14) | collective-permute-done | bytes 1048608 | tf_op jit(solution)/shard_map/ppermute | solution.py:22
  55.8 0.0 collective-permute-start.15
  55.8 0.1 slice_bitcast_fusion
  55.8 3.1 %collective-permute-start.12 = (f32[1024,256]{1,0:T(8,128)S(1)}, f32[1024,256]{1,0:T(8,128)S(1)}, u32[]{:S(2)}, u32[]{:S(2)}) collective-permute-start(f32[1024,256]{1,0:T(8,128)S(1)} %slice_bitcast_fusion), channel_id=1, source_target_pairs={{0,12},{1,13},{2,14},{3,15},{4,0},{5,1},{6,2},{7,3},{8,4},{9,5},{1... | collective-permute-start | bytes 3145736 | tf_op jit(solution)/shard_map/ppermute | solution.py:22
  58.9 0.1 slice_bitcast_fusion.1
  59.0 0.1 collective-permute-start.11
  59.1 0.8 split_a.1
  59.9 11.8 %collective-permute-done.15.refs_3_ = f32[4,64,1024]{2,1,0:T(8,128)S(1)} collective-permute-done((f32[4,64,1024]{2,1,0:T(8,128)S(1)}, f32[4,64,1024]{2,1,0:T(8,128)S(1)}, u32[]{:S(2)}, u32[]{:S(2)}) %collective-permute-start.15) | collective-permute-done | bytes 1048608 | tf_op jit(solution)/shard_map/ppermute | solution.py:22
  71.8 0.7 split_b.1
  72.4 2.6 %collective-permute-done.11.top = f32[1024,256]{1,0:T(8,128)S(1)} collective-permute-done((f32[1024,256]{1,0:T(8,128)S(1)}, f32[1024,256]{1,0:T(8,128)S(1)}, u32[]{:S(2)}, u32[]{:S(2)}) %collective-permute-start.11) | collective-permute-done | bytes 1048608 | tf_op jit(solution)/shard_map/ppermute | solution.py:22
  75.1 3.4 %first_product.1 = (bf16[2,1024,256]{2,1,0:T(8,128)(2,1)S(1)}, bf16[2,1024,256]{2,1,0:T(8,128)(2,1)S(1)}, f32[1024,256]{1,0:T(8,128)S(1)}, f32[1024,256]{1,0:T(8,128)S(1)}) custom-call(bf16[2,1024,768]{2,1,0:T(8,128)(2,1)S(1)} %get-tuple-element.47.high, bf16[2,1024,768]{2,1,0:T(8,128)(2,1)S(1)} %get-tuple-element.48.low, ...), custom_call_target="tpu_custom_call" | custom-call | flops 3221225472 | bytes 2097152 | tf_op jit(solution)/shard_map/first_product/pallas_call | solution.py:275
  78.5 0.9 collective-permute-start.20
  79.4 2.4 %collective-permute-start.17 = (f32[1024,256]{1,0:T(8,128)S(1)}, f32[1024,256]{1,0:T(8,128)S(1)}, u32[]{:S(2)}, u32[]{:S(2)}) collective-permute-start(f32[1024,256]{1,0:T(8,128)S(1)} %get-tuple-element.60), channel_id=1, source_target_pairs={{0,1},{1,2},{2,3},{3,0},{4,5},{5,6},{6,7},{7,4},{8,9},{9,10},{10,1... | collective-permute-start | bytes 3145736 | tf_op jit(solution)/shard_map/ppermute | solution.py:22
  81.8 3.4 %product.5 = (f32[1024,256]{1,0:T(8,128)S(1)}, f32[1024,256]{1,0:T(8,128)S(1)}) custom-call(bf16[2,1024,768]{2,1,0:T(8,128)(2,1)S(1)} %get-tuple-element.47.high, bf16[2,1024,768]{2,1,0:T(8,128)(2,1)S(1)} %get-tuple-element.48.low, bf16[2,1024,256]{2,1,0:T(8,128)(2,1)S(1)} %get-tuple-element.55.far_high, ...), custom_call_target="tpu_custom_call" | custom-call | flops 3221225472 | bytes 2097152 | tf_op jit(solution)/shard_map/product/pallas_call | solution.py:290
  85.2 3.4 %product.4 = (f32[1024,256]{1,0:T(8,128)S(1)}, f32[1024,256]{1,0:T(8,128)S(1)}) custom-call(bf16[2,1024,768]{2,1,0:T(8,128)(2,1)S(1)} %get-tuple-element.47.high, bf16[2,1024,768]{2,1,0:T(8,128)(2,1)S(1)} %get-tuple-element.48.low, bf16[2,1024,256]{2,1,0:T(8,128)(2,1)S(1)} %get-tuple-element.55.far_high, ...), custom_call_target="tpu_custom_call" | custom-call | flops 3221225472 | bytes 2097152 | tf_op jit(solution)/shard_map/product/pallas_call | solution.py:290
  88.6 0.1 collective-permute-start.19
  88.7 5.9 %collective-permute-done.20 = f32[1024,256]{1,0:T(8,128)S(1)} collective-permute-done((f32[1024,256]{1,0:T(8,128)S(1)}, f32[1024,256]{1,0:T(8,128)S(1)}, u32[]{:S(2)}, u32[]{:S(2)}) %collective-permute-start.20) | collective-permute-done | bytes 1048608 | tf_op jit(solution)/shard_map/ppermute | solution.py:22
  94.6 0.1 add.14
  94.7 0.1 collective-permute-start.21
  94.8 0.1 collective-permute-start.16
  94.9 3.4 %product.3 = (f32[1024,256]{1,0:T(8,128)S(1)}, f32[1024,256]{1,0:T(8,128)S(1)}) custom-call(bf16[2,1024,768]{2,1,0:T(8,128)(2,1)S(1)} %get-tuple-element.47.high, bf16[2,1024,768]{2,1,0:T(8,128)(2,1)S(1)} %get-tuple-element.48.low, bf16[2,1024,256]{2,1,0:T(8,128)(2,1)S(1)} %get-tuple-element.55.far_high, ...), custom_call_target="tpu_custom_call" | custom-call | flops 3221225472 | bytes 2097152 | tf_op jit(solution)/shard_map/product/pallas_call | solution.py:290
  98.3 0.0 collective-permute-done.17
  98.3 0.1 add.12
  98.5 3.2 %collective-permute-start.18 = (f32[1024,256]{1,0:T(8,128)S(1)}, f32[1024,256]{1,0:T(8,128)S(1)}, u32[]{:S(2)}, u32[]{:S(2)}) collective-permute-start(f32[1024,256]{1,0:T(8,128)S(1)} %add.12), channel_id=1, source_target_pairs={{0,1},{1,2},{2,3},{3,0},{4,5},{5,6},{6,7},{7,4},{8,9},{9,10},{10,1... | collective-permute-start | bytes 3145736 | tf_op jit(solution)/shard_map/ppermute | solution.py:22
  101.7 3.7 %collective-permute-done.19 = f32[1024,256]{1,0:T(8,128)S(1)} collective-permute-done((f32[1024,256]{1,0:T(8,128)S(1)}, f32[1024,256]{1,0:T(8,128)S(1)}, u32[]{:S(2)}, u32[]{:S(2)}) %collective-permute-start.19) | collective-permute-done | bytes 1048608 | tf_op jit(solution)/shard_map/ppermute | solution.py:22
  105.4 5.4 %collective-permute-done.21 = f32[1024,256]{1,0:T(8,128)S(1)} collective-permute-done((f32[1024,256]{1,0:T(8,128)S(1)}, f32[1024,256]{1,0:T(8,128)S(1)}, u32[]{:S(2)}, u32[]{:S(2)}) %collective-permute-start.21) | collective-permute-done | bytes 1048608 | tf_op jit(solution)/shard_map/ppermute | solution.py:22
  110.8 0.2 add_add_fusion
  111.0 0.1 collective-permute-start.22
  111.1 10.9 %collective-permute-done.16.top3 = f32[1024,256]{1,0:T(8,128)S(1)} collective-permute-done((f32[1024,256]{1,0:T(8,128)S(1)}, f32[1024,256]{1,0:T(8,128)S(1)}, u32[]{:S(2)}, u32[]{:S(2)}) %collective-permute-start.16) | collective-permute-done | bytes 1048608 | tf_op jit(solution)/shard_map/ppermute | solution.py:22
  122.0 0.0 collective-permute-done.18.top1
  122.0 0.0 collective-permute-done.22.got
  122.0 2.5 %finish.1 = f32[1024,512]{1,0:T(8,128)} custom-call(s32[4]{0:T(128)S(1)} %pad_add_fusion.place, f32[1024,256]{1,0:T(8,128)S(1)} %get-tuple-element.57.top0, f32[1024,256]{1,0:T(8,128)S(1)} %collective-permute-done.16.top3, f32[1024,256]{1,0:T(8,128)S(1)} %collective-permute-done.18.top1, f32[1024,256]{1,0:T(8,128)S(1)} %collective-permute-done.22.got), custom_call_target="tpu_custom_call" | custom-call | tf_op jit(solution)/shard_map/finish/pallas_call | solution.py:322
  (5 shorter events, 0.0 us)
Async XLA Ops:
  0.1 1.2 copy-start
  1.9 2.6 %collective-permute-start = (f32[4,32,1024]{2,1,0:T(8,128)S(1)}, f32[4,32,1024]{2,1,0:T(8,128)S(1)}, u32[]{:S(2)}, u32[]{:S(2)}) collective-permute-start(f32[4,32,1024]{2,1,0:T(8,128)S(1)} %get-tuple-element.36), channel_id=1, source_target_pairs={{0,16},{1,17},{2,18},{3,19},{4,20},{5,21},{6,22},{7,23},{8,24},{9,... | collective-permute-start | bytes 1572872 | tf_op jit(solution)/shard_map/ppermute | solution.py:22
  2.0 1.2 copy-start.1
  4.0 6.2 %collective-permute-start.3 = (f32[4,32,1024]{2,1,0:T(8,128)S(1)}, f32[4,32,1024]{2,1,0:T(8,128)S(1)}, u32[]{:S(2)}, u32[]{:S(2)}) collective-permute-start(f32[4,32,1024]{2,1,0:T(8,128)S(1)} %get-tuple-element.40), channel_id=1, source_target_pairs={{0,16},{1,17},{2,18},{3,19},{4,20},{5,21},{6,22},{7,23},{8,24},{9,... | collective-permute-start | bytes 1572872 | tf_op jit(solution)/shard_map/ppermute | solution.py:22
  4.6 18.4 %collective-permute-start.2 = (f32[64,2048]{1,0:T(8,128)S(1)}, f32[64,2048]{1,0:T(8,128)S(1)}, u32[]{:S(2)}, u32[]{:S(2)}) collective-permute-start(f32[64,2048]{1,0:T(8,128)S(1)} %join_a.1), channel_id=1, source_target_pairs={{0,32},{1,33},{2,34},{3,35},{4,36},{5,37},{6,38},{7,39},{8,40},{9,... | collective-permute-start | bytes 1572872 | tf_op jit(solution)/shard_map/ppermute | solution.py:22
  6.6 16.4 %collective-permute-start.1 = (f32[32,2048]{1,0:T(8,128)S(1)}, f32[32,2048]{1,0:T(8,128)S(1)}, u32[]{:S(2)}, u32[]{:S(2)}) collective-permute-start(f32[32,2048]{1,0:T(8,128)S(1)} %get-tuple-element.37), channel_id=1, source_target_pairs={{0,64},{1,65},{2,66},{3,67},{4,68},{5,69},{6,70},{7,71},{8,72},{9,... | collective-permute-start | bytes 786440 | tf_op jit(solution)/shard_map/ppermute | solution.py:22
  10.2 12.7 %collective-permute-start.4 = (f32[64,1024]{1,0:T(8,128)S(1)}, f32[64,1024]{1,0:T(8,128)S(1)}, u32[]{:S(2)}, u32[]{:S(2)}) collective-permute-start(f32[64,1024]{1,0:T(8,128)S(1)} %get-tuple-element.42), channel_id=1, source_target_pairs={{0,4},{1,5},{2,6},{3,7},{4,8},{5,9},{6,10},{7,11},{8,12},{9,13},{1... | collective-permute-start | bytes 786440 | tf_op jit(solution)/shard_map/ppermute | solution.py:22
  11.9 11.1 %collective-permute-start.5 = (f32[64,1024]{1,0:T(8,128)S(1)}, f32[64,1024]{1,0:T(8,128)S(1)}, u32[]{:S(2)}, u32[]{:S(2)}) collective-permute-start(f32[64,1024]{1,0:T(8,128)S(1)} %get-tuple-element.43), channel_id=1, source_target_pairs={{0,8},{1,9},{2,10},{3,11},{4,12},{5,13},{6,14},{7,15},{8,0},{9,1},... | collective-permute-start | bytes 786440 | tf_op jit(solution)/shard_map/ppermute | solution.py:22
  14.8 8.2 %collective-permute-start.6 = (f32[64,1024]{1,0:T(8,128)S(1)}, f32[64,1024]{1,0:T(8,128)S(1)}, u32[]{:S(2)}, u32[]{:S(2)}) collective-permute-start(f32[64,1024]{1,0:T(8,128)S(1)} %get-tuple-element.44), channel_id=1, source_target_pairs={{0,12},{1,13},{2,14},{3,15},{4,0},{5,1},{6,2},{7,3},{8,4},{9,5},{1... | collective-permute-start | bytes 786440 | tf_op jit(solution)/shard_map/ppermute | solution.py:22
  23.0 2.4 %collective-permute-start.8 = (f32[64,2048]{1,0:T(8,128)S(1)}, f32[64,2048]{1,0:T(8,128)S(1)}, u32[]{:S(2)}, u32[]{:S(2)}) collective-permute-start(f32[64,2048]{1,0:T(8,128)S(1)} %collective-permute-done.2.side), channel_id=1, source_target_pairs={{0,16},{1,17},{2,18},{3,19},{4,20},{5,21},{6,22},{7,23},{8,24},{9,... | collective-permute-start | bytes 1572872 | tf_op jit(solution)/shard_map/ppermute | solution.py:22
  23.1 2.3 %collective-permute-start.7 = (f32[32,2048]{1,0:T(8,128)S(1)}, f32[32,2048]{1,0:T(8,128)S(1)}, u32[]{:S(2)}, u32[]{:S(2)}) collective-permute-start(f32[32,2048]{1,0:T(8,128)S(1)} %collective-permute-done.1.two), channel_id=1, source_target_pairs={{0,16},{1,17},{2,18},{3,19},{4,20},{5,21},{6,22},{7,23},{8,24},{9,... | collective-permute-start | bytes 786440 | tf_op jit(solution)/shard_map/ppermute | solution.py:22
  23.7 16.1 %collective-permute-start.13 = (f32[4,64,1024]{2,1,0:T(8,128)S(1)}, f32[4,64,1024]{2,1,0:T(8,128)S(1)}, u32[]{:S(2)}, u32[]{:S(2)}) collective-permute-start(f32[4,64,1024]{2,1,0:T(8,128)S(1)} %pad_maximum_fusion.refs_0_), channel_id=1, source_target_pairs={{0,32},{1,33},{2,34},{3,35},{4,36},{5,37},{6,38},{7,39},{8,40},{9,... | collective-permute-start | bytes 3145736 | tf_op jit(solution)/shard_map/ppermute | solution.py:22
  26.5 29.3 %collective-permute-start.10 = (f32[2,1024,256]{2,1,0:T(8,128)S(1)}, f32[2,1024,256]{2,1,0:T(8,128)S(1)}, u32[]{:S(2)}, u32[]{:S(2)}) collective-permute-start(f32[2,1024,256]{2,1,0:T(8,128)S(1)} %turn.1.a0), channel_id=1, source_target_pairs={{0,12},{1,13},{2,14},{3,15},{4,0},{5,1},{6,2},{7,3},{8,4},{9,5},{1... | collective-permute-start | bytes 6291464 | tf_op jit(solution)/shard_map/ppermute | solution.py:22
  29.6 29.3 %collective-permute-start.9 = (f32[2,1024,256]{2,1,0:T(8,128)S(1)}, f32[2,1024,256]{2,1,0:T(8,128)S(1)}, u32[]{:S(2)}, u32[]{:S(2)}) collective-permute-start(f32[2,1024,256]{2,1,0:T(8,128)S(1)} %turn.1.a0), channel_id=1, source_target_pairs={{0,4},{1,5},{2,6},{3,7},{4,8},{5,9},{6,10},{7,11},{8,12},{9,13},{1... | collective-permute-start | bytes 6291464 | tf_op jit(solution)/shard_map/ppermute | solution.py:22
  39.7 16.0 %collective-permute-start.14 = (f32[4,64,1024]{2,1,0:T(8,128)S(1)}, f32[4,64,1024]{2,1,0:T(8,128)S(1)}, u32[]{:S(2)}, u32[]{:S(2)}) collective-permute-start(f32[4,64,1024]{2,1,0:T(8,128)S(1)} %collective-permute-done.13.refs_1_), channel_id=1, source_target_pairs={{0,32},{1,33},{2,34},{3,35},{4,36},{5,37},{6,38},{7,39},{8,40},{9,... | collective-permute-start | bytes 3145736 | tf_op jit(solution)/shard_map/ppermute | solution.py:22
  55.8 16.0 %collective-permute-start.15 = (f32[4,64,1024]{2,1,0:T(8,128)S(1)}, f32[4,64,1024]{2,1,0:T(8,128)S(1)}, u32[]{:S(2)}, u32[]{:S(2)}) collective-permute-start(f32[4,64,1024]{2,1,0:T(8,128)S(1)} %collective-permute-done.14.refs_2_), channel_id=1, source_target_pairs={{0,32},{1,33},{2,34},{3,35},{4,36},{5,37},{6,38},{7,39},{8,40},{9,... | collective-permute-start | bytes 3145736 | tf_op jit(solution)/shard_map/ppermute | solution.py:22
  55.8 16.6 %collective-permute-start.12 = (f32[1024,256]{1,0:T(8,128)S(1)}, f32[1024,256]{1,0:T(8,128)S(1)}, u32[]{:S(2)}, u32[]{:S(2)}) collective-permute-start(f32[1024,256]{1,0:T(8,128)S(1)} %slice_bitcast_fusion), channel_id=1, source_target_pairs={{0,12},{1,13},{2,14},{3,15},{4,0},{5,1},{6,2},{7,3},{8,4},{9,5},{1... | collective-permute-start | bytes 3145736 | tf_op jit(solution)/shard_map/ppermute | solution.py:22
  59.0 16.1 %collective-permute-start.11 = (f32[1024,256]{1,0:T(8,128)S(1)}, f32[1024,256]{1,0:T(8,128)S(1)}, u32[]{:S(2)}, u32[]{:S(2)}) collective-permute-start(f32[1024,256]{1,0:T(8,128)S(1)} %slice_bitcast_fusion.1), channel_id=1, source_target_pairs={{0,4},{1,5},{2,6},{3,7},{4,8},{5,9},{6,10},{7,11},{8,12},{9,13},{1... | collective-permute-start | bytes 3145736 | tf_op jit(solution)/shard_map/ppermute | solution.py:22
  78.5 16.1 %collective-permute-start.20 = (f32[1024,256]{1,0:T(8,128)S(1)}, f32[1024,256]{1,0:T(8,128)S(1)}, u32[]{:S(2)}, u32[]{:S(2)}) collective-permute-start(f32[1024,256]{1,0:T(8,128)S(1)} %get-tuple-element.64), channel_id=1, source_target_pairs={{0,3},{1,0},{2,1},{3,2},{4,7},{5,4},{6,5},{7,6},{8,11},{9,8},{10,9... | collective-permute-start | bytes 3145736 | tf_op jit(solution)/shard_map/ppermute | solution.py:22
  79.4 18.9 %collective-permute-start.17 = (f32[1024,256]{1,0:T(8,128)S(1)}, f32[1024,256]{1,0:T(8,128)S(1)}, u32[]{:S(2)}, u32[]{:S(2)}) collective-permute-start(f32[1024,256]{1,0:T(8,128)S(1)} %get-tuple-element.60), channel_id=1, source_target_pairs={{0,1},{1,2},{2,3},{3,0},{4,5},{5,6},{6,7},{7,4},{8,9},{9,10},{10,1... | collective-permute-start | bytes 3145736 | tf_op jit(solution)/shard_map/ppermute | solution.py:22
  88.6 16.8 %collective-permute-start.19 = (f32[1024,256]{1,0:T(8,128)S(1)}, f32[1024,256]{1,0:T(8,128)S(1)}, u32[]{:S(2)}, u32[]{:S(2)}) collective-permute-start(f32[1024,256]{1,0:T(8,128)S(1)} %get-tuple-element.62), channel_id=1, source_target_pairs={{0,1},{1,2},{2,3},{3,0},{4,5},{5,6},{6,7},{7,4},{8,9},{9,10},{10,1... | collective-permute-start | bytes 3145736 | tf_op jit(solution)/shard_map/ppermute | solution.py:22
  94.7 16.1 %collective-permute-start.21 = (f32[1024,256]{1,0:T(8,128)S(1)}, f32[1024,256]{1,0:T(8,128)S(1)}, u32[]{:S(2)}, u32[]{:S(2)}) collective-permute-start(f32[1024,256]{1,0:T(8,128)S(1)} %add.14), channel_id=1, source_target_pairs={{0,3},{1,0},{2,1},{3,2},{4,7},{5,4},{6,5},{7,6},{8,11},{9,8},{10,9... | collective-permute-start | bytes 3145736 | tf_op jit(solution)/shard_map/ppermute | solution.py:22
  94.8 27.2 %collective-permute-start.16 = (f32[1024,256]{1,0:T(8,128)S(1)}, f32[1024,256]{1,0:T(8,128)S(1)}, u32[]{:S(2)}, u32[]{:S(2)}) collective-permute-start(f32[1024,256]{1,0:T(8,128)S(1)} %get-tuple-element.58), channel_id=1, source_target_pairs={{0,3},{1,0},{2,1},{3,2},{4,7},{5,4},{6,5},{7,6},{8,11},{9,8},{10,9... | collective-permute-start | bytes 3145736 | tf_op jit(solution)/shard_map/ppermute | solution.py:22
  98.5 23.5 %collective-permute-start.18 = (f32[1024,256]{1,0:T(8,128)S(1)}, f32[1024,256]{1,0:T(8,128)S(1)}, u32[]{:S(2)}, u32[]{:S(2)}) collective-permute-start(f32[1024,256]{1,0:T(8,128)S(1)} %add.12), channel_id=1, source_target_pairs={{0,1},{1,2},{2,3},{3,0},{4,5},{5,6},{6,7},{7,4},{8,9},{9,10},{10,1... | collective-permute-start | bytes 3145736 | tf_op jit(solution)/shard_map/ppermute | solution.py:22
  111.0 11.0 %collective-permute-start.22 = (f32[1024,256]{1,0:T(8,128)S(1)}, f32[1024,256]{1,0:T(8,128)S(1)}, u32[]{:S(2)}, u32[]{:S(2)}) collective-permute-start(f32[1024,256]{1,0:T(8,128)S(1)} %add_add_fusion), channel_id=1, source_target_pairs={{0,16},{1,17},{2,18},{3,19},{4,20},{5,21},{6,22},{7,23},{8,24},{9,... | collective-permute-start | bytes 3145736 | tf_op jit(solution)/shard_map/ppermute | solution.py:22

commit v3 on v2

v3 whole, which is shorter than its diff:
```python
import functools
import itertools

import jax
import jax.numpy as jnp
from jax import lax
from jax.experimental import pallas as pl
from jax.experimental.pallas import tpu as pltpu
from jax.sharding import Mesh, PartitionSpec as P

N = 4
ALL = ("z", "c", "y", "x")
VMEM_LIMIT = 16 * 1024 * 1024


def permute(value, target):
    pairs = []
    for z, c, y, x in itertools.product(range(N), range(2), range(N), range(N)):
        tz, tc, ty, tx = target(z, c, y, x)
        place = ((tz % N * 2 + tc % 2) * N + ty % N) * N + tx % N
        pairs.append((((z * 2 + c) * N + y) * N + x, place))
    return lax.ppermute(value, ALL, pairs)


def swap(value):
    return permute(value, lambda z, c, y, x: (z, 1 - c, y, x))


def along_z(value, step):
    return permute(value, lambda z, c, y, x: (z + step * (1 - 2 * c), c, y, x))


def along_gather(value, step):
    return permute(value, lambda z, c, y, x: (z, c, y + step * (1 - c), x + step * c))


def along_reduce(value, step):
    return permute(value, lambda z, c, y, x: (z, c, y + step * c, x + step * (1 - c)))


def split(value):
    high = value.astype(jnp.bfloat16)
    low = (value - high.astype(jnp.float32)).astype(jnp.bfloat16)
    return high, low


def dot(first, second):
    return lax.dot_general(
        first, second, (((1,), (0,)), ((), ())), preferred_element_type=jnp.float32
    )


SMEM = pl.BlockSpec(memory_space=pltpu.SMEM)
VMEM = pl.BlockSpec(memory_space=pltpu.VMEM)
ANY = pl.BlockSpec(memory_space=pl.ANY)
HBM = pl.BlockSpec(memory_space=pltpu.HBM)
PARAMS = pltpu.CompilerParams(vmem_limit_bytes=VMEM_LIMIT)


def prepare_a_kernel(place, a_ref, own_ref, two_ref, side_ref, pass_ref):
    z, c = place[0], place[1]
    half = own_ref.shape[2]

    def piece(step, part):
        start = (lax.rem(z + step, N) * 2 + part) * half
        return a_ref[:, pl.ds(pl.multiple_of(start, half), half)]

    for part in range(2):
        mine = lax.rem(c + part, 2)
        own_ref[part] = piece(0, mine)
        two_ref[part] = piece(2, mine)
        side_ref[part] = piece(1 + 2 * c, mine)
        pass_ref[0, part] = piece(0, 1 - mine)
        pass_ref[1, part] = piece(3 - 2 * c, 1 - mine)


def prepare_a(a, place):
    rows, columns = a.shape
    piece = jax.ShapeDtypeStruct((2, rows, columns // (2 * N)), a.dtype)
    passed = jax.ShapeDtypeStruct((2, 2, rows, columns // (2 * N)), a.dtype)
    return pl.pallas_call(
        prepare_a_kernel,
        out_shape=(piece, piece, piece, passed),
        in_specs=[SMEM, VMEM],
        out_specs=(VMEM,) * 4,
        compiler_params=PARAMS,
        name="prepare_a",
    )(place, a)


STREAMS = 2
ORDER = (2, 1, 3, 0)


def prepare_b_kernel(place, b_ref, keep_ref, pass_ref):
    c, y, x = place[1], place[2], place[3]
    width = keep_ref.shape[2] // N
    for core, ref in ((c, keep_ref), (1 - c, pass_ref)):
        for g in range(N):
            for i, h in enumerate(ORDER):
                ty = lax.rem(y + g * (1 - core) + h * core, N)
                tx = lax.rem(x + g * core + h * (1 - core), N)
                start = pl.multiple_of(((ty * N + tx) * 2 + core) * width, width)
                ref[g, :, i * width : (i + 1) * width] = b_ref[:, pl.ds(start, width)]


def prepare_b(b, place):
    rows, columns = b.shape
    part = jax.ShapeDtypeStruct((N, rows, columns // (2 * N)), b.dtype)
    return pl.pallas_call(
        prepare_b_kernel,
        out_shape=(part, part),
        in_specs=[SMEM, VMEM],
        out_specs=(VMEM, VMEM),
        compiler_params=PARAMS,
        name="prepare_b",
    )(place, b)


def join_a_kernel(side, got, out_ref):
    rows = side.shape[1]
    out_ref[:, :rows] = side[...]
    out_ref[:, rows:] = got[1]


def join_a(side, got):
    _, rows, half = side.shape
    return pl.pallas_call(
        join_a_kernel,
        out_shape=jax.ShapeDtypeStruct((2, 2 * rows, half), side.dtype),
        in_specs=[VMEM] * 2,
        out_specs=VMEM,
        compiler_params=PARAMS,
        name="join_a",
    )(side, got)


def join_b_kernel(keep, got, *refs):
    rows = keep.shape[1]
    for g, ref in enumerate(refs):
        ref[:rows] = keep[g]
        ref[rows:] = got[g]


def join_b(keep, got):
    _, rows, columns = keep.shape
    return pl.pallas_call(
        join_b_kernel,
        out_shape=(jax.ShapeDtypeStruct((2 * rows, columns), keep.dtype),) * N,
        in_specs=[VMEM] * 2,
        out_specs=(VMEM,) * N,
        compiler_params=PARAMS,
        name="join_b",
    )(keep, got)


def panel_kernel(*refs):
    out_refs = refs[N:]
    width = out_refs[0].shape[2]
    for g in range(N):
        for part, ref in enumerate(out_refs):
            ref[g] = refs[g][:, part * width : (part + 1) * width]


def make_panels(blocks):
    rows, columns = blocks[0].shape
    out = jax.ShapeDtypeStruct((N, rows, columns // STREAMS), blocks[0].dtype)
    return pl.pallas_call(
        panel_kernel,
        out_shape=(out,) * STREAMS,
        in_specs=[VMEM] * N,
        out_specs=(VMEM,) * STREAMS,
        compiler_params=PARAMS,
        name="panel",
    )(*blocks)


def stack_kernel(own, got, side, two, two_got, side_got, *out_refs):
    rows = two.shape[1]
    for part, ref in enumerate(out_refs):
        blocks = [
            own[part],
            got[0, part],
            side[part, :rows],
            side[part, rows:],
            two[part],
            two_got[1 - part],
            side_got[1 - part, rows:],
            side_got[1 - part, :rows],
        ]
        for i, block in enumerate(blocks):
            ref[i * rows : (i + 1) * rows] = block


def stack(own, got, side, two, two_got, side_got):
    _, rows, half = two.shape
    out = jax.ShapeDtypeStruct((2 * N * rows, half), two.dtype)
    return pl.pallas_call(
        stack_kernel,
        out_shape=(out, out),
        in_specs=[VMEM] * 6,
        out_specs=(VMEM, VMEM),
        compiler_params=PARAMS,
        name="stack",
    )(own, got, side, two, two_got, side_got)


NEAR = 3


def split_a_kernel(*refs):
    high_ref, low_ref = refs[2 * NEAR :]
    for i in range(2 * NEAR):
        depth = refs[i].shape[0]
        place = slice(i % NEAR * depth, (i % NEAR + 1) * depth)
        high_ref[i // NEAR, :, place], low_ref[i // NEAR, :, place] = split(refs[i][...].T)


def split_a(tops, bottoms):
    depth, columns = tops[0].shape
    out = jax.ShapeDtypeStruct((2, columns, NEAR * depth), jnp.bfloat16)
    return pl.pallas_call(
        split_a_kernel,
        out_shape=(out, out),
        in_specs=[VMEM] * (2 * NEAR),
        out_specs=(VMEM, VMEM),
        compiler_params=PARAMS,
        name="split_a",
    )(*tops, *bottoms)


def split_b_kernel(*refs):
    high_ref, low_ref = refs[N:]
    slab = refs[0].shape[1]
    for i, g in enumerate((0, 1, 3, 2)):
        for s in range(N):
            place = slice((i * N + s) * slab, (i * N + s + 1) * slab)
            high_ref[place], low_ref[place] = split(refs[s][g])


def split_b(panels):
    _, slab, columns = panels[0].shape
    out = jax.ShapeDtypeStruct((N * N * slab, columns), jnp.bfloat16)
    return pl.pallas_call(
        split_b_kernel,
        out_shape=(out, out),
        in_specs=[VMEM] * N,
        out_specs=(VMEM, VMEM),
        compiler_params=PARAMS,
        name="split_b",
    )(*panels)


TILE = 512
WEIGHT = 2


def three_products(high, low, bh, bl):
    return dot(high, bh) + dot(high, bl) + dot(low, bh)


def near_kernel(high, low, bh, bl, *out_refs):
    depth = high.shape[2]
    for half, ref in enumerate(out_refs):
        rows, width = ref.shape
        for start in range(0, rows, TILE):
            tile = slice(start, start + TILE)
            ref[tile] = three_products(
                high[half, tile], low[half, tile], bh[:depth, :width], bl[:depth, :width]
            )


def first_kernel(top, bottom, near_top, near_bottom, bh, bl, far_high, far_low, *out_refs):
    depth = far_high.shape[2]
    rest = slice(bh.shape[0] - depth, bh.shape[0])
    for half, (far, near, ref) in enumerate(zip((top, bottom), (near_top, near_bottom), out_refs)):
        rows, width = ref.shape
        far_high[half], far_low[half] = split(far[...].T)
        for start in range(0, rows, TILE):
            tile = slice(start, start + TILE)
            ref[tile] = near[tile] + three_products(
                far_high[half, tile], far_low[half, tile], bh[rest, :width], bl[rest, :width]
            )


def product_kernel(tasks, high, low, far_high, far_low, *refs):
    near = high.shape[2]
    b_refs, out_refs = refs[: 2 * STREAMS], refs[2 * STREAMS :]
    for (half, place), ref in zip(tasks, out_refs):
        rows, width = ref.shape
        which, place = divmod(place, N // STREAMS)
        h, l = b_refs[2 * which : 2 * which + 2]
        columns = slice(place * width, (place + 1) * width)
        for start in range(0, rows, TILE):
            tile = slice(start, start + TILE)
            ref[tile] = three_products(
                high[half, tile], low[half, tile], h[:near, columns], l[:near, columns]
            ) + three_products(
                far_high[half, tile], far_low[half, tile], h[near:, columns], l[near:, columns]
            )


def cost(rows, depth, width):
    return pl.CostEstimate(
        flops=12 * rows * depth * width, bytes_accessed=8 * rows * width, transcendentals=0
    )


def near_product(high, low, bh, bl):
    _, rows, depth = high.shape
    width = bh.shape[1] * STREAMS // N
    out = jax.ShapeDtypeStruct((rows, width), jnp.float32)
    return pl.pallas_call(
        near_kernel,
        out_shape=(out, out),
        in_specs=[VMEM] * 4,
        out_specs=(VMEM,) * 2,
        compiler_params=PARAMS,
        cost_estimate=cost(rows, WEIGHT * depth, width),
        name="near_product",
    )(high, low, bh, bl)


def first_product(top, bottom, near_top, near_bottom, bh, bl):
    depth, rows = top.shape
    width = bh.shape[1] * STREAMS // N
    far = jax.ShapeDtypeStruct((2, rows, depth), jnp.bfloat16)
    out = jax.ShapeDtypeStruct((rows, width), jnp.float32)
    return pl.pallas_call(
        first_kernel,
        out_shape=(far, far, out, out),
        in_specs=[VMEM] * 6,
        out_specs=(VMEM,) * 4,
        compiler_params=PARAMS,
        cost_estimate=cost(rows, depth, width),
        name="first_product",
    )(top, bottom, near_top, near_bottom, bh, bl)


def product(tasks, high, low, far_high, far_low, *b):
    _, rows, depth = far_high.shape
    width = b[0].shape[1] * STREAMS // N
    out = jax.ShapeDtypeStruct((rows, width), jnp.float32)
    tasks = tuple((half, ORDER.index(r)) for half, r in tasks)
    return pl.pallas_call(
        functools.partial(product_kernel, tasks),
        out_shape=(out, out),
        in_specs=[VMEM] * (4 + 2 * STREAMS),
        out_specs=(VMEM,) * 2,
        compiler_params=PARAMS,
        cost_estimate=cost(rows, N * depth, width),
        name="product",
    )(high, low, far_high, far_low, *b)


def finish_kernel(place, top0, top3, top1, got, out_ref, mine, sems):
    rows, width = top0.shape
    tile = rows // 4
    copies = []
    for i in range(4):
        tile_rows = slice(i * tile, (i + 1) * tile)
        mine[tile_rows] = top0[tile_rows] + top3[tile_rows] + top1[tile_rows]
        for k, ref, core in ((0, mine, place[1]), (1, got, 1 - place[1])):
            start = pl.multiple_of(core * width, width)
            copy = pltpu.make_async_copy(
                ref.at[tile_rows], out_ref.at[tile_rows, pl.ds(start, width)], sems.at[k, i]
            )
            copy.start()
            copies.append(copy)
    for copy in copies:
        copy.wait()


def finish(place, top0, top3, top1, got):
    rows, width = top0.shape
    return pl.pallas_call(
        finish_kernel,
        out_shape=jax.ShapeDtypeStruct((rows, 2 * width), jnp.float32),
        in_specs=[SMEM] + [VMEM] * 4,
        out_specs=HBM,
        scratch_shapes=[pltpu.VMEM((rows, width), jnp.float32), pltpu.SemaphoreType.DMA((2, 4))],
        compiler_params=PARAMS,
        name="finish",
    )(place, top0, top3, top1, got)


TOP, BOTTOM = 0, 1


def shards(a, b):
    place = jnp.stack([lax.axis_index(name) for name in ALL]).astype(jnp.int32)

    own, two, side, handed = prepare_a(a, place)
    two = along_z(two, 2)
    got = swap(handed)
    side = along_z(join_a(side, got), 1)

    keep, give = prepare_b(b, place)
    blocks = join_b(keep, swap(give))
    blocks = [blocks[0]] + [along_gather(blocks[g], g) for g in range(1, N)]
    two, side, blocks = lax.optimization_barrier((two, side, blocks))

    two_got, side_got = swap(two), swap(side)
    panels = make_panels(blocks)
    two_got, side_got, panels = lax.optimization_barrier((two_got, side_got, panels))
    streams = [[panel] for panel in panels]
    for _ in range(N - 1):
        for stream in streams:
            stream.append(along_z(stream[-1], 1))

    top, bottom = stack(own, got, side, two, two_got, side_got)
    top_behind = along_gather(top, 1)
    bottom_ahead = along_gather(bottom, -1)
    bottom_behind = along_gather(bottom, 1)
    top_ahead = along_gather(top, -1)
    top_far = along_gather(top_behind, 1)
    bottom_far = along_gather(bottom_ahead, -1)

    high, low = split_a((top, top_behind, top_ahead), (bottom, bottom_behind, bottom_ahead))
    splits = [half for stream in streams for half in split_b(stream)]
    near = near_product(high, low, *splits[:2])
    far_high, far_low, top2, bottom2 = first_product(top_far, bottom_far, *near, *splits[:2])
    operands = (high, low, far_high, far_low, *splits)
    bottom1, top3 = product(((BOTTOM, 1), (TOP, 3)), *operands)
    top1, bottom3 = product(((TOP, 1), (BOTTOM, 3)), *operands)

    top2 = along_reduce(top2, 1)
    bottom2 = along_reduce(bottom2, -1)
    top2, bottom2, operands = lax.optimization_barrier((top2, bottom2, operands))
    bottom1 = along_reduce(bottom1, 1)
    top3 = along_reduce(top3, -1)
    top1 = along_reduce(top1 + top2, 1)
    bottom3 = along_reduce(bottom3 + bottom2, -1)
    top0, bottom0 = product(((TOP, 0), (BOTTOM, 0)), *operands)
    got = swap(bottom0 + bottom1 + bottom3)
    return finish(place, top0, top3, top1, got)


def solution(mesh):
    fine = Mesh(mesh.devices.reshape(N, 2, N, N), ALL)
    return jax.shard_map(
        shards,
        mesh=fine,
        in_specs=(P(ALL, None), P(ALL, None)),
        out_specs=P(("z", "c"), ("y", "x")),
        check_vma=False,
    )
```

time: 125 us -> 118 us (0.944)
  waiting for transfers between devices: 74.9 us -> 63.1 us
  starting transfers between devices: 25.9 us -> 31.9 us
    ppermute x23 -> x28, waiting for transfers between devices: 74.9 us -> 63.1 us  [permute(): return lax.ppermute(value, ALL, pairs)]
    ppermute x23 -> x28, starting transfers between devices: 25.9 us -> 31.9 us  [permute(): return lax.ppermute(value, ALL, pairs)]
    pallas_call x1, Pallas kernels: 3.41 us -> 1.23 us  [first_product(): pl.pallas_call(first_kernel, out_shape=(far, far, out, out), in_specs=[VM...]
    pallas_call x7 -> x9, Pallas kernels: 14.8 us -> 16.7 us  [the longest x3 10.2 us: product(): pl.pallas_call(functools.partial(product_kernel, tasks), out_shape=(out,...]
  transfers between devices with their start and end apart: 23 -> 28, of which waited for: 10 -> 12; matrix products, arithmetic and copies ran while one was open for 1% -> 0% of each run, Pallas kernels for 11% -> 15%
where the time goes in v3:
time: 118 us
  waiting for transfers between devices  63.1 us (53%)
  starting transfers between devices  31.9 us (27%)
  Pallas kernels  19.8 us (17%)
  local copies, waits for them, and re-layouts  2.45 us (2%)
    ppermute x28, waiting for transfers between devices, permute(): return lax.ppermute(value, ALL, pairs)  63.1 us
    ppermute x28, starting transfers between devices, permute(): return lax.ppermute(value, ALL, pairs)  31.9 us
    pallas_call x3, Pallas kernels, product(): pl.pallas_call(functools.partial(product_kernel, tasks), out_shape=(out,...  10.2 us
    pallas_call x1, Pallas kernels, near_product(): pl.pallas_call(near_kernel, out_shape=(out, out), in_specs=[VMEM] * 4, ou...  2.59 us
    unnamed x4, local copies, waits for them, and re-layouts  2.45 us
  transfers between devices with their start and end apart: 28, of which 12 were waited for; matrix products, arithmetic and copies ran while one was open for 0% of the time, Pallas kernels for 15%

profile of v3, /device:TPU:6, one launch (start us, length us, event | category | flops | bytes accessed | tf_op | source)
XLA Modules:
  0.0 118.2 jit_solution(4679719140003082154)
XLA Ops:
  0.0 0.1 pad_add_fusion.place
  0.1 1.2 %copy-done = f32[32,8192]{1,0:T(8,128)S(1)} copy-done((f32[32,8192]{1,0:T(8,128)S(1)}, f32[32,8192]{1,0:T(8,128)}, u32[]{:S(2)}) %copy-start) | copy-done | bytes 1048600
  1.3 0.6 prepare_a.1
  1.9 0.1 collective-permute-start
  2.0 0.0 copy-start.1
  2.1 1.2 %copy-done.1 = f32[32,8192]{1,0:T(8,128)S(1)} copy-done((f32[32,8192]{1,0:T(8,128)S(1)}, f32[32,8192]{1,0:T(8,128)}, u32[]{:S(2)}) %copy-start.1) | copy-done | bytes 1048600
  3.3 0.7 prepare_b.1
  4.0 0.6 collective-permute-start.3
  4.6 2.0 %collective-permute-start.2 = (f32[2,64,1024]{2,1,0:T(8,128)S(1)}, f32[2,64,1024]{2,1,0:T(8,128)S(1)}, u32[]{:S(2)}, u32[]{:S(2)}) collective-permute-start(f32[2,64,1024]{2,1,0:T(8,128)S(1)} %join_a.1), channel_id=1, source_target_pairs={{0,32},{1,33},{2,34},{3,35},{4,36},{5,37},{6,38},{7,39},{8,40},{9,... | collective-permute-start | bytes 1572872 | tf_op jit(solution)/shard_map/ppermute | solution.py:22
  6.6 3.6 %collective-permute-start.1 = (f32[2,32,1024]{2,1,0:T(8,128)S(1)}, f32[2,32,1024]{2,1,0:T(8,128)S(1)}, u32[]{:S(2)}, u32[]{:S(2)}) collective-permute-start(f32[2,32,1024]{2,1,0:T(8,128)S(1)} %get-tuple-element.59), channel_id=1, source_target_pairs={{0,64},{1,65},{2,66},{3,67},{4,68},{5,69},{6,70},{7,71},{8,72},{9,... | collective-permute-start | bytes 786440 | tf_op jit(solution)/shard_map/ppermute | solution.py:22
  10.2 0.0 collective-permute-done.3.got
  10.2 0.1 join_b.1
  10.3 1.6 %collective-permute-start.4 = (f32[64,1024]{1,0:T(8,128)S(1)}, f32[64,1024]{1,0:T(8,128)S(1)}, u32[]{:S(2)}, u32[]{:S(2)}) collective-permute-start(f32[64,1024]{1,0:T(8,128)S(1)} %get-tuple-element.64), channel_id=1, source_target_pairs={{0,4},{1,5},{2,6},{3,7},{4,8},{5,9},{6,10},{7,11},{8,12},{9,13},{1... | collective-permute-start | bytes 786440 | tf_op jit(solution)/shard_map/ppermute | solution.py:22
  11.9 2.9 %collective-permute-start.5 = (f32[64,1024]{1,0:T(8,128)S(1)}, f32[64,1024]{1,0:T(8,128)S(1)}, u32[]{:S(2)}, u32[]{:S(2)}) collective-permute-start(f32[64,1024]{1,0:T(8,128)S(1)} %get-tuple-element.65), channel_id=1, source_target_pairs={{0,8},{1,9},{2,10},{3,11},{4,12},{5,13},{6,14},{7,15},{8,0},{9,1},... | collective-permute-start | bytes 786440 | tf_op jit(solution)/shard_map/ppermute | solution.py:22
  14.8 1.3 %collective-permute-start.6 = (f32[64,1024]{1,0:T(8,128)S(1)}, f32[64,1024]{1,0:T(8,128)S(1)}, u32[]{:S(2)}, u32[]{:S(2)}) collective-permute-start(f32[64,1024]{1,0:T(8,128)S(1)} %get-tuple-element.66), channel_id=1, source_target_pairs={{0,12},{1,13},{2,14},{3,15},{4,0},{5,1},{6,2},{7,3},{8,4},{9,5},{1... | collective-permute-start | bytes 786440 | tf_op jit(solution)/shard_map/ppermute | solution.py:22
  16.1 6.8 %collective-permute-done.1.two = f32[2,32,1024]{2,1,0:T(8,128)S(1)} collective-permute-done((f32[2,32,1024]{2,1,0:T(8,128)S(1)}, f32[2,32,1024]{2,1,0:T(8,128)S(1)}, u32[]{:S(2)}, u32[]{:S(2)}) %collective-permute-start.1) | collective-permute-done | bytes 262176 | tf_op jit(solution)/shard_map/ppermute | solution.py:22
  23.0 0.0 collective-permute-done.2.side
  23.0 0.1 collective-permute-start.8
  23.1 0.5 collective-permute-start.7
  23.6 0.1 panel.1
  23.6 1.7 %collective-permute-done.7.two_got = f32[2,32,1024]{2,1,0:T(8,128)S(1)} collective-permute-done((f32[2,32,1024]{2,1,0:T(8,128)S(1)}, f32[2,32,1024]{2,1,0:T(8,128)S(1)}, u32[]{:S(2)}, u32[]{:S(2)}) %collective-permute-start.7) | collective-permute-done | bytes 262176 | tf_op jit(solution)/shard_map/ppermute | solution.py:22
  25.3 0.0 collective-permute-done.8.side_got
  25.3 0.0 collective-permute-start.20
  25.3 0.1 stack.21
  25.5 1.6 %collective-permute-start.9 = (f32[256,1024]{1,0:T(8,128)S(1)}, f32[256,1024]{1,0:T(8,128)S(1)}, u32[]{:S(2)}, u32[]{:S(2)}) collective-permute-start(f32[256,1024]{1,0:T(8,128)S(1)} %get-tuple-element.77.refs_0_), channel_id=1, source_target_pairs={{0,4},{1,5},{2,6},{3,7},{4,8},{5,9},{6,10},{7,11},{8,12},{9,13},{1... | collective-permute-start | bytes 3145736 | tf_op jit(solution)/shard_map/ppermute | solution.py:22
  27.1 1.7 %collective-permute-start.11 = (f32[256,1024]{1,0:T(8,128)S(1)}, f32[256,1024]{1,0:T(8,128)S(1)}, u32[]{:S(2)}, u32[]{:S(2)}) collective-permute-start(f32[256,1024]{1,0:T(8,128)S(1)} %get-tuple-element.78.refs_3_), channel_id=1, source_target_pairs={{0,12},{1,13},{2,14},{3,15},{4,0},{5,1},{6,2},{7,3},{8,4},{9,5},{1... | collective-permute-start | bytes 3145736 | tf_op jit(solution)/shard_map/ppermute | solution.py:22
  28.8 0.3 collective-permute-start.15
  29.0 6.7 %collective-permute-done.20.refs_1_ = f32[4,64,512]{2,1,0:T(8,128)S(1)} collective-permute-done((f32[4,64,512]{2,1,0:T(8,128)S(1)}, f32[4,64,512]{2,1,0:T(8,128)S(1)}, u32[]{:S(2)}, u32[]{:S(2)}) %collective-permute-start.20) | collective-permute-done | bytes 524320 | tf_op jit(solution)/shard_map/ppermute | solution.py:22
  35.7 3.0 %collective-permute-start.13 = (f32[256,1024]{1,0:T(8,128)S(1)}, f32[256,1024]{1,0:T(8,128)S(1)}, u32[]{:S(2)}, u32[]{:S(2)}) collective-permute-start(f32[256,1024]{1,0:T(8,128)S(1)} %get-tuple-element.77.refs_0_), channel_id=1, source_target_pairs={{0,12},{1,13},{2,14},{3,15},{4,0},{5,1},{6,2},{7,3},{8,4},{9,5},{1... | collective-permute-start | bytes 3145736 | tf_op jit(solution)/shard_map/ppermute | solution.py:22
  38.8 2.6 %collective-permute-done.15.refs_1_ = f32[4,64,512]{2,1,0:T(8,128)S(1)} collective-permute-done((f32[4,64,512]{2,1,0:T(8,128)S(1)}, f32[4,64,512]{2,1,0:T(8,128)S(1)}, u32[]{:S(2)}, u32[]{:S(2)}) %collective-permute-start.15) | collective-permute-done | bytes 524320 | tf_op jit(solution)/shard_map/ppermute | solution.py:22
  41.4 1.6 %collective-permute-start.14 = (f32[256,1024]{1,0:T(8,128)S(1)}, f32[256,1024]{1,0:T(8,128)S(1)}, u32[]{:S(2)}, u32[]{:S(2)}) collective-permute-start(f32[256,1024]{1,0:T(8,128)S(1)} %get-tuple-element.78.refs_3_), channel_id=1, source_target_pairs={{0,4},{1,5},{2,6},{3,7},{4,8},{5,9},{6,10},{7,11},{8,12},{9,13},{1... | collective-permute-start | bytes 3145736 | tf_op jit(solution)/shard_map/ppermute | solution.py:22
  42.9 4.0 %collective-permute-done.21.refs_2_ = f32[4,64,512]{2,1,0:T(8,128)S(1)} collective-permute-done((f32[4,64,512]{2,1,0:T(8,128)S(1)}, f32[4,64,512]{2,1,0:T(8,128)S(1)}, u32[]{:S(2)}, u32[]{:S(2)}) %collective-permute-start.21) | collective-permute-done | bytes 524320 | tf_op jit(solution)/shard_map/ppermute | solution.py:22
  47.0 0.0 collective-permute-start.16
  47.0 0.0 collective-permute-done.9.refs_1_
  47.0 1.6 %collective-permute-start.10 = (f32[256,1024]{1,0:T(8,128)S(1)}, f32[256,1024]{1,0:T(8,128)S(1)}, u32[]{:S(2)}, u32[]{:S(2)}) collective-permute-start(f32[256,1024]{1,0:T(8,128)S(1)} %collective-permute-done.9.refs_1_), channel_id=1, source_target_pairs={{0,4},{1,5},{2,6},{3,7},{4,8},{5,9},{6,10},{7,11},{8,12},{9,13},{1... | collective-permute-start | bytes 3145736 | tf_op jit(solution)/shard_map/ppermute | solution.py:22
  48.6 1.7 %collective-permute-start.12 = (f32[256,1024]{1,0:T(8,128)S(1)}, f32[256,1024]{1,0:T(8,128)S(1)}, u32[]{:S(2)}, u32[]{:S(2)}) collective-permute-start(f32[256,1024]{1,0:T(8,128)S(1)} %collective-permute-done.11.refs_5_), channel_id=1, source_target_pairs={{0,12},{1,13},{2,14},{3,15},{4,0},{5,1},{6,2},{7,3},{8,4},{9,5},{1... | collective-permute-start | bytes 3145736 | tf_op jit(solution)/shard_map/ppermute | solution.py:22
  50.2 7.1 %collective-permute-done.16.refs_2_ = f32[4,64,512]{2,1,0:T(8,128)S(1)} collective-permute-done((f32[4,64,512]{2,1,0:T(8,128)S(1)}, f32[4,64,512]{2,1,0:T(8,128)S(1)}, u32[]{:S(2)}, u32[]{:S(2)}) %collective-permute-start.16) | collective-permute-done | bytes 524320 | tf_op jit(solution)/shard_map/ppermute | solution.py:22
  57.4 0.0 collective-permute-start.17
  57.4 0.0 collective-permute-done.13.refs_2_
  57.4 1.7 %split_a.1 = (bf16[2,1024,768]{2,1,0:T(8,128)(2,1)S(1)}, bf16[2,1024,768]{2,1,0:T(8,128)(2,1)S(1)}) custom-call(f32[256,1024]{1,0:T(8,128)S(1)} %get-tuple-element.77.refs_0_, f32[256,1024]{1,0:T(8,128)S(1)} %collective-permute-done.9.refs_1_, f32[256,1024]{1,0:T(8,128)S(1)} %collective-permute-done.13.refs_2_, f32[256,1024]{1,0:T(8,128)S(1)} %get-tuple-element.78.refs_3_, ...), custom_call_target="tpu_custom_call" | custom-call | tf_op jit(solution)/shard_map/split_a/pallas_call | solution.py:222
  59.1 8.7 %collective-permute-done.17.refs_3_ = f32[4,64,512]{2,1,0:T(8,128)S(1)} collective-permute-done((f32[4,64,512]{2,1,0:T(8,128)S(1)}, f32[4,64,512]{2,1,0:T(8,128)S(1)}, u32[]{:S(2)}, u32[]{:S(2)}) %collective-permute-start.17) | collective-permute-done | bytes 524320 | tf_op jit(solution)/shard_map/ppermute | solution.py:22
  67.8 0.2 split_b.2
  68.0 2.6 %near_product.1 = (f32[1024,256]{1,0:T(8,128)S(1)}, f32[1024,256]{1,0:T(8,128)S(1)}) custom-call(bf16[2,1024,768]{2,1,0:T(8,128)(2,1)S(1)} %get-tuple-element.93.high, bf16[2,1024,768]{2,1,0:T(8,128)(2,1)S(1)} %get-tuple-element.94.low, bf16[1024,512]{1,0:T(8,128)(2,1)S(1)} %get-tuple-element.97.bh.refs_0_, bf16[1024,512]{1,0:T(8,128)(2,1)S(1)} %get-tuple-element.98.bl.refs_1_), custom_call_target="tpu_custom_call" | custom-call | flops 4831838208 | bytes 2097152 | tf_op jit(solution)/shard_map/near_product/pallas_call | solution.py:313
  70.6 1.2 %first_product.1 = (bf16[2,1024,256]{2,1,0:T(8,128)(2,1)S(1)}, bf16[2,1024,256]{2,1,0:T(8,128)(2,1)S(1)}, f32[1024,256]{1,0:T(8,128)S(1)}, f32[1024,256]{1,0:T(8,128)S(1)}) custom-call(f32[256,1024]{1,0:T(8,128)S(1)} %collective-permute-done.10.top, f32[256,1024]{1,0:T(8,128)S(1)} %collective-permute-done.12.bottom, ...), custom_call_target="tpu_custom_call" | custom-call | flops 805306368 | bytes 2097152 | tf_op jit(solution)/shard_map/first_product/pallas_call | solution.py:329
  71.8 0.7 collective-permute-start.18
  72.6 1.6 %collective-permute-start.19 = (f32[1024,256]{1,0:T(8,128)S(1)}, f32[1024,256]{1,0:T(8,128)S(1)}, u32[]{:S(2)}, u32[]{:S(2)}) collective-permute-start(f32[1024,256]{1,0:T(8,128)S(1)} %get-tuple-element.87), channel_id=1, source_target_pairs={{0,3},{1,0},{2,1},{3,2},{4,7},{5,4},{6,5},{7,6},{8,11},{9,8},{10,9... | collective-permute-start | bytes 3145736 | tf_op jit(solution)/shard_map/ppermute | solution.py:22
  74.1 0.2 split_b.3
  74.4 3.4 %product.4 = (f32[1024,256]{1,0:T(8,128)S(1)}, f32[1024,256]{1,0:T(8,128)S(1)}) custom-call(bf16[2,1024,768]{2,1,0:T(8,128)(2,1)S(1)} %get-tuple-element.93.high, bf16[2,1024,768]{2,1,0:T(8,128)(2,1)S(1)} %get-tuple-element.94.low, bf16[2,1024,256]{2,1,0:T(8,128)(2,1)S(1)} %get-tuple-element.95.far_high, ...), custom_call_target="tpu_custom_call" | custom-call | flops 3221225472 | bytes 2097152 | tf_op jit(solution)/shard_map/product/pallas_call | solution.py:345
  77.8 1.8 %collective-permute-start.25 = (f32[1024,256]{1,0:T(8,128)S(1)}, f32[1024,256]{1,0:T(8,128)S(1)}, u32[]{:S(2)}, u32[]{:S(2)}) collective-permute-start(f32[1024,256]{1,0:T(8,128)S(1)} %get-tuple-element.106), channel_id=1, source_target_pairs={{0,1},{1,2},{2,3},{3,0},{4,5},{5,6},{6,7},{7,4},{8,9},{9,10},{10,1... | collective-permute-start | bytes 3145736 | tf_op jit(solution)/shard_map/ppermute | solution.py:22
  79.5 3.4 %product.5 = (f32[1024,256]{1,0:T(8,128)S(1)}, f32[1024,256]{1,0:T(8,128)S(1)}) custom-call(bf16[2,1024,768]{2,1,0:T(8,128)(2,1)S(1)} %get-tuple-element.93.high, bf16[2,1024,768]{2,1,0:T(8,128)(2,1)S(1)} %get-tuple-element.94.low, bf16[2,1024,256]{2,1,0:T(8,128)(2,1)S(1)} %get-tuple-element.95.far_high, ...), custom_call_target="tpu_custom_call" | custom-call | flops 3221225472 | bytes 2097152 | tf_op jit(solution)/shard_map/product/pallas_call | solution.py:345
  82.9 4.0 %collective-permute-done.18 = f32[1024,256]{1,0:T(8,128)S(1)} collective-permute-done((f32[1024,256]{1,0:T(8,128)S(1)}, f32[1024,256]{1,0:T(8,128)S(1)}, u32[]{:S(2)}, u32[]{:S(2)}) %collective-permute-start.18) | collective-permute-done | bytes 1048608 | tf_op jit(solution)/shard_map/ppermute | solution.py:22
  86.9 1.7 %collective-permute-done.19 = f32[1024,256]{1,0:T(8,128)S(1)} collective-permute-done((f32[1024,256]{1,0:T(8,128)S(1)}, f32[1024,256]{1,0:T(8,128)S(1)}, u32[]{:S(2)}, u32[]{:S(2)}) %collective-permute-start.19) | collective-permute-done | bytes 1048608 | tf_op jit(solution)/shard_map/ppermute | solution.py:22
  88.6 0.1 add.14
  88.7 0.4 collective-permute-start.26
  89.1 0.8 collective-permute-start.23
  90.0 0.1 add.12
  90.1 2.5 %collective-permute-start.24 = (f32[1024,256]{1,0:T(8,128)S(1)}, f32[1024,256]{1,0:T(8,128)S(1)}, u32[]{:S(2)}, u32[]{:S(2)}) collective-permute-start(f32[1024,256]{1,0:T(8,128)S(1)} %add.12), channel_id=1, source_target_pairs={{0,1},{1,2},{2,3},{3,0},{4,5},{5,6},{6,7},{7,4},{8,9},{9,10},{10,1... | collective-permute-start | bytes 3145736 | tf_op jit(solution)/shard_map/ppermute | solution.py:22
  92.6 3.4 %product.3 = (f32[1024,256]{1,0:T(8,128)S(1)}, f32[1024,256]{1,0:T(8,128)S(1)}) custom-call(bf16[2,1024,768]{2,1,0:T(8,128)(2,1)S(1)} %get-tuple-element.93.high, bf16[2,1024,768]{2,1,0:T(8,128)(2,1)S(1)} %get-tuple-element.94.low, bf16[2,1024,256]{2,1,0:T(8,128)(2,1)S(1)} %get-tuple-element.95.far_high, ...), custom_call_target="tpu_custom_call" | custom-call | flops 3221225472 | bytes 2097152 | tf_op jit(solution)/shard_map/product/pallas_call | solution.py:345
  96.0 2.2 %collective-permute-done.25 = f32[1024,256]{1,0:T(8,128)S(1)} collective-permute-done((f32[1024,256]{1,0:T(8,128)S(1)}, f32[1024,256]{1,0:T(8,128)S(1)}, u32[]{:S(2)}, u32[]{:S(2)}) %collective-permute-start.25) | collective-permute-done | bytes 1048608 | tf_op jit(solution)/shard_map/ppermute | solution.py:22
  98.1 6.7 %collective-permute-done.26 = f32[1024,256]{1,0:T(8,128)S(1)} collective-permute-done((f32[1024,256]{1,0:T(8,128)S(1)}, f32[1024,256]{1,0:T(8,128)S(1)}, u32[]{:S(2)}, u32[]{:S(2)}) %collective-permute-start.26) | collective-permute-done | bytes 1048608 | tf_op jit(solution)/shard_map/ppermute | solution.py:22
  104.8 0.2 add_add_fusion
  105.0 0.1 collective-permute-start.27
  105.1 10.9 %collective-permute-done.23.top3 = f32[1024,256]{1,0:T(8,128)S(1)} collective-permute-done((f32[1024,256]{1,0:T(8,128)S(1)}, f32[1024,256]{1,0:T(8,128)S(1)}, u32[]{:S(2)}, u32[]{:S(2)}) %collective-permute-start.23) | collective-permute-done | bytes 1048608 | tf_op jit(solution)/shard_map/ppermute | solution.py:22
  116.0 2.0 %finish.1 = f32[1024,512]{1,0:T(8,128)} custom-call(s32[4]{0:T(128)S(1)} %pad_add_fusion.place, f32[1024,256]{1,0:T(8,128)S(1)} %get-tuple-element.101.top0, f32[1024,256]{1,0:T(8,128)S(1)} %collective-permute-done.23.top3, f32[1024,256]{1,0:T(8,128)S(1)} %collective-permute-done.24.top1, f32[1024,256]{1,0:T(8,128)S(1)} %collective-permute-done.27.got), custom_call_target="tpu_custom_call" | custom-call | tf_op jit(solution)/shard_map/finish/pallas_call | solution.py:376
  (15 shorter events, 0.1 us)
Async XLA Ops:
  0.1 1.2 %copy-start = (f32[32,8192]{1,0:T(8,128)S(1)}, f32[32,8192]{1,0:T(8,128)}, u32[]{:S(2)}) copy-start(f32[32,8192]{1,0:T(8,128)} %a_ref.1) | copy-start | bytes 3145732
  1.9 2.6 %collective-permute-start = (f32[2,2,32,1024]{3,2,1,0:T(8,128)S(1)}, f32[2,2,32,1024]{3,2,1,0:T(8,128)S(1)}, u32[]{:S(2)}, u32[]{:S(2)}) collective-permute-start(f32[2,2,32,1024]{3,2,1,0:T(8,128)S(1)} %get-tuple-element.58), channel_id=1, source_target_pairs={{0,16},{1,17},{2,18},{3,19},{4,20},{5,21},{6,22},{7,23},{8,24},{9,... | collective-permute-start | bytes 1572872 | tf_op jit(solution)/shard_map/ppermute | solution.py:22
  2.0 1.2 %copy-start.1 = (f32[32,8192]{1,0:T(8,128)S(1)}, f32[32,8192]{1,0:T(8,128)}, u32[]{:S(2)}) copy-start(f32[32,8192]{1,0:T(8,128)} %b_ref.1) | copy-start | bytes 3145732
  4.0 6.2 %collective-permute-start.3 = (f32[4,32,1024]{2,1,0:T(8,128)S(1)}, f32[4,32,1024]{2,1,0:T(8,128)S(1)}, u32[]{:S(2)}, u32[]{:S(2)}) collective-permute-start(f32[4,32,1024]{2,1,0:T(8,128)S(1)} %get-tuple-element.62), channel_id=1, source_target_pairs={{0,16},{1,17},{2,18},{3,19},{4,20},{5,21},{6,22},{7,23},{8,24},{9,... | collective-permute-start | bytes 1572872 | tf_op jit(solution)/shard_map/ppermute | solution.py:22
  4.6 18.4 %collective-permute-start.2 = (f32[2,64,1024]{2,1,0:T(8,128)S(1)}, f32[2,64,1024]{2,1,0:T(8,128)S(1)}, u32[]{:S(2)}, u32[]{:S(2)}) collective-permute-start(f32[2,64,1024]{2,1,0:T(8,128)S(1)} %join_a.1), channel_id=1, source_target_pairs={{0,32},{1,33},{2,34},{3,35},{4,36},{5,37},{6,38},{7,39},{8,40},{9,... | collective-permute-start | bytes 1572872 | tf_op jit(solution)/shard_map/ppermute | solution.py:22
  6.6 16.4 %collective-permute-start.1 = (f32[2,32,1024]{2,1,0:T(8,128)S(1)}, f32[2,32,1024]{2,1,0:T(8,128)S(1)}, u32[]{:S(2)}, u32[]{:S(2)}) collective-permute-start(f32[2,32,1024]{2,1,0:T(8,128)S(1)} %get-tuple-element.59), channel_id=1, source_target_pairs={{0,64},{1,65},{2,66},{3,67},{4,68},{5,69},{6,70},{7,71},{8,72},{9,... | collective-permute-start | bytes 786440 | tf_op jit(solution)/shard_map/ppermute | solution.py:22
  10.3 12.7 %collective-permute-start.4 = (f32[64,1024]{1,0:T(8,128)S(1)}, f32[64,1024]{1,0:T(8,128)S(1)}, u32[]{:S(2)}, u32[]{:S(2)}) collective-permute-start(f32[64,1024]{1,0:T(8,128)S(1)} %get-tuple-element.64), channel_id=1, source_target_pairs={{0,4},{1,5},{2,6},{3,7},{4,8},{5,9},{6,10},{7,11},{8,12},{9,13},{1... | collective-permute-start | bytes 786440 | tf_op jit(solution)/shard_map/ppermute | solution.py:22
  11.9 11.1 %collective-permute-start.5 = (f32[64,1024]{1,0:T(8,128)S(1)}, f32[64,1024]{1,0:T(8,128)S(1)}, u32[]{:S(2)}, u32[]{:S(2)}) collective-permute-start(f32[64,1024]{1,0:T(8,128)S(1)} %get-tuple-element.65), channel_id=1, source_target_pairs={{0,8},{1,9},{2,10},{3,11},{4,12},{5,13},{6,14},{7,15},{8,0},{9,1},... | collective-permute-start | bytes 786440 | tf_op jit(solution)/shard_map/ppermute | solution.py:22
  14.8 8.2 %collective-permute-start.6 = (f32[64,1024]{1,0:T(8,128)S(1)}, f32[64,1024]{1,0:T(8,128)S(1)}, u32[]{:S(2)}, u32[]{:S(2)}) collective-permute-start(f32[64,1024]{1,0:T(8,128)S(1)} %get-tuple-element.66), channel_id=1, source_target_pairs={{0,12},{1,13},{2,14},{3,15},{4,0},{5,1},{6,2},{7,3},{8,4},{9,5},{1... | collective-permute-start | bytes 786440 | tf_op jit(solution)/shard_map/ppermute | solution.py:22
  23.0 2.4 %collective-permute-start.8 = (f32[2,64,1024]{2,1,0:T(8,128)S(1)}, f32[2,64,1024]{2,1,0:T(8,128)S(1)}, u32[]{:S(2)}, u32[]{:S(2)}) collective-permute-start(f32[2,64,1024]{2,1,0:T(8,128)S(1)} %collective-permute-done.2.side), channel_id=1, source_target_pairs={{0,16},{1,17},{2,18},{3,19},{4,20},{5,21},{6,22},{7,23},{8,24},{9,... | collective-permute-start | bytes 1572872 | tf_op jit(solution)/shard_map/ppermute | solution.py:22
  23.1 2.3 %collective-permute-start.7 = (f32[2,32,1024]{2,1,0:T(8,128)S(1)}, f32[2,32,1024]{2,1,0:T(8,128)S(1)}, u32[]{:S(2)}, u32[]{:S(2)}) collective-permute-start(f32[2,32,1024]{2,1,0:T(8,128)S(1)} %collective-permute-done.1.two), channel_id=1, source_target_pairs={{0,16},{1,17},{2,18},{3,19},{4,20},{5,21},{6,22},{7,23},{8,24},{9,... | collective-permute-start | bytes 786440 | tf_op jit(solution)/shard_map/ppermute | solution.py:22
  25.3 10.4 %collective-permute-start.20 = (f32[4,64,512]{2,1,0:T(8,128)S(1)}, f32[4,64,512]{2,1,0:T(8,128)S(1)}, u32[]{:S(2)}, u32[]{:S(2)}) collective-permute-start(f32[4,64,512]{2,1,0:T(8,128)S(1)} %get-tuple-element.90.refs_0_), channel_id=1, source_target_pairs={{0,32},{1,33},{2,34},{3,35},{4,36},{5,37},{6,38},{7,39},{8,40},{9,... | collective-permute-start | bytes 1572872 | tf_op jit(solution)/shard_map/ppermute | solution.py:22
  25.5 21.5 %collective-permute-start.9 = (f32[256,1024]{1,0:T(8,128)S(1)}, f32[256,1024]{1,0:T(8,128)S(1)}, u32[]{:S(2)}, u32[]{:S(2)}) collective-permute-start(f32[256,1024]{1,0:T(8,128)S(1)} %get-tuple-element.77.refs_0_), channel_id=1, source_target_pairs={{0,4},{1,5},{2,6},{3,7},{4,8},{5,9},{6,10},{7,11},{8,12},{9,13},{1... | collective-permute-start | bytes 3145736 | tf_op jit(solution)/shard_map/ppermute | solution.py:22
  27.1 21.4 %collective-permute-start.11 = (f32[256,1024]{1,0:T(8,128)S(1)}, f32[256,1024]{1,0:T(8,128)S(1)}, u32[]{:S(2)}, u32[]{:S(2)}) collective-permute-start(f32[256,1024]{1,0:T(8,128)S(1)} %get-tuple-element.78.refs_3_), channel_id=1, source_target_pairs={{0,12},{1,13},{2,14},{3,15},{4,0},{5,1},{6,2},{7,3},{8,4},{9,5},{1... | collective-permute-start | bytes 3145736 | tf_op jit(solution)/shard_map/ppermute | solution.py:22
  28.8 12.6 %collective-permute-start.15 = (f32[4,64,512]{2,1,0:T(8,128)S(1)}, f32[4,64,512]{2,1,0:T(8,128)S(1)}, u32[]{:S(2)}, u32[]{:S(2)}) collective-permute-start(f32[4,64,512]{2,1,0:T(8,128)S(1)} %get-tuple-element.81.refs_0_), channel_id=1, source_target_pairs={{0,32},{1,33},{2,34},{3,35},{4,36},{5,37},{6,38},{7,39},{8,40},{9,... | collective-permute-start | bytes 1572872 | tf_op jit(solution)/shard_map/ppermute | solution.py:22
  35.7 11.2 %collective-permute-start.21 = (f32[4,64,512]{2,1,0:T(8,128)S(1)}, f32[4,64,512]{2,1,0:T(8,128)S(1)}, u32[]{:S(2)}, u32[]{:S(2)}) collective-permute-start(f32[4,64,512]{2,1,0:T(8,128)S(1)} %collective-permute-done.20.refs_1_), channel_id=1, source_target_pairs={{0,32},{1,33},{2,34},{3,35},{4,36},{5,37},{6,38},{7,39},{8,40},{9,... | collective-permute-start | bytes 1572872 | tf_op jit(solution)/shard_map/ppermute | solution.py:22
  35.7 21.6 %collective-permute-start.13 = (f32[256,1024]{1,0:T(8,128)S(1)}, f32[256,1024]{1,0:T(8,128)S(1)}, u32[]{:S(2)}, u32[]{:S(2)}) collective-permute-start(f32[256,1024]{1,0:T(8,128)S(1)} %get-tuple-element.77.refs_0_), channel_id=1, source_target_pairs={{0,12},{1,13},{2,14},{3,15},{4,0},{5,1},{6,2},{7,3},{8,4},{9,5},{1... | collective-permute-start | bytes 3145736 | tf_op jit(solution)/shard_map/ppermute | solution.py:22
  41.4 16.0 %collective-permute-start.14 = (f32[256,1024]{1,0:T(8,128)S(1)}, f32[256,1024]{1,0:T(8,128)S(1)}, u32[]{:S(2)}, u32[]{:S(2)}) collective-permute-start(f32[256,1024]{1,0:T(8,128)S(1)} %get-tuple-element.78.refs_3_), channel_id=1, source_target_pairs={{0,4},{1,5},{2,6},{3,7},{4,8},{5,9},{6,10},{7,11},{8,12},{9,13},{1... | collective-permute-start | bytes 3145736 | tf_op jit(solution)/shard_map/ppermute | solution.py:22
  47.0 10.4 %collective-permute-start.16 = (f32[4,64,512]{2,1,0:T(8,128)S(1)}, f32[4,64,512]{2,1,0:T(8,128)S(1)}, u32[]{:S(2)}, u32[]{:S(2)}) collective-permute-start(f32[4,64,512]{2,1,0:T(8,128)S(1)} %collective-permute-done.15.refs_1_), channel_id=1, source_target_pairs={{0,32},{1,33},{2,34},{3,35},{4,36},{5,37},{6,38},{7,39},{8,40},{9,... | collective-permute-start | bytes 1572872 | tf_op jit(solution)/shard_map/ppermute | solution.py:22
  47.0 23.6 %collective-permute-start.10 = (f32[256,1024]{1,0:T(8,128)S(1)}, f32[256,1024]{1,0:T(8,128)S(1)}, u32[]{:S(2)}, u32[]{:S(2)}) collective-permute-start(f32[256,1024]{1,0:T(8,128)S(1)} %collective-permute-done.9.refs_1_), channel_id=1, source_target_pairs={{0,4},{1,5},{2,6},{3,7},{4,8},{5,9},{6,10},{7,11},{8,12},{9,13},{1... | collective-permute-start | bytes 3145736 | tf_op jit(solution)/shard_map/ppermute | solution.py:22
  48.6 22.1 %collective-permute-start.12 = (f32[256,1024]{1,0:T(8,128)S(1)}, f32[256,1024]{1,0:T(8,128)S(1)}, u32[]{:S(2)}, u32[]{:S(2)}) collective-permute-start(f32[256,1024]{1,0:T(8,128)S(1)} %collective-permute-done.11.refs_5_), channel_id=1, source_target_pairs={{0,12},{1,13},{2,14},{3,15},{4,0},{5,1},{6,2},{7,3},{8,4},{9,5},{1... | collective-permute-start | bytes 3145736 | tf_op jit(solution)/shard_map/ppermute | solution.py:22
  57.4 10.4 %collective-permute-start.17 = (f32[4,64,512]{2,1,0:T(8,128)S(1)}, f32[4,64,512]{2,1,0:T(8,128)S(1)}, u32[]{:S(2)}, u32[]{:S(2)}) collective-permute-start(f32[4,64,512]{2,1,0:T(8,128)S(1)} %collective-permute-done.16.refs_2_), channel_id=1, source_target_pairs={{0,32},{1,33},{2,34},{3,35},{4,36},{5,37},{6,38},{7,39},{8,40},{9,... | collective-permute-start | bytes 1572872 | tf_op jit(solution)/shard_map/ppermute | solution.py:22
  57.4 16.8 %collective-permute-start.22 = (f32[4,64,512]{2,1,0:T(8,128)S(1)}, f32[4,64,512]{2,1,0:T(8,128)S(1)}, u32[]{:S(2)}, u32[]{:S(2)}) collective-permute-start(f32[4,64,512]{2,1,0:T(8,128)S(1)} %collective-permute-done.21.refs_2_), channel_id=1, source_target_pairs={{0,32},{1,33},{2,34},{3,35},{4,36},{5,37},{6,38},{7,39},{8,40},{9,... | collective-permute-start | bytes 1572872 | tf_op jit(solution)/shard_map/ppermute | solution.py:22
  71.8 15.0 %collective-permute-start.18 = (f32[1024,256]{1,0:T(8,128)S(1)}, f32[1024,256]{1,0:T(8,128)S(1)}, u32[]{:S(2)}, u32[]{:S(2)}) collective-permute-start(f32[1024,256]{1,0:T(8,128)S(1)} %get-tuple-element.86), channel_id=1, source_target_pairs={{0,1},{1,2},{2,3},{3,0},{4,5},{5,6},{6,7},{7,4},{8,9},{9,10},{10,1... | collective-permute-start | bytes 3145736 | tf_op jit(solution)/shard_map/ppermute | solution.py:22
  72.6 16.0 %collective-permute-start.19 = (f32[1024,256]{1,0:T(8,128)S(1)}, f32[1024,256]{1,0:T(8,128)S(1)}, u32[]{:S(2)}, u32[]{:S(2)}) collective-permute-start(f32[1024,256]{1,0:T(8,128)S(1)} %get-tuple-element.87), channel_id=1, source_target_pairs={{0,3},{1,0},{2,1},{3,2},{4,7},{5,4},{6,5},{7,6},{8,11},{9,8},{10,9... | collective-permute-start | bytes 3145736 | tf_op jit(solution)/shard_map/ppermute | solution.py:22
  77.8 20.4 %collective-permute-start.25 = (f32[1024,256]{1,0:T(8,128)S(1)}, f32[1024,256]{1,0:T(8,128)S(1)}, u32[]{:S(2)}, u32[]{:S(2)}) collective-permute-start(f32[1024,256]{1,0:T(8,128)S(1)} %get-tuple-element.106), channel_id=1, source_target_pairs={{0,1},{1,2},{2,3},{3,0},{4,5},{5,6},{6,7},{7,4},{8,9},{9,10},{10,1... | collective-permute-start | bytes 3145736 | tf_op jit(solution)/shard_map/ppermute | solution.py:22
  88.7 16.1 %collective-permute-start.26 = (f32[1024,256]{1,0:T(8,128)S(1)}, f32[1024,256]{1,0:T(8,128)S(1)}, u32[]{:S(2)}, u32[]{:S(2)}) collective-permute-start(f32[1024,256]{1,0:T(8,128)S(1)} %add.14), channel_id=1, source_target_pairs={{0,3},{1,0},{2,1},{3,2},{4,7},{5,4},{6,5},{7,6},{8,11},{9,8},{10,9... | collective-permute-start | bytes 3145736 | tf_op jit(solution)/shard_map/ppermute | solution.py:22
  89.1 26.9 %collective-permute-start.23 = (f32[1024,256]{1,0:T(8,128)S(1)}, f32[1024,256]{1,0:T(8,128)S(1)}, u32[]{:S(2)}, u32[]{:S(2)}) collective-permute-start(f32[1024,256]{1,0:T(8,128)S(1)} %get-tuple-element.102), channel_id=1, source_target_pairs={{0,3},{1,0},{2,1},{3,2},{4,7},{5,4},{6,5},{7,6},{8,11},{9,8},{10,9... | collective-permute-start | bytes 3145736 | tf_op jit(solution)/shard_map/ppermute | solution.py:22
  90.1 25.9 %collective-permute-start.24 = (f32[1024,256]{1,0:T(8,128)S(1)}, f32[1024,256]{1,0:T(8,128)S(1)}, u32[]{:S(2)}, u32[]{:S(2)}) collective-permute-start(f32[1024,256]{1,0:T(8,128)S(1)} %add.12), channel_id=1, source_target_pairs={{0,1},{1,2},{2,3},{3,0},{4,5},{5,6},{6,7},{7,4},{8,9},{9,10},{10,1... | collective-permute-start | bytes 3145736 | tf_op jit(solution)/shard_map/ppermute | solution.py:22
  105.0 11.0 %collective-permute-start.27 = (f32[1024,256]{1,0:T(8,128)S(1)}, f32[1024,256]{1,0:T(8,128)S(1)}, u32[]{:S(2)}, u32[]{:S(2)}) collective-permute-start(f32[1024,256]{1,0:T(8,128)S(1)} %add_add_fusion), channel_id=1, source_target_pairs={{0,16},{1,17},{2,18},{3,19},{4,20},{5,21},{6,22},{7,23},{8,24},{9,... | collective-permute-start | bytes 3145736 | tf_op jit(solution)/shard_map/ppermute | solution.py:22

commit v4 on v3

--- a/solution.py
+++ b/solution.py
@@ -88,7 +88,7 @@
     )(place, a)
 
 
-STREAMS = 2
+AHEAD = 3
 ORDER = (2, 1, 3, 0)
 
 
@@ -158,18 +158,21 @@
     out_refs = refs[N:]
     width = out_refs[0].shape[2]
     for g in range(N):
-        for part, ref in enumerate(out_refs):
-            ref[g] = refs[g][:, part * width : (part + 1) * width]
+        out_refs[0][g] = refs[g][:, :width]
+        out_refs[1][g] = refs[g][:, width:]
 
 
 def make_panels(blocks):
     rows, columns = blocks[0].shape
-    out = jax.ShapeDtypeStruct((N, rows, columns // STREAMS), blocks[0].dtype)
+    width = columns * AHEAD // N
     return pl.pallas_call(
         panel_kernel,
-        out_shape=(out,) * STREAMS,
+        out_shape=(
+            jax.ShapeDtypeStruct((N, rows, width), blocks[0].dtype),
+            jax.ShapeDtypeStruct((N, rows, columns - width), blocks[0].dtype),
+        ),
         in_specs=[VMEM] * N,
-        out_specs=(VMEM,) * STREAMS,
+        out_specs=(VMEM, VMEM),
         compiler_params=PARAMS,
         name="panel",
     )(*blocks)
@@ -252,7 +255,6 @@
 
 
 TILE = 512
-WEIGHT = 2
 
 
 def three_products(high, low, bh, bl):
@@ -283,20 +285,17 @@
             )
 
 
-def product_kernel(tasks, high, low, far_high, far_low, *refs):
+def product_kernel(tasks, high, low, far_high, far_low, bh, bl, *out_refs):
     near = high.shape[2]
-    b_refs, out_refs = refs[: 2 * STREAMS], refs[2 * STREAMS :]
     for (half, place), ref in zip(tasks, out_refs):
         rows, width = ref.shape
-        which, place = divmod(place, N // STREAMS)
-        h, l = b_refs[2 * which : 2 * which + 2]
         columns = slice(place * width, (place + 1) * width)
         for start in range(0, rows, TILE):
             tile = slice(start, start + TILE)
             ref[tile] = three_products(
-                high[half, tile], low[half, tile], h[:near, columns], l[:near, columns]
+                high[half, tile], low[half, tile], bh[:near, columns], bl[:near, columns]
             ) + three_products(
-                far_high[half, tile], far_low[half, tile], h[near:, columns], l[near:, columns]
+                far_high[half, tile], far_low[half, tile], bh[near:, columns], bl[near:, columns]
             )
 
 
@@ -308,7 +307,7 @@
 
 def near_product(high, low, bh, bl):
     _, rows, depth = high.shape
-    width = bh.shape[1] * STREAMS // N
+    width = bh.shape[1] // AHEAD
     out = jax.ShapeDtypeStruct((rows, width), jnp.float32)
     return pl.pallas_call(
         near_kernel,
@@ -316,14 +315,14 @@
         in_specs=[VMEM] * 4,
         out_specs=(VMEM,) * 2,
         compiler_params=PARAMS,
-        cost_estimate=cost(rows, WEIGHT * depth, width),
+        cost_estimate=cost(rows, depth, width),
         name="near_product",
     )(high, low, bh, bl)
 
 
 def first_product(top, bottom, near_top, near_bottom, bh, bl):
     depth, rows = top.shape
-    width = bh.shape[1] * STREAMS // N
+    width = bh.shape[1] // AHEAD
     far = jax.ShapeDtypeStruct((2, rows, depth), jnp.bfloat16)
     out = jax.ShapeDtypeStruct((rows, width), jnp.float32)
     return pl.pallas_call(
@@ -337,20 +336,21 @@
     )(top, bottom, near_top, near_bottom, bh, bl)
 
 
-def product(tasks, high, low, far_high, far_low, *b):
+def product(r, high, low, far_high, far_low, bh, bl):
     _, rows, depth = far_high.shape
-    width = b[0].shape[1] * STREAMS // N
+    place = ORDER.index(r)
+    width = bh.shape[1] // (AHEAD if place < AHEAD else N - AHEAD)
     out = jax.ShapeDtypeStruct((rows, width), jnp.float32)
-    tasks = tuple((half, ORDER.index(r)) for half, r in tasks)
+    tasks = ((TOP, place % AHEAD), (BOTTOM, place % AHEAD))
     return pl.pallas_call(
         functools.partial(product_kernel, tasks),
         out_shape=(out, out),
-        in_specs=[VMEM] * (4 + 2 * STREAMS),
+        in_specs=[VMEM] * 6,
         out_specs=(VMEM,) * 2,
         compiler_params=PARAMS,
         cost_estimate=cost(rows, N * depth, width),
         name="product",
-    )(high, low, far_high, far_low, *b)
+    )(high, low, far_high, far_low, bh, bl)
 
 
 def finish_kernel(place, top0, top3, top1, got, out_ref, mine, sems):
@@ -403,10 +403,11 @@
     two_got, side_got = swap(two), swap(side)
     panels = make_panels(blocks)
     two_got, side_got, panels = lax.optimization_barrier((two_got, side_got, panels))
-    streams = [[panel] for panel in panels]
+    panels, later = [panels[0]], [panels[1]]
     for _ in range(N - 1):
-        for stream in streams:
-            stream.append(along_z(stream[-1], 1))
+        panels.append(along_z(panels[-1], 1))
+    panels[-1], later[0] = lax.optimization_barrier((panels[-1], later[0]))
+    later.append(along_z(later[-1], 1))
 
     top, bottom = stack(own, got, side, two, two_got, side_got)
     top_behind = along_gather(top, 1)
@@ -417,21 +418,24 @@
     bottom_far = along_gather(bottom_ahead, -1)
 
     high, low = split_a((top, top_behind, top_ahead), (bottom, bottom_behind, bottom_ahead))
-    splits = [half for stream in streams for half in split_b(stream)]
-    near = near_product(high, low, *splits[:2])
-    far_high, far_low, top2, bottom2 = first_product(top_far, bottom_far, *near, *splits[:2])
-    operands = (high, low, far_high, far_low, *splits)
-    bottom1, top3 = product(((BOTTOM, 1), (TOP, 3)), *operands)
-    top1, bottom3 = product(((TOP, 1), (BOTTOM, 3)), *operands)
+    bh, bl = split_b(panels)
+    near = near_product(high, low, bh, bl)
+    far_high, far_low, top2, bottom2 = first_product(top_far, bottom_far, *near, bh, bl)
+    _, later[1] = lax.optimization_barrier((top2, later[1]))
+    later.append(along_z(later[-1], 1))
+    halves = (high, low, far_high, far_low)
+    top1, bottom1 = product(1, *halves, bh, bl)
+    top3, bottom3 = product(3, *halves, bh, bl)
 
     top2 = along_reduce(top2, 1)
     bottom2 = along_reduce(bottom2, -1)
-    top2, bottom2, operands = lax.optimization_barrier((top2, bottom2, operands))
+    _, later[2] = lax.optimization_barrier((top2, later[2]))
     bottom1 = along_reduce(bottom1, 1)
     top3 = along_reduce(top3, -1)
     top1 = along_reduce(top1 + top2, 1)
     bottom3 = along_reduce(bottom3 + bottom2, -1)
-    top0, bottom0 = product(((TOP, 0), (BOTTOM, 0)), *operands)
+    later.append(along_z(later[-1], 1))
+    top0, bottom0 = product(0, *halves, *split_b(later))
     got = swap(bottom0 + bottom1 + bottom3)
     return finish(place, top0, top3, top1, got)
 

time: 118 us -> 116 us (0.983)
  starting transfers between devices: 31.9 us -> 29.3 us
    ppermute x28, starting transfers between devices: 31.9 us -> 29.3 us  [permute(): return lax.ppermute(value, ALL, pairs)]
  transfers between devices with their start and end apart: 28 -> 28, of which waited for: 12 -> 12; matrix products, arithmetic and copies ran while one was open for 0% -> 0% of each run, Pallas kernels for 15% -> 14%
where the time goes in v4:
time: 116 us
  waiting for transfers between devices  63.2 us (54%)
  starting transfers between devices  29.3 us (25%)
  Pallas kernels  19.9 us (17%)
  local copies, waits for them, and re-layouts  2.45 us (2%)
    ppermute x28, waiting for transfers between devices, permute(): return lax.ppermute(value, ALL, pairs)  63.2 us
    ppermute x28, starting transfers between devices, permute(): return lax.ppermute(value, ALL, pairs)  29.3 us
    pallas_call x3, Pallas kernels, product(): pl.pallas_call(functools.partial(product_kernel, tasks), out_shape=(out,...  10.2 us
    pallas_call x1, Pallas kernels, near_product(): pl.pallas_call(near_kernel, out_shape=(out, out), in_specs=[VMEM] * 4, ou...  2.59 us
    unnamed x4, local copies, waits for them, and re-layouts  2.45 us
  transfers between devices with their start and end apart: 28, of which 12 were waited for; matrix products, arithmetic and copies ran while one was open for 0% of the time, Pallas kernels for 14%

profile of v4, /device:TPU:6, one launch (start us, length us, event | category | flops | bytes accessed | tf_op | source)
XLA Modules:
  0.0 115.7 jit_solution(11490726378720484938)
XLA Ops:
  0.0 0.1 pad_add_fusion.place
  0.1 1.2 %copy-done = f32[32,8192]{1,0:T(8,128)S(1)} copy-done((f32[32,8192]{1,0:T(8,128)S(1)}, f32[32,8192]{1,0:T(8,128)}, u32[]{:S(2)}) %copy-start) | copy-done | bytes 1048600
  1.3 0.6 prepare_a.1
  1.9 0.1 collective-permute-start
  2.0 0.0 copy-start.1
  2.1 1.2 %copy-done.1 = f32[32,8192]{1,0:T(8,128)S(1)} copy-done((f32[32,8192]{1,0:T(8,128)S(1)}, f32[32,8192]{1,0:T(8,128)}, u32[]{:S(2)}) %copy-start.1) | copy-done | bytes 1048600
  3.3 0.7 prepare_b.1
  4.0 0.6 collective-permute-start.3
  4.6 2.0 %collective-permute-start.2 = (f32[2,64,1024]{2,1,0:T(8,128)S(1)}, f32[2,64,1024]{2,1,0:T(8,128)S(1)}, u32[]{:S(2)}, u32[]{:S(2)}) collective-permute-start(f32[2,64,1024]{2,1,0:T(8,128)S(1)} %join_a.1), channel_id=1, source_target_pairs={{0,32},{1,33},{2,34},{3,35},{4,36},{5,37},{6,38},{7,39},{8,40},{9,... | collective-permute-start | bytes 1572872 | tf_op jit(solution)/shard_map/ppermute | solution.py:22
  6.6 3.6 %collective-permute-start.1 = (f32[2,32,1024]{2,1,0:T(8,128)S(1)}, f32[2,32,1024]{2,1,0:T(8,128)S(1)}, u32[]{:S(2)}, u32[]{:S(2)}) collective-permute-start(f32[2,32,1024]{2,1,0:T(8,128)S(1)} %get-tuple-element.53), channel_id=1, source_target_pairs={{0,64},{1,65},{2,66},{3,67},{4,68},{5,69},{6,70},{7,71},{8,72},{9,... | collective-permute-start | bytes 786440 | tf_op jit(solution)/shard_map/ppermute | solution.py:22
  10.2 0.0 collective-permute-done.3.got
  10.2 0.1 join_b.1
  10.3 1.6 %collective-permute-start.4 = (f32[64,1024]{1,0:T(8,128)S(1)}, f32[64,1024]{1,0:T(8,128)S(1)}, u32[]{:S(2)}, u32[]{:S(2)}) collective-permute-start(f32[64,1024]{1,0:T(8,128)S(1)} %get-tuple-element.58), channel_id=1, source_target_pairs={{0,4},{1,5},{2,6},{3,7},{4,8},{5,9},{6,10},{7,11},{8,12},{9,13},{1... | collective-permute-start | bytes 786440 | tf_op jit(solution)/shard_map/ppermute | solution.py:22
  11.9 2.9 %collective-permute-start.5 = (f32[64,1024]{1,0:T(8,128)S(1)}, f32[64,1024]{1,0:T(8,128)S(1)}, u32[]{:S(2)}, u32[]{:S(2)}) collective-permute-start(f32[64,1024]{1,0:T(8,128)S(1)} %get-tuple-element.59), channel_id=1, source_target_pairs={{0,8},{1,9},{2,10},{3,11},{4,12},{5,13},{6,14},{7,15},{8,0},{9,1},... | collective-permute-start | bytes 786440 | tf_op jit(solution)/shard_map/ppermute | solution.py:22
  14.8 1.3 %collective-permute-start.6 = (f32[64,1024]{1,0:T(8,128)S(1)}, f32[64,1024]{1,0:T(8,128)S(1)}, u32[]{:S(2)}, u32[]{:S(2)}) collective-permute-start(f32[64,1024]{1,0:T(8,128)S(1)} %get-tuple-element.60), channel_id=1, source_target_pairs={{0,12},{1,13},{2,14},{3,15},{4,0},{5,1},{6,2},{7,3},{8,4},{9,5},{1... | collective-permute-start | bytes 786440 | tf_op jit(solution)/shard_map/ppermute | solution.py:22
  16.1 6.8 %collective-permute-done.1.two = f32[2,32,1024]{2,1,0:T(8,128)S(1)} collective-permute-done((f32[2,32,1024]{2,1,0:T(8,128)S(1)}, f32[2,32,1024]{2,1,0:T(8,128)S(1)}, u32[]{:S(2)}, u32[]{:S(2)}) %collective-permute-start.1) | collective-permute-done | bytes 262176 | tf_op jit(solution)/shard_map/ppermute | solution.py:22
  23.0 0.0 collective-permute-done.5.refs_2_
  23.0 0.0 collective-permute-done.6.refs_3_
  23.0 0.0 collective-permute-done.2.side
  23.0 0.1 collective-permute-start.8
  23.1 0.5 collective-permute-start.7
  23.6 0.1 panel.1
  23.6 1.7 %collective-permute-done.7.two_got = f32[2,32,1024]{2,1,0:T(8,128)S(1)} collective-permute-done((f32[2,32,1024]{2,1,0:T(8,128)S(1)}, f32[2,32,1024]{2,1,0:T(8,128)S(1)}, u32[]{:S(2)}, u32[]{:S(2)}) %collective-permute-start.7) | collective-permute-done | bytes 262176 | tf_op jit(solution)/shard_map/ppermute | solution.py:22
  25.3 0.0 collective-permute-done.8.side_got
  25.3 0.1 stack.21
  25.5 1.6 %collective-permute-start.9 = (f32[256,1024]{1,0:T(8,128)S(1)}, f32[256,1024]{1,0:T(8,128)S(1)}, u32[]{:S(2)}, u32[]{:S(2)}) collective-permute-start(f32[256,1024]{1,0:T(8,128)S(1)} %get-tuple-element.71.refs_0_), channel_id=1, source_target_pairs={{0,4},{1,5},{2,6},{3,7},{4,8},{5,9},{6,10},{7,11},{8,12},{9,13},{1... | collective-permute-start | bytes 3145736 | tf_op jit(solution)/shard_map/ppermute | solution.py:22
  27.1 1.7 %collective-permute-start.12 = (f32[256,1024]{1,0:T(8,128)S(1)}, f32[256,1024]{1,0:T(8,128)S(1)}, u32[]{:S(2)}, u32[]{:S(2)}) collective-permute-start(f32[256,1024]{1,0:T(8,128)S(1)} %get-tuple-element.72.refs_3_), channel_id=1, source_target_pairs={{0,12},{1,13},{2,14},{3,15},{4,0},{5,1},{6,2},{7,3},{8,4},{9,5},{1... | collective-permute-start | bytes 3145736 | tf_op jit(solution)/shard_map/ppermute | solution.py:22
  28.8 9.8 %collective-permute-done.15.refs_1_ = f32[4,64,768]{2,1,0:T(8,128)S(1)} collective-permute-done((f32[4,64,768]{2,1,0:T(8,128)S(1)}, f32[4,64,768]{2,1,0:T(8,128)S(1)}, u32[]{:S(2)}, u32[]{:S(2)}) %collective-permute-start.15) | collective-permute-done | bytes 786464 | tf_op jit(solution)/shard_map/ppermute | solution.py:22
  38.5 0.0 collective-permute-start.16
  38.5 3.0 %collective-permute-start.10 = (f32[256,1024]{1,0:T(8,128)S(1)}, f32[256,1024]{1,0:T(8,128)S(1)}, u32[]{:S(2)}, u32[]{:S(2)}) collective-permute-start(f32[256,1024]{1,0:T(8,128)S(1)} %get-tuple-element.71.refs_0_), channel_id=1, source_target_pairs={{0,12},{1,13},{2,14},{3,15},{4,0},{5,1},{6,2},{7,3},{8,4},{9,5},{1... | collective-permute-start | bytes 3145736 | tf_op jit(solution)/shard_map/ppermute | solution.py:22
  41.6 0.0 collective-permute-start.11
  41.6 0.0 collective-permute-done.9.refs_1_
  41.6 0.6 collective-permute-start.13
  42.2 2.7 %collective-permute-start.14 = (f32[256,1024]{1,0:T(8,128)S(1)}, f32[256,1024]{1,0:T(8,128)S(1)}, u32[]{:S(2)}, u32[]{:S(2)}) collective-permute-start(f32[256,1024]{1,0:T(8,128)S(1)} %collective-permute-done.12.refs_5_), channel_id=1, source_target_pairs={{0,12},{1,13},{2,14},{3,15},{4,0},{5,1},{6,2},{7,3},{8,4},{9,5},{1... | collective-permute-start | bytes 3145736 | tf_op jit(solution)/shard_map/ppermute | solution.py:22
  44.9 6.9 %collective-permute-done.16.refs_2_ = f32[4,64,768]{2,1,0:T(8,128)S(1)} collective-permute-done((f32[4,64,768]{2,1,0:T(8,128)S(1)}, f32[4,64,768]{2,1,0:T(8,128)S(1)}, u32[]{:S(2)}, u32[]{:S(2)}) %collective-permute-start.16) | collective-permute-done | bytes 786464 | tf_op jit(solution)/shard_map/ppermute | solution.py:22
  51.7 2.1 %collective-permute-done.10.refs_2_ = f32[256,1024]{1,0:T(8,128)S(1)} collective-permute-done((f32[256,1024]{1,0:T(8,128)S(1)}, f32[256,1024]{1,0:T(8,128)S(1)}, u32[]{:S(2)}, u32[]{:S(2)}) %collective-permute-start.10) | collective-permute-done | bytes 1048608 | tf_op jit(solution)/shard_map/ppermute | solution.py:22
  53.9 3.7 %collective-permute-done.11.refs_4_ = f32[256,1024]{1,0:T(8,128)S(1)} collective-permute-done((f32[256,1024]{1,0:T(8,128)S(1)}, f32[256,1024]{1,0:T(8,128)S(1)}, u32[]{:S(2)}, u32[]{:S(2)}) %collective-permute-start.11) | collective-permute-done | bytes 1048608 | tf_op jit(solution)/shard_map/ppermute | solution.py:22
  57.6 1.7 %split_a.1 = (bf16[2,1024,768]{2,1,0:T(8,128)(2,1)S(1)}, bf16[2,1024,768]{2,1,0:T(8,128)(2,1)S(1)}) custom-call(f32[256,1024]{1,0:T(8,128)S(1)} %get-tuple-element.71.refs_0_, f32[256,1024]{1,0:T(8,128)S(1)} %collective-permute-done.9.refs_1_, f32[256,1024]{1,0:T(8,128)S(1)} %collective-permute-done.10.refs_2_, f32[256,1024]{1,0:T(8,128)S(1)} %get-tuple-element.72.refs_3_, ...), custom_call_target="tpu_custom_call" | custom-call | tf_op jit(solution)/shard_map/split_a/pallas_call | solution.py:225
  59.3 5.7 %collective-permute-done.17.refs_3_ = f32[4,64,768]{2,1,0:T(8,128)S(1)} collective-permute-done((f32[4,64,768]{2,1,0:T(8,128)S(1)}, f32[4,64,768]{2,1,0:T(8,128)S(1)}, u32[]{:S(2)}, u32[]{:S(2)}) %collective-permute-start.17) | collective-permute-done | bytes 786464 | tf_op jit(solution)/shard_map/ppermute | solution.py:22
  64.9 0.4 split_b.2
  65.4 2.6 %near_product.1 = (f32[1024,256]{1,0:T(8,128)S(1)}, f32[1024,256]{1,0:T(8,128)S(1)}) custom-call(bf16[2,1024,768]{2,1,0:T(8,128)(2,1)S(1)} %get-tuple-element.73.high, bf16[2,1024,768]{2,1,0:T(8,128)(2,1)S(1)} %get-tuple-element.74.low, bf16[1024,768]{1,0:T(8,128)(2,1)S(1)} %get-tuple-element.78.bh, bf16[1024,768]{1,0:T(8,128)(2,1)S(1)} %get-tuple-element.79.bl), custom_call_target="tpu_custom_call" | custom-call | flops 2415919104 | bytes 2097152 | tf_op jit(solution)/shard_map/near_product/pallas_call | solution.py:312
  68.0 0.8 collective-permute-done.13.top
  68.8 1.2 %first_product.1 = (bf16[2,1024,256]{2,1,0:T(8,128)(2,1)S(1)}, bf16[2,1024,256]{2,1,0:T(8,128)(2,1)S(1)}, f32[1024,256]{1,0:T(8,128)S(1)}, f32[1024,256]{1,0:T(8,128)S(1)}) custom-call(f32[256,1024]{1,0:T(8,128)S(1)} %collective-permute-done.13.top, f32[256,1024]{1,0:T(8,128)S(1)} %collective-permute-done.14.bottom, ...), custom_call_target="tpu_custom_call" | custom-call | flops 805306368 | bytes 2097152 | tf_op jit(solution)/shard_map/first_product/pallas_call | solution.py:328
  70.0 0.9 collective-permute-start.25
  70.9 2.4 %collective-permute-start.19 = (f32[1024,256]{1,0:T(8,128)S(1)}, f32[1024,256]{1,0:T(8,128)S(1)}, u32[]{:S(2)}, u32[]{:S(2)}) collective-permute-start(f32[1024,256]{1,0:T(8,128)S(1)} %get-tuple-element.85), channel_id=1, source_target_pairs={{0,1},{1,2},{2,3},{3,0},{4,5},{5,6},{6,7},{7,4},{8,9},{9,10},{10,1... | collective-permute-start | bytes 3145736 | tf_op jit(solution)/shard_map/ppermute | solution.py:22
  73.4 0.0 collective-permute-start.18
  73.4 3.4 %product.4 = (f32[1024,256]{1,0:T(8,128)S(1)}, f32[1024,256]{1,0:T(8,128)S(1)}) custom-call(bf16[2,1024,768]{2,1,0:T(8,128)(2,1)S(1)} %get-tuple-element.73.high, bf16[2,1024,768]{2,1,0:T(8,128)(2,1)S(1)} %get-tuple-element.74.low, bf16[2,1024,256]{2,1,0:T(8,128)(2,1)S(1)} %get-tuple-element.82.far_high, ...), custom_call_target="tpu_custom_call" | custom-call | flops 3221225472 | bytes 2097152 | tf_op jit(solution)/shard_map/product/pallas_call | solution.py:345
  76.8 3.4 %product.5 = (f32[1024,256]{1,0:T(8,128)S(1)}, f32[1024,256]{1,0:T(8,128)S(1)}) custom-call(bf16[2,1024,768]{2,1,0:T(8,128)(2,1)S(1)} %get-tuple-element.73.high, bf16[2,1024,768]{2,1,0:T(8,128)(2,1)S(1)} %get-tuple-element.74.low, bf16[2,1024,256]{2,1,0:T(8,128)(2,1)S(1)} %get-tuple-element.82.far_high, ...), custom_call_target="tpu_custom_call" | custom-call | flops 3221225472 | bytes 2097152 | tf_op jit(solution)/shard_map/product/pallas_call | solution.py:345
  80.2 0.1 collective-permute-start.24
  80.2 5.9 %collective-permute-done.25 = f32[1024,256]{1,0:T(8,128)S(1)} collective-permute-done((f32[1024,256]{1,0:T(8,128)S(1)}, f32[1024,256]{1,0:T(8,128)S(1)}, u32[]{:S(2)}, u32[]{:S(2)}) %collective-permute-start.25) | collective-permute-done | bytes 1048608 | tf_op jit(solution)/shard_map/ppermute | solution.py:22
  86.1 0.1 add.14
  86.3 0.1 collective-permute-start.26
  86.4 0.1 collective-permute-start.20
  86.4 7.6 %collective-permute-done.20.refs_2_ = f32[4,64,256]{2,1,0:T(8,128)S(1)} collective-permute-done((f32[4,64,256]{2,1,0:T(8,128)S(1)}, f32[4,64,256]{2,1,0:T(8,128)S(1)}, u32[]{:S(2)}, u32[]{:S(2)}) %collective-permute-start.20) | collective-permute-done | bytes 262176 | tf_op jit(solution)/shard_map/ppermute | solution.py:22
  94.0 0.1 collective-permute-start.22
  94.1 0.1 add.12
  94.2 3.2 %collective-permute-start.23 = (f32[1024,256]{1,0:T(8,128)S(1)}, f32[1024,256]{1,0:T(8,128)S(1)}, u32[]{:S(2)}, u32[]{:S(2)}) collective-permute-start(f32[1024,256]{1,0:T(8,128)S(1)} %add.12), channel_id=1, source_target_pairs={{0,1},{1,2},{2,3},{3,0},{4,5},{5,6},{6,7},{7,4},{8,9},{9,10},{10,1... | collective-permute-start | bytes 3145736 | tf_op jit(solution)/shard_map/ppermute | solution.py:22
  97.5 4.1 %collective-permute-done.21.refs_3_ = f32[4,64,256]{2,1,0:T(8,128)S(1)} collective-permute-done((f32[4,64,256]{2,1,0:T(8,128)S(1)}, f32[4,64,256]{2,1,0:T(8,128)S(1)}, u32[]{:S(2)}, u32[]{:S(2)}) %collective-permute-start.21) | collective-permute-done | bytes 262176 | tf_op jit(solution)/shard_map/ppermute | solution.py:22
  101.6 0.1 split_b.3
  101.7 3.4 %product.3 = (f32[1024,256]{1,0:T(8,128)S(1)}, f32[1024,256]{1,0:T(8,128)S(1)}) custom-call(bf16[2,1024,768]{2,1,0:T(8,128)(2,1)S(1)} %get-tuple-element.73.high, bf16[2,1024,768]{2,1,0:T(8,128)(2,1)S(1)} %get-tuple-element.74.low, bf16[2,1024,256]{2,1,0:T(8,128)(2,1)S(1)} %get-tuple-element.82.far_high, ...), custom_call_target="tpu_custom_call" | custom-call | flops 3221225472 | bytes 2097152 | tf_op jit(solution)/shard_map/product/pallas_call | solution.py:345
  105.1 0.2 add_add_fusion
  105.4 0.1 collective-permute-start.27
  105.5 8.1 %collective-permute-done.22.top3 = f32[1024,256]{1,0:T(8,128)S(1)} collective-permute-done((f32[1024,256]{1,0:T(8,128)S(1)}, f32[1024,256]{1,0:T(8,128)S(1)}, u32[]{:S(2)}, u32[]{:S(2)}) %collective-permute-start.22) | collective-permute-done | bytes 1048608 | tf_op jit(solution)/shard_map/ppermute | solution.py:22
  113.6 2.0 %finish.1 = f32[1024,512]{1,0:T(8,128)} custom-call(s32[4]{0:T(128)S(1)} %pad_add_fusion.place, f32[1024,256]{1,0:T(8,128)S(1)} %get-tuple-element.90.top0, f32[1024,256]{1,0:T(8,128)S(1)} %collective-permute-done.22.top3, f32[1024,256]{1,0:T(8,128)S(1)} %collective-permute-done.23.top1, f32[1024,256]{1,0:T(8,128)S(1)} %collective-permute-done.27.got), custom_call_target="tpu_custom_call" | custom-call | tf_op jit(solution)/shard_map/finish/pallas_call | solution.py:376
  (15 shorter events, 0.1 us)
Async XLA Ops:
  0.1 1.2 %copy-start = (f32[32,8192]{1,0:T(8,128)S(1)}, f32[32,8192]{1,0:T(8,128)}, u32[]{:S(2)}) copy-start(f32[32,8192]{1,0:T(8,128)} %a_ref.1) | copy-start | bytes 3145732
  1.9 2.6 %collective-permute-start = (f32[2,2,32,1024]{3,2,1,0:T(8,128)S(1)}, f32[2,2,32,1024]{3,2,1,0:T(8,128)S(1)}, u32[]{:S(2)}, u32[]{:S(2)}) collective-permute-start(f32[2,2,32,1024]{3,2,1,0:T(8,128)S(1)} %get-tuple-element.52), channel_id=1, source_target_pairs={{0,16},{1,17},{2,18},{3,19},{4,20},{5,21},{6,22},{7,23},{8,24},{9,... | collective-permute-start | bytes 1572872 | tf_op jit(solution)/shard_map/ppermute | solution.py:22
  2.0 1.2 %copy-start.1 = (f32[32,8192]{1,0:T(8,128)S(1)}, f32[32,8192]{1,0:T(8,128)}, u32[]{:S(2)}) copy-start(f32[32,8192]{1,0:T(8,128)} %b_ref.1) | copy-start | bytes 3145732
  4.0 6.2 %collective-permute-start.3 = (f32[4,32,1024]{2,1,0:T(8,128)S(1)}, f32[4,32,1024]{2,1,0:T(8,128)S(1)}, u32[]{:S(2)}, u32[]{:S(2)}) collective-permute-start(f32[4,32,1024]{2,1,0:T(8,128)S(1)} %get-tuple-element.56), channel_id=1, source_target_pairs={{0,16},{1,17},{2,18},{3,19},{4,20},{5,21},{6,22},{7,23},{8,24},{9,... | collective-permute-start | bytes 1572872 | tf_op jit(solution)/shard_map/ppermute | solution.py:22
  4.6 18.4 %collective-permute-start.2 = (f32[2,64,1024]{2,1,0:T(8,128)S(1)}, f32[2,64,1024]{2,1,0:T(8,128)S(1)}, u32[]{:S(2)}, u32[]{:S(2)}) collective-permute-start(f32[2,64,1024]{2,1,0:T(8,128)S(1)} %join_a.1), channel_id=1, source_target_pairs={{0,32},{1,33},{2,34},{3,35},{4,36},{5,37},{6,38},{7,39},{8,40},{9,... | collective-permute-start | bytes 1572872 | tf_op jit(solution)/shard_map/ppermute | solution.py:22
  6.6 16.4 %collective-permute-start.1 = (f32[2,32,1024]{2,1,0:T(8,128)S(1)}, f32[2,32,1024]{2,1,0:T(8,128)S(1)}, u32[]{:S(2)}, u32[]{:S(2)}) collective-permute-start(f32[2,32,1024]{2,1,0:T(8,128)S(1)} %get-tuple-element.53), channel_id=1, source_target_pairs={{0,64},{1,65},{2,66},{3,67},{4,68},{5,69},{6,70},{7,71},{8,72},{9,... | collective-permute-start | bytes 786440 | tf_op jit(solution)/shard_map/ppermute | solution.py:22
  10.3 12.7 %collective-permute-start.4 = (f32[64,1024]{1,0:T(8,128)S(1)}, f32[64,1024]{1,0:T(8,128)S(1)}, u32[]{:S(2)}, u32[]{:S(2)}) collective-permute-start(f32[64,1024]{1,0:T(8,128)S(1)} %get-tuple-element.58), channel_id=1, source_target_pairs={{0,4},{1,5},{2,6},{3,7},{4,8},{5,9},{6,10},{7,11},{8,12},{9,13},{1... | collective-permute-start | bytes 786440 | tf_op jit(solution)/shard_map/ppermute | solution.py:22
  11.9 11.1 %collective-permute-start.5 = (f32[64,1024]{1,0:T(8,128)S(1)}, f32[64,1024]{1,0:T(8,128)S(1)}, u32[]{:S(2)}, u32[]{:S(2)}) collective-permute-start(f32[64,1024]{1,0:T(8,128)S(1)} %get-tuple-element.59), channel_id=1, source_target_pairs={{0,8},{1,9},{2,10},{3,11},{4,12},{5,13},{6,14},{7,15},{8,0},{9,1},... | collective-permute-start | bytes 786440 | tf_op jit(solution)/shard_map/ppermute | solution.py:22
  14.8 8.2 %collective-permute-start.6 = (f32[64,1024]{1,0:T(8,128)S(1)}, f32[64,1024]{1,0:T(8,128)S(1)}, u32[]{:S(2)}, u32[]{:S(2)}) collective-permute-start(f32[64,1024]{1,0:T(8,128)S(1)} %get-tuple-element.60), channel_id=1, source_target_pairs={{0,12},{1,13},{2,14},{3,15},{4,0},{5,1},{6,2},{7,3},{8,4},{9,5},{1... | collective-permute-start | bytes 786440 | tf_op jit(solution)/shard_map/ppermute | solution.py:22
  23.0 2.4 %collective-permute-start.8 = (f32[2,64,1024]{2,1,0:T(8,128)S(1)}, f32[2,64,1024]{2,1,0:T(8,128)S(1)}, u32[]{:S(2)}, u32[]{:S(2)}) collective-permute-start(f32[2,64,1024]{2,1,0:T(8,128)S(1)} %collective-permute-done.2.side), channel_id=1, source_target_pairs={{0,16},{1,17},{2,18},{3,19},{4,20},{5,21},{6,22},{7,23},{8,24},{9,... | collective-permute-start | bytes 1572872 | tf_op jit(solution)/shard_map/ppermute | solution.py:22
  23.1 2.3 %collective-permute-start.7 = (f32[2,32,1024]{2,1,0:T(8,128)S(1)}, f32[2,32,1024]{2,1,0:T(8,128)S(1)}, u32[]{:S(2)}, u32[]{:S(2)}) collective-permute-start(f32[2,32,1024]{2,1,0:T(8,128)S(1)} %collective-permute-done.1.two), channel_id=1, source_target_pairs={{0,16},{1,17},{2,18},{3,19},{4,20},{5,21},{6,22},{7,23},{8,24},{9,... | collective-permute-start | bytes 786440 | tf_op jit(solution)/shard_map/ppermute | solution.py:22
  25.3 13.2 %collective-permute-start.15 = (f32[4,64,768]{2,1,0:T(8,128)S(1)}, f32[4,64,768]{2,1,0:T(8,128)S(1)}, u32[]{:S(2)}, u32[]{:S(2)}) collective-permute-start(f32[4,64,768]{2,1,0:T(8,128)S(1)} %get-tuple-element.75.refs_0_), channel_id=1, source_target_pairs={{0,32},{1,33},{2,34},{3,35},{4,36},{5,37},{6,38},{7,39},{8,40},{9,... | collective-permute-start | bytes 2359304 | tf_op jit(solution)/shard_map/ppermute | solution.py:22
  25.5 16.1 %collective-permute-start.9 = (f32[256,1024]{1,0:T(8,128)S(1)}, f32[256,1024]{1,0:T(8,128)S(1)}, u32[]{:S(2)}, u32[]{:S(2)}) collective-permute-start(f32[256,1024]{1,0:T(8,128)S(1)} %get-tuple-element.71.refs_0_), channel_id=1, source_target_pairs={{0,4},{1,5},{2,6},{3,7},{4,8},{5,9},{6,10},{7,11},{8,12},{9,13},{1... | collective-permute-start | bytes 3145736 | tf_op jit(solution)/shard_map/ppermute | solution.py:22
  27.1 15.0 %collective-permute-start.12 = (f32[256,1024]{1,0:T(8,128)S(1)}, f32[256,1024]{1,0:T(8,128)S(1)}, u32[]{:S(2)}, u32[]{:S(2)}) collective-permute-start(f32[256,1024]{1,0:T(8,128)S(1)} %get-tuple-element.72.refs_3_), channel_id=1, source_target_pairs={{0,12},{1,13},{2,14},{3,15},{4,0},{5,1},{6,2},{7,3},{8,4},{9,5},{1... | collective-permute-start | bytes 3145736 | tf_op jit(solution)/shard_map/ppermute | solution.py:22
  38.5 13.2 %collective-permute-start.16 = (f32[4,64,768]{2,1,0:T(8,128)S(1)}, f32[4,64,768]{2,1,0:T(8,128)S(1)}, u32[]{:S(2)}, u32[]{:S(2)}) collective-permute-start(f32[4,64,768]{2,1,0:T(8,128)S(1)} %collective-permute-done.15.refs_1_), channel_id=1, source_target_pairs={{0,32},{1,33},{2,34},{3,35},{4,36},{5,37},{6,38},{7,39},{8,40},{9,... | collective-permute-start | bytes 2359304 | tf_op jit(solution)/shard_map/ppermute | solution.py:22
  38.5 15.3 %collective-permute-start.10 = (f32[256,1024]{1,0:T(8,128)S(1)}, f32[256,1024]{1,0:T(8,128)S(1)}, u32[]{:S(2)}, u32[]{:S(2)}) collective-permute-start(f32[256,1024]{1,0:T(8,128)S(1)} %get-tuple-element.71.refs_0_), channel_id=1, source_target_pairs={{0,12},{1,13},{2,14},{3,15},{4,0},{5,1},{6,2},{7,3},{8,4},{9,5},{1... | collective-permute-start | bytes 3145736 | tf_op jit(solution)/shard_map/ppermute | solution.py:22
  41.6 16.0 %collective-permute-start.11 = (f32[256,1024]{1,0:T(8,128)S(1)}, f32[256,1024]{1,0:T(8,128)S(1)}, u32[]{:S(2)}, u32[]{:S(2)}) collective-permute-start(f32[256,1024]{1,0:T(8,128)S(1)} %get-tuple-element.72.refs_3_), channel_id=1, source_target_pairs={{0,4},{1,5},{2,6},{3,7},{4,8},{5,9},{6,10},{7,11},{8,12},{9,13},{1... | collective-permute-start | bytes 3145736 | tf_op jit(solution)/shard_map/ppermute | solution.py:22
  41.6 27.2 %collective-permute-start.13 = (f32[256,1024]{1,0:T(8,128)S(1)}, f32[256,1024]{1,0:T(8,128)S(1)}, u32[]{:S(2)}, u32[]{:S(2)}) collective-permute-start(f32[256,1024]{1,0:T(8,128)S(1)} %collective-permute-done.9.refs_1_), channel_id=1, source_target_pairs={{0,4},{1,5},{2,6},{3,7},{4,8},{5,9},{6,10},{7,11},{8,12},{9,13},{1... | collective-permute-start | bytes 3145736 | tf_op jit(solution)/shard_map/ppermute | solution.py:22
  42.2 26.7 %collective-permute-start.14 = (f32[256,1024]{1,0:T(8,128)S(1)}, f32[256,1024]{1,0:T(8,128)S(1)}, u32[]{:S(2)}, u32[]{:S(2)}) collective-permute-start(f32[256,1024]{1,0:T(8,128)S(1)} %collective-permute-done.12.refs_5_), channel_id=1, source_target_pairs={{0,12},{1,13},{2,14},{3,15},{4,0},{5,1},{6,2},{7,3},{8,4},{9,5},{1... | collective-permute-start | bytes 3145736 | tf_op jit(solution)/shard_map/ppermute | solution.py:22
  51.7 13.2 %collective-permute-start.17 = (f32[4,64,768]{2,1,0:T(8,128)S(1)}, f32[4,64,768]{2,1,0:T(8,128)S(1)}, u32[]{:S(2)}, u32[]{:S(2)}) collective-permute-start(f32[4,64,768]{2,1,0:T(8,128)S(1)} %collective-permute-done.16.refs_2_), channel_id=1, source_target_pairs={{0,32},{1,33},{2,34},{3,35},{4,36},{5,37},{6,38},{7,39},{8,40},{9,... | collective-permute-start | bytes 2359304 | tf_op jit(solution)/shard_map/ppermute | solution.py:22
  70.0 16.1 %collective-permute-start.25 = (f32[1024,256]{1,0:T(8,128)S(1)}, f32[1024,256]{1,0:T(8,128)S(1)}, u32[]{:S(2)}, u32[]{:S(2)}) collective-permute-start(f32[1024,256]{1,0:T(8,128)S(1)} %get-tuple-element.96), channel_id=1, source_target_pairs={{0,3},{1,0},{2,1},{3,2},{4,7},{5,4},{6,5},{7,6},{8,11},{9,8},{10,9... | collective-permute-start | bytes 3145736 | tf_op jit(solution)/shard_map/ppermute | solution.py:22
  70.9 23.1 %collective-permute-start.19 = (f32[1024,256]{1,0:T(8,128)S(1)}, f32[1024,256]{1,0:T(8,128)S(1)}, u32[]{:S(2)}, u32[]{:S(2)}) collective-permute-start(f32[1024,256]{1,0:T(8,128)S(1)} %get-tuple-element.85), channel_id=1, source_target_pairs={{0,1},{1,2},{2,3},{3,0},{4,5},{5,6},{6,7},{7,4},{8,9},{9,10},{10,1... | collective-permute-start | bytes 3145736 | tf_op jit(solution)/shard_map/ppermute | solution.py:22
  73.4 13.0 %collective-permute-start.18 = (f32[4,64,256]{2,1,0:T(8,128)S(1)}, f32[4,64,256]{2,1,0:T(8,128)S(1)}, u32[]{:S(2)}, u32[]{:S(2)}) collective-permute-start(f32[4,64,256]{2,1,0:T(8,128)S(1)} %get-tuple-element.84.refs_0_), channel_id=1, source_target_pairs={{0,32},{1,33},{2,34},{3,35},{4,36},{5,37},{6,38},{7,39},{8,40},{9,... | collective-permute-start | bytes 786440 | tf_op jit(solution)/shard_map/ppermute | solution.py:22
  80.2 25.0 %collective-permute-start.24 = (f32[1024,256]{1,0:T(8,128)S(1)}, f32[1024,256]{1,0:T(8,128)S(1)}, u32[]{:S(2)}, u32[]{:S(2)}) collective-permute-start(f32[1024,256]{1,0:T(8,128)S(1)} %get-tuple-element.94), channel_id=1, source_target_pairs={{0,1},{1,2},{2,3},{3,0},{4,5},{5,6},{6,7},{7,4},{8,9},{9,10},{10,1... | collective-permute-start | bytes 3145736 | tf_op jit(solution)/shard_map/ppermute | solution.py:22
  86.3 18.9 %collective-permute-start.26 = (f32[1024,256]{1,0:T(8,128)S(1)}, f32[1024,256]{1,0:T(8,128)S(1)}, u32[]{:S(2)}, u32[]{:S(2)}) collective-permute-start(f32[1024,256]{1,0:T(8,128)S(1)} %add.14), channel_id=1, source_target_pairs={{0,3},{1,0},{2,1},{3,2},{4,7},{5,4},{6,5},{7,6},{8,11},{9,8},{10,9... | collective-permute-start | bytes 3145736 | tf_op jit(solution)/shard_map/ppermute | solution.py:22
  86.4 7.7 %collective-permute-start.20 = (f32[4,64,256]{2,1,0:T(8,128)S(1)}, f32[4,64,256]{2,1,0:T(8,128)S(1)}, u32[]{:S(2)}, u32[]{:S(2)}) collective-permute-start(f32[4,64,256]{2,1,0:T(8,128)S(1)} %collective-permute-done.18.refs_1_), channel_id=1, source_target_pairs={{0,32},{1,33},{2,34},{3,35},{4,36},{5,37},{6,38},{7,39},{8,40},{9,... | collective-permute-start | bytes 786440 | tf_op jit(solution)/shard_map/ppermute | solution.py:22
  94.0 7.6 %collective-permute-start.21 = (f32[4,64,256]{2,1,0:T(8,128)S(1)}, f32[4,64,256]{2,1,0:T(8,128)S(1)}, u32[]{:S(2)}, u32[]{:S(2)}) collective-permute-start(f32[4,64,256]{2,1,0:T(8,128)S(1)} %collective-permute-done.20.refs_2_), channel_id=1, source_target_pairs={{0,32},{1,33},{2,34},{3,35},{4,36},{5,37},{6,38},{7,39},{8,40},{9,... | collective-permute-start | bytes 786440 | tf_op jit(solution)/shard_map/ppermute | solution.py:22
  94.0 19.6 %collective-permute-start.22 = (f32[1024,256]{1,0:T(8,128)S(1)}, f32[1024,256]{1,0:T(8,128)S(1)}, u32[]{:S(2)}, u32[]{:S(2)}) collective-permute-start(f32[1024,256]{1,0:T(8,128)S(1)} %get-tuple-element.91), channel_id=1, source_target_pairs={{0,3},{1,0},{2,1},{3,2},{4,7},{5,4},{6,5},{7,6},{8,11},{9,8},{10,9... | collective-permute-start | bytes 3145736 | tf_op jit(solution)/shard_map/ppermute | solution.py:22
  94.2 19.4 %collective-permute-start.23 = (f32[1024,256]{1,0:T(8,128)S(1)}, f32[1024,256]{1,0:T(8,128)S(1)}, u32[]{:S(2)}, u32[]{:S(2)}) collective-permute-start(f32[1024,256]{1,0:T(8,128)S(1)} %add.12), channel_id=1, source_target_pairs={{0,1},{1,2},{2,3},{3,0},{4,5},{5,6},{6,7},{7,4},{8,9},{9,10},{10,1... | collective-permute-start | bytes 3145736 | tf_op jit(solution)/shard_map/ppermute | solution.py:22
  105.4 8.2 %collective-permute-start.27 = (f32[1024,256]{1,0:T(8,128)S(1)}, f32[1024,256]{1,0:T(8,128)S(1)}, u32[]{:S(2)}, u32[]{:S(2)}) collective-permute-start(f32[1024,256]{1,0:T(8,128)S(1)} %add_add_fusion), channel_id=1, source_target_pairs={{0,16},{1,17},{2,18},{3,19},{4,20},{5,21},{6,22},{7,23},{8,24},{9,... | collective-permute-start | bytes 3145736 | tf_op jit(solution)/shard_map/ppermute | solution.py:22

commit v5 on v4

--- a/solution.py
+++ b/solution.py
@@ -89,7 +89,7 @@
 
 
 AHEAD = 3
-ORDER = (2, 1, 3, 0)
+ORDER = (2, 3, 1, 0)
 
 
 def prepare_b_kernel(place, b_ref, keep_ref, pass_ref):
@@ -357,13 +357,14 @@
     rows, width = top0.shape
     tile = rows // 4
     copies = []
-    for i in range(4):
-        tile_rows = slice(i * tile, (i + 1) * tile)
-        mine[tile_rows] = top0[tile_rows] + top3[tile_rows] + top1[tile_rows]
-        for k, ref, core in ((0, mine, place[1]), (1, got, 1 - place[1])):
-            start = pl.multiple_of(core * width, width)
+    for k, ref, core in ((1, got, 1 - place[1]), (0, mine, place[1])):
+        columns = pl.ds(pl.multiple_of(core * width, width), width)
+        for i in range(4):
+            tile_rows = slice(i * tile, (i + 1) * tile)
+            if k == 0:
+                mine[tile_rows] = top0[tile_rows] + top3[tile_rows] + top1[tile_rows]
             copy = pltpu.make_async_copy(
-                ref.at[tile_rows], out_ref.at[tile_rows, pl.ds(start, width)], sems.at[k, i]
+                ref.at[tile_rows], out_ref.at[tile_rows, columns], sems.at[k, i]
             )
             copy.start()
             copies.append(copy)
@@ -424,8 +425,8 @@
     _, later[1] = lax.optimization_barrier((top2, later[1]))
     later.append(along_z(later[-1], 1))
     halves = (high, low, far_high, far_low)
+    top3, bottom3 = product(3, *halves, bh, bl)
     top1, bottom1 = product(1, *halves, bh, bl)
-    top3, bottom3 = product(3, *halves, bh, bl)
 
     top2 = along_reduce(top2, 1)
     bottom2 = along_reduce(bottom2, -1)

time: 116 us -> 116 us (level)
  no operation moved by 1% of the time
where the time goes in v5:
time: 116 us
  waiting for transfers between devices  63.2 us (54%)
  starting transfers between devices  29.3 us (25%)
  Pallas kernels  19.8 us (17%)
  local copies, waits for them, and re-layouts  2.45 us (2%)
    ppermute x28, waiting for transfers between devices, permute(): return lax.ppermute(value, ALL, pairs)  63.2 us
    ppermute x28, starting transfers between devices, permute(): return lax.ppermute(value, ALL, pairs)  29.3 us
    pallas_call x3, Pallas kernels, product(): pl.pallas_call(functools.partial(product_kernel, tasks), out_shape=(out,...  10.2 us
    pallas_call x1, Pallas kernels, near_product(): pl.pallas_call(near_kernel, out_shape=(out, out), in_specs=[VMEM] * 4, ou...  2.59 us
    unnamed x4, local copies, waits for them, and re-layouts  2.45 us
  transfers between devices with their start and end apart: 28, of which 12 were waited for; matrix products, arithmetic and copies ran while one was open for 0% of the time, Pallas kernels for 14%

profile of v5, /device:TPU:6, one launch (start us, length us, event | category | flops | bytes accessed | tf_op | source)
XLA Modules:
  0.0 115.7 jit_solution(5953014158109226741)
XLA Ops:
  0.0 0.1 pad_add_fusion.place
  0.1 1.2 %copy-done = f32[32,8192]{1,0:T(8,128)S(1)} copy-done((f32[32,8192]{1,0:T(8,128)S(1)}, f32[32,8192]{1,0:T(8,128)}, u32[]{:S(2)}) %copy-start) | copy-done | bytes 1048600
  1.3 0.6 prepare_a.1
  1.9 0.1 collective-permute-start
  2.0 0.0 copy-start.1
  2.1 1.2 %copy-done.1 = f32[32,8192]{1,0:T(8,128)S(1)} copy-done((f32[32,8192]{1,0:T(8,128)S(1)}, f32[32,8192]{1,0:T(8,128)}, u32[]{:S(2)}) %copy-start.1) | copy-done | bytes 1048600
  3.3 0.7 prepare_b.1
  4.0 0.6 collective-permute-start.3
  4.6 0.0 collective-permute-done.got
  4.6 2.0 %collective-permute-start.2 = (f32[2,64,1024]{2,1,0:T(8,128)S(1)}, f32[2,64,1024]{2,1,0:T(8,128)S(1)}, u32[]{:S(2)}, u32[]{:S(2)}) collective-permute-start(f32[2,64,1024]{2,1,0:T(8,128)S(1)} %join_a.1), channel_id=1, source_target_pairs={{0,32},{1,33},{2,34},{3,35},{4,36},{5,37},{6,38},{7,39},{8,40},{9,... | collective-permute-start | bytes 1572872 | tf_op jit(solution)/shard_map/ppermute | solution.py:22
  6.6 3.6 %collective-permute-start.1 = (f32[2,32,1024]{2,1,0:T(8,128)S(1)}, f32[2,32,1024]{2,1,0:T(8,128)S(1)}, u32[]{:S(2)}, u32[]{:S(2)}) collective-permute-start(f32[2,32,1024]{2,1,0:T(8,128)S(1)} %get-tuple-element.53), channel_id=1, source_target_pairs={{0,64},{1,65},{2,66},{3,67},{4,68},{5,69},{6,70},{7,71},{8,72},{9,... | collective-permute-start | bytes 786440 | tf_op jit(solution)/shard_map/ppermute | solution.py:22
  10.2 0.0 collective-permute-done.3.got
  10.2 0.1 join_b.1
  10.3 1.6 %collective-permute-start.4 = (f32[64,1024]{1,0:T(8,128)S(1)}, f32[64,1024]{1,0:T(8,128)S(1)}, u32[]{:S(2)}, u32[]{:S(2)}) collective-permute-start(f32[64,1024]{1,0:T(8,128)S(1)} %get-tuple-element.58), channel_id=1, source_target_pairs={{0,4},{1,5},{2,6},{3,7},{4,8},{5,9},{6,10},{7,11},{8,12},{9,13},{1... | collective-permute-start | bytes 786440 | tf_op jit(solution)/shard_map/ppermute | solution.py:22
  11.9 2.9 %collective-permute-start.5 = (f32[64,1024]{1,0:T(8,128)S(1)}, f32[64,1024]{1,0:T(8,128)S(1)}, u32[]{:S(2)}, u32[]{:S(2)}) collective-permute-start(f32[64,1024]{1,0:T(8,128)S(1)} %get-tuple-element.59), channel_id=1, source_target_pairs={{0,8},{1,9},{2,10},{3,11},{4,12},{5,13},{6,14},{7,15},{8,0},{9,1},... | collective-permute-start | bytes 786440 | tf_op jit(solution)/shard_map/ppermute | solution.py:22
  14.8 1.3 %collective-permute-start.6 = (f32[64,1024]{1,0:T(8,128)S(1)}, f32[64,1024]{1,0:T(8,128)S(1)}, u32[]{:S(2)}, u32[]{:S(2)}) collective-permute-start(f32[64,1024]{1,0:T(8,128)S(1)} %get-tuple-element.60), channel_id=1, source_target_pairs={{0,12},{1,13},{2,14},{3,15},{4,0},{5,1},{6,2},{7,3},{8,4},{9,5},{1... | collective-permute-start | bytes 786440 | tf_op jit(solution)/shard_map/ppermute | solution.py:22
  16.1 6.8 %collective-permute-done.1.two = f32[2,32,1024]{2,1,0:T(8,128)S(1)} collective-permute-done((f32[2,32,1024]{2,1,0:T(8,128)S(1)}, f32[2,32,1024]{2,1,0:T(8,128)S(1)}, u32[]{:S(2)}, u32[]{:S(2)}) %collective-permute-start.1) | collective-permute-done | bytes 262176 | tf_op jit(solution)/shard_map/ppermute | solution.py:22
  23.0 0.0 collective-permute-done.2.side
  23.0 0.1 collective-permute-start.8
  23.1 0.5 collective-permute-start.7
  23.6 0.1 panel.1
  23.6 1.7 %collective-permute-done.7.two_got = f32[2,32,1024]{2,1,0:T(8,128)S(1)} collective-permute-done((f32[2,32,1024]{2,1,0:T(8,128)S(1)}, f32[2,32,1024]{2,1,0:T(8,128)S(1)}, u32[]{:S(2)}, u32[]{:S(2)}) %collective-permute-start.7) | collective-permute-done | bytes 262176 | tf_op jit(solution)/shard_map/ppermute | solution.py:22
  25.3 0.0 collective-permute-done.8.side_got
  25.3 0.0 collective-permute-start.15
  25.3 0.1 stack.21
  25.5 1.6 %collective-permute-start.9 = (f32[256,1024]{1,0:T(8,128)S(1)}, f32[256,1024]{1,0:T(8,128)S(1)}, u32[]{:S(2)}, u32[]{:S(2)}) collective-permute-start(f32[256,1024]{1,0:T(8,128)S(1)} %get-tuple-element.71.refs_0_), channel_id=1, source_target_pairs={{0,4},{1,5},{2,6},{3,7},{4,8},{5,9},{6,10},{7,11},{8,12},{9,13},{1... | collective-permute-start | bytes 3145736 | tf_op jit(solution)/shard_map/ppermute | solution.py:22
  27.1 1.7 %collective-permute-start.12 = (f32[256,1024]{1,0:T(8,128)S(1)}, f32[256,1024]{1,0:T(8,128)S(1)}, u32[]{:S(2)}, u32[]{:S(2)}) collective-permute-start(f32[256,1024]{1,0:T(8,128)S(1)} %get-tuple-element.72.refs_3_), channel_id=1, source_target_pairs={{0,12},{1,13},{2,14},{3,15},{4,0},{5,1},{6,2},{7,3},{8,4},{9,5},{1... | collective-permute-start | bytes 3145736 | tf_op jit(solution)/shard_map/ppermute | solution.py:22
  28.8 9.8 %collective-permute-done.15.refs_1_ = f32[4,64,768]{2,1,0:T(8,128)S(1)} collective-permute-done((f32[4,64,768]{2,1,0:T(8,128)S(1)}, f32[4,64,768]{2,1,0:T(8,128)S(1)}, u32[]{:S(2)}, u32[]{:S(2)}) %collective-permute-start.15) | collective-permute-done | bytes 786464 | tf_op jit(solution)/shard_map/ppermute | solution.py:22
  38.5 0.0 collective-permute-start.16
  38.5 3.0 %collective-permute-start.10 = (f32[256,1024]{1,0:T(8,128)S(1)}, f32[256,1024]{1,0:T(8,128)S(1)}, u32[]{:S(2)}, u32[]{:S(2)}) collective-permute-start(f32[256,1024]{1,0:T(8,128)S(1)} %get-tuple-element.71.refs_0_), channel_id=1, source_target_pairs={{0,12},{1,13},{2,14},{3,15},{4,0},{5,1},{6,2},{7,3},{8,4},{9,5},{1... | collective-permute-start | bytes 3145736 | tf_op jit(solution)/shard_map/ppermute | solution.py:22
  41.6 0.0 collective-permute-start.11
  41.6 0.0 collective-permute-done.9.refs_1_
  41.6 0.6 collective-permute-start.13
  42.2 2.7 %collective-permute-start.14 = (f32[256,1024]{1,0:T(8,128)S(1)}, f32[256,1024]{1,0:T(8,128)S(1)}, u32[]{:S(2)}, u32[]{:S(2)}) collective-permute-start(f32[256,1024]{1,0:T(8,128)S(1)} %collective-permute-done.12.refs_5_), channel_id=1, source_target_pairs={{0,12},{1,13},{2,14},{3,15},{4,0},{5,1},{6,2},{7,3},{8,4},{9,5},{1... | collective-permute-start | bytes 3145736 | tf_op jit(solution)/shard_map/ppermute | solution.py:22
  44.9 6.9 %collective-permute-done.16.refs_2_ = f32[4,64,768]{2,1,0:T(8,128)S(1)} collective-permute-done((f32[4,64,768]{2,1,0:T(8,128)S(1)}, f32[4,64,768]{2,1,0:T(8,128)S(1)}, u32[]{:S(2)}, u32[]{:S(2)}) %collective-permute-start.16) | collective-permute-done | bytes 786464 | tf_op jit(solution)/shard_map/ppermute | solution.py:22
  51.7 2.1 %collective-permute-done.10.refs_2_ = f32[256,1024]{1,0:T(8,128)S(1)} collective-permute-done((f32[256,1024]{1,0:T(8,128)S(1)}, f32[256,1024]{1,0:T(8,128)S(1)}, u32[]{:S(2)}, u32[]{:S(2)}) %collective-permute-start.10) | collective-permute-done | bytes 1048608 | tf_op jit(solution)/shard_map/ppermute | solution.py:22
  53.9 3.7 %collective-permute-done.11.refs_4_ = f32[256,1024]{1,0:T(8,128)S(1)} collective-permute-done((f32[256,1024]{1,0:T(8,128)S(1)}, f32[256,1024]{1,0:T(8,128)S(1)}, u32[]{:S(2)}, u32[]{:S(2)}) %collective-permute-start.11) | collective-permute-done | bytes 1048608 | tf_op jit(solution)/shard_map/ppermute | solution.py:22
  57.6 1.7 %split_a.1 = (bf16[2,1024,768]{2,1,0:T(8,128)(2,1)S(1)}, bf16[2,1024,768]{2,1,0:T(8,128)(2,1)S(1)}) custom-call(f32[256,1024]{1,0:T(8,128)S(1)} %get-tuple-element.71.refs_0_, f32[256,1024]{1,0:T(8,128)S(1)} %collective-permute-done.9.refs_1_, f32[256,1024]{1,0:T(8,128)S(1)} %collective-permute-done.10.refs_2_, f32[256,1024]{1,0:T(8,128)S(1)} %get-tuple-element.72.refs_3_, ...), custom_call_target="tpu_custom_call" | custom-call | tf_op jit(solution)/shard_map/split_a/pallas_call | solution.py:225
  59.3 5.7 %collective-permute-done.17.refs_3_ = f32[4,64,768]{2,1,0:T(8,128)S(1)} collective-permute-done((f32[4,64,768]{2,1,0:T(8,128)S(1)}, f32[4,64,768]{2,1,0:T(8,128)S(1)}, u32[]{:S(2)}, u32[]{:S(2)}) %collective-permute-start.17) | collective-permute-done | bytes 786464 | tf_op jit(solution)/shard_map/ppermute | solution.py:22
  64.9 0.4 split_b.2
  65.4 2.6 %near_product.1 = (f32[1024,256]{1,0:T(8,128)S(1)}, f32[1024,256]{1,0:T(8,128)S(1)}) custom-call(bf16[2,1024,768]{2,1,0:T(8,128)(2,1)S(1)} %get-tuple-element.73.high, bf16[2,1024,768]{2,1,0:T(8,128)(2,1)S(1)} %get-tuple-element.74.low, bf16[1024,768]{1,0:T(8,128)(2,1)S(1)} %get-tuple-element.78.bh, bf16[1024,768]{1,0:T(8,128)(2,1)S(1)} %get-tuple-element.79.bl), custom_call_target="tpu_custom_call" | custom-call | flops 2415919104 | bytes 2097152 | tf_op jit(solution)/shard_map/near_product/pallas_call | solution.py:312
  68.0 0.8 collective-permute-done.13.top
  68.8 1.2 %first_product.1 = (bf16[2,1024,256]{2,1,0:T(8,128)(2,1)S(1)}, bf16[2,1024,256]{2,1,0:T(8,128)(2,1)S(1)}, f32[1024,256]{1,0:T(8,128)S(1)}, f32[1024,256]{1,0:T(8,128)S(1)}) custom-call(f32[256,1024]{1,0:T(8,128)S(1)} %collective-permute-done.13.top, f32[256,1024]{1,0:T(8,128)S(1)} %collective-permute-done.14.bottom, ...), custom_call_target="tpu_custom_call" | custom-call | flops 805306368 | bytes 2097152 | tf_op jit(solution)/shard_map/first_product/pallas_call | solution.py:328
  70.0 0.9 collective-permute-start.25
  70.9 2.4 %collective-permute-start.19 = (f32[1024,256]{1,0:T(8,128)S(1)}, f32[1024,256]{1,0:T(8,128)S(1)}, u32[]{:S(2)}, u32[]{:S(2)}) collective-permute-start(f32[1024,256]{1,0:T(8,128)S(1)} %get-tuple-element.85), channel_id=1, source_target_pairs={{0,1},{1,2},{2,3},{3,0},{4,5},{5,6},{6,7},{7,4},{8,9},{9,10},{10,1... | collective-permute-start | bytes 3145736 | tf_op jit(solution)/shard_map/ppermute | solution.py:22
  73.4 0.0 collective-permute-start.18
  73.4 3.4 %product.4 = (f32[1024,256]{1,0:T(8,128)S(1)}, f32[1024,256]{1,0:T(8,128)S(1)}) custom-call(bf16[2,1024,768]{2,1,0:T(8,128)(2,1)S(1)} %get-tuple-element.73.high, bf16[2,1024,768]{2,1,0:T(8,128)(2,1)S(1)} %get-tuple-element.74.low, bf16[2,1024,256]{2,1,0:T(8,128)(2,1)S(1)} %get-tuple-element.82.far_high, ...), custom_call_target="tpu_custom_call" | custom-call | flops 3221225472 | bytes 2097152 | tf_op jit(solution)/shard_map/product/pallas_call | solution.py:345
  76.8 3.4 %product.5 = (f32[1024,256]{1,0:T(8,128)S(1)}, f32[1024,256]{1,0:T(8,128)S(1)}) custom-call(bf16[2,1024,768]{2,1,0:T(8,128)(2,1)S(1)} %get-tuple-element.73.high, bf16[2,1024,768]{2,1,0:T(8,128)(2,1)S(1)} %get-tuple-element.74.low, bf16[2,1024,256]{2,1,0:T(8,128)(2,1)S(1)} %get-tuple-element.82.far_high, ...), custom_call_target="tpu_custom_call" | custom-call | flops 3221225472 | bytes 2097152 | tf_op jit(solution)/shard_map/product/pallas_call | solution.py:345
  80.2 0.1 collective-permute-start.24
  80.2 5.9 %collective-permute-done.25 = f32[1024,256]{1,0:T(8,128)S(1)} collective-permute-done((f32[1024,256]{1,0:T(8,128)S(1)}, f32[1024,256]{1,0:T(8,128)S(1)}, u32[]{:S(2)}, u32[]{:S(2)}) %collective-permute-start.25) | collective-permute-done | bytes 1048608 | tf_op jit(solution)/shard_map/ppermute | solution.py:22
  86.1 0.1 add.14
  86.3 0.1 collective-permute-start.26
  86.4 0.1 collective-permute-start.20
  86.4 7.6 %collective-permute-done.20.refs_2_ = f32[4,64,256]{2,1,0:T(8,128)S(1)} collective-permute-done((f32[4,64,256]{2,1,0:T(8,128)S(1)}, f32[4,64,256]{2,1,0:T(8,128)S(1)}, u32[]{:S(2)}, u32[]{:S(2)}) %collective-permute-start.20) | collective-permute-done | bytes 262176 | tf_op jit(solution)/shard_map/ppermute | solution.py:22
  94.0 0.1 collective-permute-start.22
  94.1 0.1 add.12
  94.2 3.2 %collective-permute-start.23 = (f32[1024,256]{1,0:T(8,128)S(1)}, f32[1024,256]{1,0:T(8,128)S(1)}, u32[]{:S(2)}, u32[]{:S(2)}) collective-permute-start(f32[1024,256]{1,0:T(8,128)S(1)} %add.12), channel_id=1, source_target_pairs={{0,1},{1,2},{2,3},{3,0},{4,5},{5,6},{6,7},{7,4},{8,9},{9,10},{10,1... | collective-permute-start | bytes 3145736 | tf_op jit(solution)/shard_map/ppermute | solution.py:22
  97.5 4.1 %collective-permute-done.21.refs_3_ = f32[4,64,256]{2,1,0:T(8,128)S(1)} collective-permute-done((f32[4,64,256]{2,1,0:T(8,128)S(1)}, f32[4,64,256]{2,1,0:T(8,128)S(1)}, u32[]{:S(2)}, u32[]{:S(2)}) %collective-permute-start.21) | collective-permute-done | bytes 262176 | tf_op jit(solution)/shard_map/ppermute | solution.py:22
  101.6 0.1 split_b.3
  101.7 3.4 %product.3 = (f32[1024,256]{1,0:T(8,128)S(1)}, f32[1024,256]{1,0:T(8,128)S(1)}) custom-call(bf16[2,1024,768]{2,1,0:T(8,128)(2,1)S(1)} %get-tuple-element.73.high, bf16[2,1024,768]{2,1,0:T(8,128)(2,1)S(1)} %get-tuple-element.74.low, bf16[2,1024,256]{2,1,0:T(8,128)(2,1)S(1)} %get-tuple-element.82.far_high, ...), custom_call_target="tpu_custom_call" | custom-call | flops 3221225472 | bytes 2097152 | tf_op jit(solution)/shard_map/product/pallas_call | solution.py:345
  105.1 0.2 add_add_fusion
  105.4 0.1 collective-permute-start.27
  105.5 8.1 %collective-permute-done.22.top3 = f32[1024,256]{1,0:T(8,128)S(1)} collective-permute-done((f32[1024,256]{1,0:T(8,128)S(1)}, f32[1024,256]{1,0:T(8,128)S(1)}, u32[]{:S(2)}, u32[]{:S(2)}) %collective-permute-start.22) | collective-permute-done | bytes 1048608 | tf_op jit(solution)/shard_map/ppermute | solution.py:22
  113.6 1.9 %finish.1 = f32[1024,512]{1,0:T(8,128)} custom-call(s32[4]{0:T(128)S(1)} %pad_add_fusion.place, f32[1024,256]{1,0:T(8,128)S(1)} %get-tuple-element.90.top0, f32[1024,256]{1,0:T(8,128)S(1)} %collective-permute-done.22.top3, f32[1024,256]{1,0:T(8,128)S(1)} %collective-permute-done.23.top1, f32[1024,256]{1,0:T(8,128)S(1)} %collective-permute-done.27.got), custom_call_target="tpu_custom_call" | custom-call | tf_op jit(solution)/shard_map/finish/pallas_call | solution.py:377
  (15 shorter events, 0.1 us)
Async XLA Ops:
  0.1 1.2 %copy-start = (f32[32,8192]{1,0:T(8,128)S(1)}, f32[32,8192]{1,0:T(8,128)}, u32[]{:S(2)}) copy-start(f32[32,8192]{1,0:T(8,128)} %a_ref.1) | copy-start | bytes 3145732
  1.9 2.6 %collective-permute-start = (f32[2,2,32,1024]{3,2,1,0:T(8,128)S(1)}, f32[2,2,32,1024]{3,2,1,0:T(8,128)S(1)}, u32[]{:S(2)}, u32[]{:S(2)}) collective-permute-start(f32[2,2,32,1024]{3,2,1,0:T(8,128)S(1)} %get-tuple-element.52), channel_id=1, source_target_pairs={{0,16},{1,17},{2,18},{3,19},{4,20},{5,21},{6,22},{7,23},{8,24},{9,... | collective-permute-start | bytes 1572872 | tf_op jit(solution)/shard_map/ppermute | solution.py:22
  2.0 1.2 %copy-start.1 = (f32[32,8192]{1,0:T(8,128)S(1)}, f32[32,8192]{1,0:T(8,128)}, u32[]{:S(2)}) copy-start(f32[32,8192]{1,0:T(8,128)} %b_ref.1) | copy-start | bytes 3145732
  4.0 6.2 %collective-permute-start.3 = (f32[4,32,1024]{2,1,0:T(8,128)S(1)}, f32[4,32,1024]{2,1,0:T(8,128)S(1)}, u32[]{:S(2)}, u32[]{:S(2)}) collective-permute-start(f32[4,32,1024]{2,1,0:T(8,128)S(1)} %get-tuple-element.56), channel_id=1, source_target_pairs={{0,16},{1,17},{2,18},{3,19},{4,20},{5,21},{6,22},{7,23},{8,24},{9,... | collective-permute-start | bytes 1572872 | tf_op jit(solution)/shard_map/ppermute | solution.py:22
  4.6 18.4 %collective-permute-start.2 = (f32[2,64,1024]{2,1,0:T(8,128)S(1)}, f32[2,64,1024]{2,1,0:T(8,128)S(1)}, u32[]{:S(2)}, u32[]{:S(2)}) collective-permute-start(f32[2,64,1024]{2,1,0:T(8,128)S(1)} %join_a.1), channel_id=1, source_target_pairs={{0,32},{1,33},{2,34},{3,35},{4,36},{5,37},{6,38},{7,39},{8,40},{9,... | collective-permute-start | bytes 1572872 | tf_op jit(solution)/shard_map/ppermute | solution.py:22
  6.6 16.4 %collective-permute-start.1 = (f32[2,32,1024]{2,1,0:T(8,128)S(1)}, f32[2,32,1024]{2,1,0:T(8,128)S(1)}, u32[]{:S(2)}, u32[]{:S(2)}) collective-permute-start(f32[2,32,1024]{2,1,0:T(8,128)S(1)} %get-tuple-element.53), channel_id=1, source_target_pairs={{0,64},{1,65},{2,66},{3,67},{4,68},{5,69},{6,70},{7,71},{8,72},{9,... | collective-permute-start | bytes 786440 | tf_op jit(solution)/shard_map/ppermute | solution.py:22
  10.3 12.7 %collective-permute-start.4 = (f32[64,1024]{1,0:T(8,128)S(1)}, f32[64,1024]{1,0:T(8,128)S(1)}, u32[]{:S(2)}, u32[]{:S(2)}) collective-permute-start(f32[64,1024]{1,0:T(8,128)S(1)} %get-tuple-element.58), channel_id=1, source_target_pairs={{0,4},{1,5},{2,6},{3,7},{4,8},{5,9},{6,10},{7,11},{8,12},{9,13},{1... | collective-permute-start | bytes 786440 | tf_op jit(solution)/shard_map/ppermute | solution.py:22
  11.9 11.1 %collective-permute-start.5 = (f32[64,1024]{1,0:T(8,128)S(1)}, f32[64,1024]{1,0:T(8,128)S(1)}, u32[]{:S(2)}, u32[]{:S(2)}) collective-permute-start(f32[64,1024]{1,0:T(8,128)S(1)} %get-tuple-element.59), channel_id=1, source_target_pairs={{0,8},{1,9},{2,10},{3,11},{4,12},{5,13},{6,14},{7,15},{8,0},{9,1},... | collective-permute-start | bytes 786440 | tf_op jit(solution)/shard_map/ppermute | solution.py:22
  14.8 8.2 %collective-permute-start.6 = (f32[64,1024]{1,0:T(8,128)S(1)}, f32[64,1024]{1,0:T(8,128)S(1)}, u32[]{:S(2)}, u32[]{:S(2)}) collective-permute-start(f32[64,1024]{1,0:T(8,128)S(1)} %get-tuple-element.60), channel_id=1, source_target_pairs={{0,12},{1,13},{2,14},{3,15},{4,0},{5,1},{6,2},{7,3},{8,4},{9,5},{1... | collective-permute-start | bytes 786440 | tf_op jit(solution)/shard_map/ppermute | solution.py:22
  23.0 2.4 %collective-permute-start.8 = (f32[2,64,1024]{2,1,0:T(8,128)S(1)}, f32[2,64,1024]{2,1,0:T(8,128)S(1)}, u32[]{:S(2)}, u32[]{:S(2)}) collective-permute-start(f32[2,64,1024]{2,1,0:T(8,128)S(1)} %collective-permute-done.2.side), channel_id=1, source_target_pairs={{0,16},{1,17},{2,18},{3,19},{4,20},{5,21},{6,22},{7,23},{8,24},{9,... | collective-permute-start | bytes 1572872 | tf_op jit(solution)/shard_map/ppermute | solution.py:22
  23.1 2.3 %collective-permute-start.7 = (f32[2,32,1024]{2,1,0:T(8,128)S(1)}, f32[2,32,1024]{2,1,0:T(8,128)S(1)}, u32[]{:S(2)}, u32[]{:S(2)}) collective-permute-start(f32[2,32,1024]{2,1,0:T(8,128)S(1)} %collective-permute-done.1.two), channel_id=1, source_target_pairs={{0,16},{1,17},{2,18},{3,19},{4,20},{5,21},{6,22},{7,23},{8,24},{9,... | collective-permute-start | bytes 786440 | tf_op jit(solution)/shard_map/ppermute | solution.py:22
  25.3 13.2 %collective-permute-start.15 = (f32[4,64,768]{2,1,0:T(8,128)S(1)}, f32[4,64,768]{2,1,0:T(8,128)S(1)}, u32[]{:S(2)}, u32[]{:S(2)}) collective-permute-start(f32[4,64,768]{2,1,0:T(8,128)S(1)} %get-tuple-element.75.refs_0_), channel_id=1, source_target_pairs={{0,32},{1,33},{2,34},{3,35},{4,36},{5,37},{6,38},{7,39},{8,40},{9,... | collective-permute-start | bytes 2359304 | tf_op jit(solution)/shard_map/ppermute | solution.py:22
  25.5 16.1 %collective-permute-start.9 = (f32[256,1024]{1,0:T(8,128)S(1)}, f32[256,1024]{1,0:T(8,128)S(1)}, u32[]{:S(2)}, u32[]{:S(2)}) collective-permute-start(f32[256,1024]{1,0:T(8,128)S(1)} %get-tuple-element.71.refs_0_), channel_id=1, source_target_pairs={{0,4},{1,5},{2,6},{3,7},{4,8},{5,9},{6,10},{7,11},{8,12},{9,13},{1... | collective-permute-start | bytes 3145736 | tf_op jit(solution)/shard_map/ppermute | solution.py:22
  27.1 15.0 %collective-permute-start.12 = (f32[256,1024]{1,0:T(8,128)S(1)}, f32[256,1024]{1,0:T(8,128)S(1)}, u32[]{:S(2)}, u32[]{:S(2)}) collective-permute-start(f32[256,1024]{1,0:T(8,128)S(1)} %get-tuple-element.72.refs_3_), channel_id=1, source_target_pairs={{0,12},{1,13},{2,14},{3,15},{4,0},{5,1},{6,2},{7,3},{8,4},{9,5},{1... | collective-permute-start | bytes 3145736 | tf_op jit(solution)/shard_map/ppermute | solution.py:22
  38.5 13.2 %collective-permute-start.16 = (f32[4,64,768]{2,1,0:T(8,128)S(1)}, f32[4,64,768]{2,1,0:T(8,128)S(1)}, u32[]{:S(2)}, u32[]{:S(2)}) collective-permute-start(f32[4,64,768]{2,1,0:T(8,128)S(1)} %collective-permute-done.15.refs_1_), channel_id=1, source_target_pairs={{0,32},{1,33},{2,34},{3,35},{4,36},{5,37},{6,38},{7,39},{8,40},{9,... | collective-permute-start | bytes 2359304 | tf_op jit(solution)/shard_map/ppermute | solution.py:22
  38.5 15.3 %collective-permute-start.10 = (f32[256,1024]{1,0:T(8,128)S(1)}, f32[256,1024]{1,0:T(8,128)S(1)}, u32[]{:S(2)}, u32[]{:S(2)}) collective-permute-start(f32[256,1024]{1,0:T(8,128)S(1)} %get-tuple-element.71.refs_0_), channel_id=1, source_target_pairs={{0,12},{1,13},{2,14},{3,15},{4,0},{5,1},{6,2},{7,3},{8,4},{9,5},{1... | collective-permute-start | bytes 3145736 | tf_op jit(solution)/shard_map/ppermute | solution.py:22
  41.6 16.0 %collective-permute-start.11 = (f32[256,1024]{1,0:T(8,128)S(1)}, f32[256,1024]{1,0:T(8,128)S(1)}, u32[]{:S(2)}, u32[]{:S(2)}) collective-permute-start(f32[256,1024]{1,0:T(8,128)S(1)} %get-tuple-element.72.refs_3_), channel_id=1, source_target_pairs={{0,4},{1,5},{2,6},{3,7},{4,8},{5,9},{6,10},{7,11},{8,12},{9,13},{1... | collective-permute-start | bytes 3145736 | tf_op jit(solution)/shard_map/ppermute | solution.py:22
  41.6 27.2 %collective-permute-start.13 = (f32[256,1024]{1,0:T(8,128)S(1)}, f32[256,1024]{1,0:T(8,128)S(1)}, u32[]{:S(2)}, u32[]{:S(2)}) collective-permute-start(f32[256,1024]{1,0:T(8,128)S(1)} %collective-permute-done.9.refs_1_), channel_id=1, source_target_pairs={{0,4},{1,5},{2,6},{3,7},{4,8},{5,9},{6,10},{7,11},{8,12},{9,13},{1... | collective-permute-start | bytes 3145736 | tf_op jit(solution)/shard_map/ppermute | solution.py:22
  42.2 26.7 %collective-permute-start.14 = (f32[256,1024]{1,0:T(8,128)S(1)}, f32[256,1024]{1,0:T(8,128)S(1)}, u32[]{:S(2)}, u32[]{:S(2)}) collective-permute-start(f32[256,1024]{1,0:T(8,128)S(1)} %collective-permute-done.12.refs_5_), channel_id=1, source_target_pairs={{0,12},{1,13},{2,14},{3,15},{4,0},{5,1},{6,2},{7,3},{8,4},{9,5},{1... | collective-permute-start | bytes 3145736 | tf_op jit(solution)/shard_map/ppermute | solution.py:22
  51.7 13.2 %collective-permute-start.17 = (f32[4,64,768]{2,1,0:T(8,128)S(1)}, f32[4,64,768]{2,1,0:T(8,128)S(1)}, u32[]{:S(2)}, u32[]{:S(2)}) collective-permute-start(f32[4,64,768]{2,1,0:T(8,128)S(1)} %collective-permute-done.16.refs_2_), channel_id=1, source_target_pairs={{0,32},{1,33},{2,34},{3,35},{4,36},{5,37},{6,38},{7,39},{8,40},{9,... | collective-permute-start | bytes 2359304 | tf_op jit(solution)/shard_map/ppermute | solution.py:22
  70.0 16.1 %collective-permute-start.25 = (f32[1024,256]{1,0:T(8,128)S(1)}, f32[1024,256]{1,0:T(8,128)S(1)}, u32[]{:S(2)}, u32[]{:S(2)}) collective-permute-start(f32[1024,256]{1,0:T(8,128)S(1)} %get-tuple-element.96), channel_id=1, source_target_pairs={{0,3},{1,0},{2,1},{3,2},{4,7},{5,4},{6,5},{7,6},{8,11},{9,8},{10,9... | collective-permute-start | bytes 3145736 | tf_op jit(solution)/shard_map/ppermute | solution.py:22
  70.9 23.1 %collective-permute-start.19 = (f32[1024,256]{1,0:T(8,128)S(1)}, f32[1024,256]{1,0:T(8,128)S(1)}, u32[]{:S(2)}, u32[]{:S(2)}) collective-permute-start(f32[1024,256]{1,0:T(8,128)S(1)} %get-tuple-element.85), channel_id=1, source_target_pairs={{0,1},{1,2},{2,3},{3,0},{4,5},{5,6},{6,7},{7,4},{8,9},{9,10},{10,1... | collective-permute-start | bytes 3145736 | tf_op jit(solution)/shard_map/ppermute | solution.py:22
  73.4 13.0 %collective-permute-start.18 = (f32[4,64,256]{2,1,0:T(8,128)S(1)}, f32[4,64,256]{2,1,0:T(8,128)S(1)}, u32[]{:S(2)}, u32[]{:S(2)}) collective-permute-start(f32[4,64,256]{2,1,0:T(8,128)S(1)} %get-tuple-element.84.refs_0_), channel_id=1, source_target_pairs={{0,32},{1,33},{2,34},{3,35},{4,36},{5,37},{6,38},{7,39},{8,40},{9,... | collective-permute-start | bytes 786440 | tf_op jit(solution)/shard_map/ppermute | solution.py:22
  80.2 25.0 %collective-permute-start.24 = (f32[1024,256]{1,0:T(8,128)S(1)}, f32[1024,256]{1,0:T(8,128)S(1)}, u32[]{:S(2)}, u32[]{:S(2)}) collective-permute-start(f32[1024,256]{1,0:T(8,128)S(1)} %get-tuple-element.94), channel_id=1, source_target_pairs={{0,1},{1,2},{2,3},{3,0},{4,5},{5,6},{6,7},{7,4},{8,9},{9,10},{10,1... | collective-permute-start | bytes 3145736 | tf_op jit(solution)/shard_map/ppermute | solution.py:22
  86.3 18.9 %collective-permute-start.26 = (f32[1024,256]{1,0:T(8,128)S(1)}, f32[1024,256]{1,0:T(8,128)S(1)}, u32[]{:S(2)}, u32[]{:S(2)}) collective-permute-start(f32[1024,256]{1,0:T(8,128)S(1)} %add.14), channel_id=1, source_target_pairs={{0,3},{1,0},{2,1},{3,2},{4,7},{5,4},{6,5},{7,6},{8,11},{9,8},{10,9... | collective-permute-start | bytes 3145736 | tf_op jit(solution)/shard_map/ppermute | solution.py:22
  86.4 7.7 %collective-permute-start.20 = (f32[4,64,256]{2,1,0:T(8,128)S(1)}, f32[4,64,256]{2,1,0:T(8,128)S(1)}, u32[]{:S(2)}, u32[]{:S(2)}) collective-permute-start(f32[4,64,256]{2,1,0:T(8,128)S(1)} %collective-permute-done.18.refs_1_), channel_id=1, source_target_pairs={{0,32},{1,33},{2,34},{3,35},{4,36},{5,37},{6,38},{7,39},{8,40},{9,... | collective-permute-start | bytes 786440 | tf_op jit(solution)/shard_map/ppermute | solution.py:22
  94.0 7.6 %collective-permute-start.21 = (f32[4,64,256]{2,1,0:T(8,128)S(1)}, f32[4,64,256]{2,1,0:T(8,128)S(1)}, u32[]{:S(2)}, u32[]{:S(2)}) collective-permute-start(f32[4,64,256]{2,1,0:T(8,128)S(1)} %collective-permute-done.20.refs_2_), channel_id=1, source_target_pairs={{0,32},{1,33},{2,34},{3,35},{4,36},{5,37},{6,38},{7,39},{8,40},{9,... | collective-permute-start | bytes 786440 | tf_op jit(solution)/shard_map/ppermute | solution.py:22
  94.0 19.6 %collective-permute-start.22 = (f32[1024,256]{1,0:T(8,128)S(1)}, f32[1024,256]{1,0:T(8,128)S(1)}, u32[]{:S(2)}, u32[]{:S(2)}) collective-permute-start(f32[1024,256]{1,0:T(8,128)S(1)} %get-tuple-element.91), channel_id=1, source_target_pairs={{0,3},{1,0},{2,1},{3,2},{4,7},{5,4},{6,5},{7,6},{8,11},{9,8},{10,9... | collective-permute-start | bytes 3145736 | tf_op jit(solution)/shard_map/ppermute | solution.py:22
  94.2 19.4 %collective-permute-start.23 = (f32[1024,256]{1,0:T(8,128)S(1)}, f32[1024,256]{1,0:T(8,128)S(1)}, u32[]{:S(2)}, u32[]{:S(2)}) collective-permute-start(f32[1024,256]{1,0:T(8,128)S(1)} %add.12), channel_id=1, source_target_pairs={{0,1},{1,2},{2,3},{3,0},{4,5},{5,6},{6,7},{7,4},{8,9},{9,10},{10,1... | collective-permute-start | bytes 3145736 | tf_op jit(solution)/shard_map/ppermute | solution.py:22
  105.4 8.2 %collective-permute-start.27 = (f32[1024,256]{1,0:T(8,128)S(1)}, f32[1024,256]{1,0:T(8,128)S(1)}, u32[]{:S(2)}, u32[]{:S(2)}) collective-permute-start(f32[1024,256]{1,0:T(8,128)S(1)} %add_add_fusion), channel_id=1, source_target_pairs={{0,16},{1,17},{2,18},{3,19},{4,20},{5,21},{6,22},{7,23},{8,24},{9,... | collective-permute-start | bytes 3145736 | tf_op jit(solution)/shard_map/ppermute | solution.py:22

commit v6 on v5

--- a/solution.py
+++ b/solution.py
@@ -403,7 +403,6 @@
 
     two_got, side_got = swap(two), swap(side)
     panels = make_panels(blocks)
-    two_got, side_got, panels = lax.optimization_barrier((two_got, side_got, panels))
     panels, later = [panels[0]], [panels[1]]
     for _ in range(N - 1):
         panels.append(along_z(panels[-1], 1))

time: 116 us -> 114 us (0.983)
  waiting for transfers between devices: 63.2 us -> 61 us
    ppermute x28, waiting for transfers between devices: 63.2 us -> 61 us  [permute(): return lax.ppermute(value, ALL, pairs)]
  transfers between devices with their start and end apart: 28 -> 28, of which waited for: 12 -> 13; matrix products, arithmetic and copies ran while one was open for 0% -> 0% of each run, Pallas kernels for 14% -> 14%
where the time goes in v6:
time: 114 us
  waiting for transfers between devices  61 us (54%)
  starting transfers between devices  29.3 us (26%)
  Pallas kernels  19.8 us (17%)
  local copies, waits for them, and re-layouts  2.45 us (2%)
    ppermute x28, waiting for transfers between devices, permute(): return lax.ppermute(value, ALL, pairs)  61 us
    ppermute x28, starting transfers between devices, permute(): return lax.ppermute(value, ALL, pairs)  29.3 us
    pallas_call x3, Pallas kernels, product(): pl.pallas_call(functools.partial(product_kernel, tasks), out_shape=(out,...  10.2 us
    pallas_call x1, Pallas kernels, near_product(): pl.pallas_call(near_kernel, out_shape=(out, out), in_specs=[VMEM] * 4, ou...  2.59 us
    unnamed x4, local copies, waits for them, and re-layouts  2.45 us
  transfers between devices with their start and end apart: 28, of which 13 were waited for; matrix products, arithmetic and copies ran while one was open for 0% of the time, Pallas kernels for 14%

profile of v6, /device:TPU:6, one launch (start us, length us, event | category | flops | bytes accessed | tf_op | source)
XLA Modules:
  0.0 113.5 jit_solution(5181379079432857532)
XLA Ops:
  0.0 0.1 pad_add_fusion.place
  0.1 1.2 %copy-done = f32[32,8192]{1,0:T(8,128)S(1)} copy-done((f32[32,8192]{1,0:T(8,128)S(1)}, f32[32,8192]{1,0:T(8,128)}, u32[]{:S(2)}) %copy-start) | copy-done | bytes 1048600
  1.3 0.6 prepare_a.1
  1.9 0.1 collective-permute-start
  2.0 0.0 copy-start.1
  2.1 1.2 %copy-done.1 = f32[32,8192]{1,0:T(8,128)S(1)} copy-done((f32[32,8192]{1,0:T(8,128)S(1)}, f32[32,8192]{1,0:T(8,128)}, u32[]{:S(2)}) %copy-start.1) | copy-done | bytes 1048600
  3.3 0.7 prepare_b.1
  4.0 0.6 collective-permute-start.3
  4.6 0.0 collective-permute-done.got
  4.6 2.0 %collective-permute-start.2 = (f32[2,64,1024]{2,1,0:T(8,128)S(1)}, f32[2,64,1024]{2,1,0:T(8,128)S(1)}, u32[]{:S(2)}, u32[]{:S(2)}) collective-permute-start(f32[2,64,1024]{2,1,0:T(8,128)S(1)} %join_a.1), channel_id=1, source_target_pairs={{0,32},{1,33},{2,34},{3,35},{4,36},{5,37},{6,38},{7,39},{8,40},{9,... | collective-permute-start | bytes 1572872 | tf_op jit(solution)/shard_map/ppermute | solution.py:22
  6.6 3.6 %collective-permute-start.1 = (f32[2,32,1024]{2,1,0:T(8,128)S(1)}, f32[2,32,1024]{2,1,0:T(8,128)S(1)}, u32[]{:S(2)}, u32[]{:S(2)}) collective-permute-start(f32[2,32,1024]{2,1,0:T(8,128)S(1)} %get-tuple-element.49), channel_id=1, source_target_pairs={{0,64},{1,65},{2,66},{3,67},{4,68},{5,69},{6,70},{7,71},{8,72},{9,... | collective-permute-start | bytes 786440 | tf_op jit(solution)/shard_map/ppermute | solution.py:22
  10.2 0.0 collective-permute-done.3.got
  10.2 0.1 join_b.1
  10.3 1.6 %collective-permute-start.4 = (f32[64,1024]{1,0:T(8,128)S(1)}, f32[64,1024]{1,0:T(8,128)S(1)}, u32[]{:S(2)}, u32[]{:S(2)}) collective-permute-start(f32[64,1024]{1,0:T(8,128)S(1)} %get-tuple-element.54), channel_id=1, source_target_pairs={{0,4},{1,5},{2,6},{3,7},{4,8},{5,9},{6,10},{7,11},{8,12},{9,13},{1... | collective-permute-start | bytes 786440 | tf_op jit(solution)/shard_map/ppermute | solution.py:22
  11.9 2.9 %collective-permute-start.5 = (f32[64,1024]{1,0:T(8,128)S(1)}, f32[64,1024]{1,0:T(8,128)S(1)}, u32[]{:S(2)}, u32[]{:S(2)}) collective-permute-start(f32[64,1024]{1,0:T(8,128)S(1)} %get-tuple-element.55), channel_id=1, source_target_pairs={{0,8},{1,9},{2,10},{3,11},{4,12},{5,13},{6,14},{7,15},{8,0},{9,1},... | collective-permute-start | bytes 786440 | tf_op jit(solution)/shard_map/ppermute | solution.py:22
  14.8 1.3 %collective-permute-start.6 = (f32[64,1024]{1,0:T(8,128)S(1)}, f32[64,1024]{1,0:T(8,128)S(1)}, u32[]{:S(2)}, u32[]{:S(2)}) collective-permute-start(f32[64,1024]{1,0:T(8,128)S(1)} %get-tuple-element.56), channel_id=1, source_target_pairs={{0,12},{1,13},{2,14},{3,15},{4,0},{5,1},{6,2},{7,3},{8,4},{9,5},{1... | collective-permute-start | bytes 786440 | tf_op jit(solution)/shard_map/ppermute | solution.py:22
  16.1 6.8 %collective-permute-done.1.two = f32[2,32,1024]{2,1,0:T(8,128)S(1)} collective-permute-done((f32[2,32,1024]{2,1,0:T(8,128)S(1)}, f32[2,32,1024]{2,1,0:T(8,128)S(1)}, u32[]{:S(2)}, u32[]{:S(2)}) %collective-permute-start.1) | collective-permute-done | bytes 262176 | tf_op jit(solution)/shard_map/ppermute | solution.py:22
  22.9 0.0 collective-permute-done.4.refs_1_
  23.0 0.0 collective-permute-done.5.refs_2_
  23.0 0.1 collective-permute-start.8
  23.1 0.1 panel.1
  23.1 0.1 collective-permute-start.15
  23.2 0.6 collective-permute-start.7
  23.8 1.5 %collective-permute-done.7.two_got = f32[2,32,1024]{2,1,0:T(8,128)S(1)} collective-permute-done((f32[2,32,1024]{2,1,0:T(8,128)S(1)}, f32[2,32,1024]{2,1,0:T(8,128)S(1)}, u32[]{:S(2)}, u32[]{:S(2)}) %collective-permute-start.7) | collective-permute-done | bytes 262176 | tf_op jit(solution)/shard_map/ppermute | solution.py:22
  25.3 0.0 collective-permute-done.8.side_got
  25.3 0.1 stack.21
  25.5 1.6 %collective-permute-start.9 = (f32[256,1024]{1,0:T(8,128)S(1)}, f32[256,1024]{1,0:T(8,128)S(1)}, u32[]{:S(2)}, u32[]{:S(2)}) collective-permute-start(f32[256,1024]{1,0:T(8,128)S(1)} %get-tuple-element.59.refs_0_), channel_id=1, source_target_pairs={{0,4},{1,5},{2,6},{3,7},{4,8},{5,9},{6,10},{7,11},{8,12},{9,13},{1... | collective-permute-start | bytes 3145736 | tf_op jit(solution)/shard_map/ppermute | solution.py:22
  27.1 1.7 %collective-permute-start.12 = (f32[256,1024]{1,0:T(8,128)S(1)}, f32[256,1024]{1,0:T(8,128)S(1)}, u32[]{:S(2)}, u32[]{:S(2)}) collective-permute-start(f32[256,1024]{1,0:T(8,128)S(1)} %get-tuple-element.60.refs_3_), channel_id=1, source_target_pairs={{0,12},{1,13},{2,14},{3,15},{4,0},{5,1},{6,2},{7,3},{8,4},{9,5},{1... | collective-permute-start | bytes 3145736 | tf_op jit(solution)/shard_map/ppermute | solution.py:22
  28.8 7.6 %collective-permute-done.15.refs_1_ = f32[4,64,768]{2,1,0:T(8,128)S(1)} collective-permute-done((f32[4,64,768]{2,1,0:T(8,128)S(1)}, f32[4,64,768]{2,1,0:T(8,128)S(1)}, u32[]{:S(2)}, u32[]{:S(2)}) %collective-permute-start.15) | collective-permute-done | bytes 786464 | tf_op jit(solution)/shard_map/ppermute | solution.py:22
  36.4 0.0 collective-permute-start.16
  36.4 3.0 %collective-permute-start.10 = (f32[256,1024]{1,0:T(8,128)S(1)}, f32[256,1024]{1,0:T(8,128)S(1)}, u32[]{:S(2)}, u32[]{:S(2)}) collective-permute-start(f32[256,1024]{1,0:T(8,128)S(1)} %get-tuple-element.59.refs_0_), channel_id=1, source_target_pairs={{0,12},{1,13},{2,14},{3,15},{4,0},{5,1},{6,2},{7,3},{8,4},{9,5},{1... | collective-permute-start | bytes 3145736 | tf_op jit(solution)/shard_map/ppermute | solution.py:22
  39.4 0.0 collective-permute-start.11
  39.4 2.1 %collective-permute-done.9.refs_1_ = f32[256,1024]{1,0:T(8,128)S(1)} collective-permute-done((f32[256,1024]{1,0:T(8,128)S(1)}, f32[256,1024]{1,0:T(8,128)S(1)}, u32[]{:S(2)}, u32[]{:S(2)}) %collective-permute-start.9) | collective-permute-done | bytes 1048608 | tf_op jit(solution)/shard_map/ppermute | solution.py:22
  41.6 0.4 collective-permute-start.13
  41.9 2.9 %collective-permute-start.14 = (f32[256,1024]{1,0:T(8,128)S(1)}, f32[256,1024]{1,0:T(8,128)S(1)}, u32[]{:S(2)}, u32[]{:S(2)}) collective-permute-start(f32[256,1024]{1,0:T(8,128)S(1)} %collective-permute-done.12.refs_5_), channel_id=1, source_target_pairs={{0,12},{1,13},{2,14},{3,15},{4,0},{5,1},{6,2},{7,3},{8,4},{9,5},{1... | collective-permute-start | bytes 3145736 | tf_op jit(solution)/shard_map/ppermute | solution.py:22
  44.8 4.8 %collective-permute-done.16.refs_2_ = f32[4,64,768]{2,1,0:T(8,128)S(1)} collective-permute-done((f32[4,64,768]{2,1,0:T(8,128)S(1)}, f32[4,64,768]{2,1,0:T(8,128)S(1)}, u32[]{:S(2)}, u32[]{:S(2)}) %collective-permute-start.16) | collective-permute-done | bytes 786464 | tf_op jit(solution)/shard_map/ppermute | solution.py:22
  49.6 3.5 %collective-permute-done.10.refs_2_ = f32[256,1024]{1,0:T(8,128)S(1)} collective-permute-done((f32[256,1024]{1,0:T(8,128)S(1)}, f32[256,1024]{1,0:T(8,128)S(1)}, u32[]{:S(2)}, u32[]{:S(2)}) %collective-permute-start.10) | collective-permute-done | bytes 1048608 | tf_op jit(solution)/shard_map/ppermute | solution.py:22
  53.2 2.3 %collective-permute-done.11.refs_4_ = f32[256,1024]{1,0:T(8,128)S(1)} collective-permute-done((f32[256,1024]{1,0:T(8,128)S(1)}, f32[256,1024]{1,0:T(8,128)S(1)}, u32[]{:S(2)}, u32[]{:S(2)}) %collective-permute-start.11) | collective-permute-done | bytes 1048608 | tf_op jit(solution)/shard_map/ppermute | solution.py:22
  55.4 1.7 %split_a.1 = (bf16[2,1024,768]{2,1,0:T(8,128)(2,1)S(1)}, bf16[2,1024,768]{2,1,0:T(8,128)(2,1)S(1)}) custom-call(f32[256,1024]{1,0:T(8,128)S(1)} %get-tuple-element.59.refs_0_, f32[256,1024]{1,0:T(8,128)S(1)} %collective-permute-done.9.refs_1_, f32[256,1024]{1,0:T(8,128)S(1)} %collective-permute-done.10.refs_2_, f32[256,1024]{1,0:T(8,128)S(1)} %get-tuple-element.60.refs_3_, ...), custom_call_target="tpu_custom_call" | custom-call | tf_op jit(solution)/shard_map/split_a/pallas_call | solution.py:225
  57.1 5.7 %collective-permute-done.17.refs_3_ = f32[4,64,768]{2,1,0:T(8,128)S(1)} collective-permute-done((f32[4,64,768]{2,1,0:T(8,128)S(1)}, f32[4,64,768]{2,1,0:T(8,128)S(1)}, u32[]{:S(2)}, u32[]{:S(2)}) %collective-permute-start.17) | collective-permute-done | bytes 786464 | tf_op jit(solution)/shard_map/ppermute | solution.py:22
  62.8 0.4 split_b.2
  63.3 2.6 %near_product.1 = (f32[1024,256]{1,0:T(8,128)S(1)}, f32[1024,256]{1,0:T(8,128)S(1)}) custom-call(bf16[2,1024,768]{2,1,0:T(8,128)(2,1)S(1)} %get-tuple-element.61.high, bf16[2,1024,768]{2,1,0:T(8,128)(2,1)S(1)} %get-tuple-element.62.low, bf16[1024,768]{1,0:T(8,128)(2,1)S(1)} %get-tuple-element.70.bh, bf16[1024,768]{1,0:T(8,128)(2,1)S(1)} %get-tuple-element.71.bl), custom_call_target="tpu_custom_call" | custom-call | flops 2415919104 | bytes 2097152 | tf_op jit(solution)/shard_map/near_product/pallas_call | solution.py:312
  65.9 0.8 collective-permute-done.13.top
  66.7 1.2 %first_product.1 = (bf16[2,1024,256]{2,1,0:T(8,128)(2,1)S(1)}, bf16[2,1024,256]{2,1,0:T(8,128)(2,1)S(1)}, f32[1024,256]{1,0:T(8,128)S(1)}, f32[1024,256]{1,0:T(8,128)S(1)}) custom-call(f32[256,1024]{1,0:T(8,128)S(1)} %collective-permute-done.13.top, f32[256,1024]{1,0:T(8,128)S(1)} %collective-permute-done.14.bottom, ...), custom_call_target="tpu_custom_call" | custom-call | flops 805306368 | bytes 2097152 | tf_op jit(solution)/shard_map/first_product/pallas_call | solution.py:328
  67.9 0.9 collective-permute-start.25
  68.8 2.4 %collective-permute-start.19 = (f32[1024,256]{1,0:T(8,128)S(1)}, f32[1024,256]{1,0:T(8,128)S(1)}, u32[]{:S(2)}, u32[]{:S(2)}) collective-permute-start(f32[1024,256]{1,0:T(8,128)S(1)} %get-tuple-element.77), channel_id=1, source_target_pairs={{0,1},{1,2},{2,3},{3,0},{4,5},{5,6},{6,7},{7,4},{8,9},{9,10},{10,1... | collective-permute-start | bytes 3145736 | tf_op jit(solution)/shard_map/ppermute | solution.py:22
  71.2 3.4 %product.4 = (f32[1024,256]{1,0:T(8,128)S(1)}, f32[1024,256]{1,0:T(8,128)S(1)}) custom-call(bf16[2,1024,768]{2,1,0:T(8,128)(2,1)S(1)} %get-tuple-element.61.high, bf16[2,1024,768]{2,1,0:T(8,128)(2,1)S(1)} %get-tuple-element.62.low, bf16[2,1024,256]{2,1,0:T(8,128)(2,1)S(1)} %get-tuple-element.74.far_high, ...), custom_call_target="tpu_custom_call" | custom-call | flops 3221225472 | bytes 2097152 | tf_op jit(solution)/shard_map/product/pallas_call | solution.py:345
  74.6 3.4 %product.5 = (f32[1024,256]{1,0:T(8,128)S(1)}, f32[1024,256]{1,0:T(8,128)S(1)}) custom-call(bf16[2,1024,768]{2,1,0:T(8,128)(2,1)S(1)} %get-tuple-element.61.high, bf16[2,1024,768]{2,1,0:T(8,128)(2,1)S(1)} %get-tuple-element.62.low, bf16[2,1024,256]{2,1,0:T(8,128)(2,1)S(1)} %get-tuple-element.74.far_high, ...), custom_call_target="tpu_custom_call" | custom-call | flops 3221225472 | bytes 2097152 | tf_op jit(solution)/shard_map/product/pallas_call | solution.py:345
  78.0 0.1 collective-permute-start.24
  78.1 5.9 %collective-permute-done.25 = f32[1024,256]{1,0:T(8,128)S(1)} collective-permute-done((f32[1024,256]{1,0:T(8,128)S(1)}, f32[1024,256]{1,0:T(8,128)S(1)}, u32[]{:S(2)}, u32[]{:S(2)}) %collective-permute-start.25) | collective-permute-done | bytes 1048608 | tf_op jit(solution)/shard_map/ppermute | solution.py:22
  84.0 0.1 add.14
  84.1 0.1 collective-permute-start.26
  84.2 0.1 collective-permute-start.20
  84.3 7.6 %collective-permute-done.20.refs_2_ = f32[4,64,256]{2,1,0:T(8,128)S(1)} collective-permute-done((f32[4,64,256]{2,1,0:T(8,128)S(1)}, f32[4,64,256]{2,1,0:T(8,128)S(1)}, u32[]{:S(2)}, u32[]{:S(2)}) %collective-permute-start.20) | collective-permute-done | bytes 262176 | tf_op jit(solution)/shard_map/ppermute | solution.py:22
  91.9 0.1 collective-permute-start.22
  91.9 0.1 add.12
  92.1 3.2 %collective-permute-start.23 = (f32[1024,256]{1,0:T(8,128)S(1)}, f32[1024,256]{1,0:T(8,128)S(1)}, u32[]{:S(2)}, u32[]{:S(2)}) collective-permute-start(f32[1024,256]{1,0:T(8,128)S(1)} %add.12), channel_id=1, source_target_pairs={{0,1},{1,2},{2,3},{3,0},{4,5},{5,6},{6,7},{7,4},{8,9},{9,10},{10,1... | collective-permute-start | bytes 3145736 | tf_op jit(solution)/shard_map/ppermute | solution.py:22
  95.3 4.1 %collective-permute-done.21.refs_3_ = f32[4,64,256]{2,1,0:T(8,128)S(1)} collective-permute-done((f32[4,64,256]{2,1,0:T(8,128)S(1)}, f32[4,64,256]{2,1,0:T(8,128)S(1)}, u32[]{:S(2)}, u32[]{:S(2)}) %collective-permute-start.21) | collective-permute-done | bytes 262176 | tf_op jit(solution)/shard_map/ppermute | solution.py:22
  99.5 0.1 split_b.3
  99.6 3.4 %product.3 = (f32[1024,256]{1,0:T(8,128)S(1)}, f32[1024,256]{1,0:T(8,128)S(1)}) custom-call(bf16[2,1024,768]{2,1,0:T(8,128)(2,1)S(1)} %get-tuple-element.61.high, bf16[2,1024,768]{2,1,0:T(8,128)(2,1)S(1)} %get-tuple-element.62.low, bf16[2,1024,256]{2,1,0:T(8,128)(2,1)S(1)} %get-tuple-element.74.far_high, ...), custom_call_target="tpu_custom_call" | custom-call | flops 3221225472 | bytes 2097152 | tf_op jit(solution)/shard_map/product/pallas_call | solution.py:345
  103.0 0.2 add_add_fusion
  103.2 0.1 collective-permute-start.27
  103.3 8.1 %collective-permute-done.22.top3 = f32[1024,256]{1,0:T(8,128)S(1)} collective-permute-done((f32[1024,256]{1,0:T(8,128)S(1)}, f32[1024,256]{1,0:T(8,128)S(1)}, u32[]{:S(2)}, u32[]{:S(2)}) %collective-permute-start.22) | collective-permute-done | bytes 1048608 | tf_op jit(solution)/shard_map/ppermute | solution.py:22
  111.4 1.9 %finish.1 = f32[1024,512]{1,0:T(8,128)} custom-call(s32[4]{0:T(128)S(1)} %pad_add_fusion.place, f32[1024,256]{1,0:T(8,128)S(1)} %get-tuple-element.82.top0, f32[1024,256]{1,0:T(8,128)S(1)} %collective-permute-done.22.top3, f32[1024,256]{1,0:T(8,128)S(1)} %collective-permute-done.23.top1, f32[1024,256]{1,0:T(8,128)S(1)} %collective-permute-done.27.got), custom_call_target="tpu_custom_call" | custom-call | tf_op jit(solution)/shard_map/finish/pallas_call | solution.py:377
  (15 shorter events, 0.1 us)
Async XLA Ops:
  0.1 1.2 %copy-start = (f32[32,8192]{1,0:T(8,128)S(1)}, f32[32,8192]{1,0:T(8,128)}, u32[]{:S(2)}) copy-start(f32[32,8192]{1,0:T(8,128)} %a_ref.1) | copy-start | bytes 3145732
  1.9 2.6 %collective-permute-start = (f32[2,2,32,1024]{3,2,1,0:T(8,128)S(1)}, f32[2,2,32,1024]{3,2,1,0:T(8,128)S(1)}, u32[]{:S(2)}, u32[]{:S(2)}) collective-permute-start(f32[2,2,32,1024]{3,2,1,0:T(8,128)S(1)} %get-tuple-element.48), channel_id=1, source_target_pairs={{0,16},{1,17},{2,18},{3,19},{4,20},{5,21},{6,22},{7,23},{8,24},{9,... | collective-permute-start | bytes 1572872 | tf_op jit(solution)/shard_map/ppermute | solution.py:22
  2.0 1.2 %copy-start.1 = (f32[32,8192]{1,0:T(8,128)S(1)}, f32[32,8192]{1,0:T(8,128)}, u32[]{:S(2)}) copy-start(f32[32,8192]{1,0:T(8,128)} %b_ref.1) | copy-start | bytes 3145732
  4.0 6.2 %collective-permute-start.3 = (f32[4,32,1024]{2,1,0:T(8,128)S(1)}, f32[4,32,1024]{2,1,0:T(8,128)S(1)}, u32[]{:S(2)}, u32[]{:S(2)}) collective-permute-start(f32[4,32,1024]{2,1,0:T(8,128)S(1)} %get-tuple-element.52), channel_id=1, source_target_pairs={{0,16},{1,17},{2,18},{3,19},{4,20},{5,21},{6,22},{7,23},{8,24},{9,... | collective-permute-start | bytes 1572872 | tf_op jit(solution)/shard_map/ppermute | solution.py:22
  4.6 18.4 %collective-permute-start.2 = (f32[2,64,1024]{2,1,0:T(8,128)S(1)}, f32[2,64,1024]{2,1,0:T(8,128)S(1)}, u32[]{:S(2)}, u32[]{:S(2)}) collective-permute-start(f32[2,64,1024]{2,1,0:T(8,128)S(1)} %join_a.1), channel_id=1, source_target_pairs={{0,32},{1,33},{2,34},{3,35},{4,36},{5,37},{6,38},{7,39},{8,40},{9,... | collective-permute-start | bytes 1572872 | tf_op jit(solution)/shard_map/ppermute | solution.py:22
  6.6 16.4 %collective-permute-start.1 = (f32[2,32,1024]{2,1,0:T(8,128)S(1)}, f32[2,32,1024]{2,1,0:T(8,128)S(1)}, u32[]{:S(2)}, u32[]{:S(2)}) collective-permute-start(f32[2,32,1024]{2,1,0:T(8,128)S(1)} %get-tuple-element.49), channel_id=1, source_target_pairs={{0,64},{1,65},{2,66},{3,67},{4,68},{5,69},{6,70},{7,71},{8,72},{9,... | collective-permute-start | bytes 786440 | tf_op jit(solution)/shard_map/ppermute | solution.py:22
  10.3 12.7 %collective-permute-start.4 = (f32[64,1024]{1,0:T(8,128)S(1)}, f32[64,1024]{1,0:T(8,128)S(1)}, u32[]{:S(2)}, u32[]{:S(2)}) collective-permute-start(f32[64,1024]{1,0:T(8,128)S(1)} %get-tuple-element.54), channel_id=1, source_target_pairs={{0,4},{1,5},{2,6},{3,7},{4,8},{5,9},{6,10},{7,11},{8,12},{9,13},{1... | collective-permute-start | bytes 786440 | tf_op jit(solution)/shard_map/ppermute | solution.py:22
  11.9 11.1 %collective-permute-start.5 = (f32[64,1024]{1,0:T(8,128)S(1)}, f32[64,1024]{1,0:T(8,128)S(1)}, u32[]{:S(2)}, u32[]{:S(2)}) collective-permute-start(f32[64,1024]{1,0:T(8,128)S(1)} %get-tuple-element.55), channel_id=1, source_target_pairs={{0,8},{1,9},{2,10},{3,11},{4,12},{5,13},{6,14},{7,15},{8,0},{9,1},... | collective-permute-start | bytes 786440 | tf_op jit(solution)/shard_map/ppermute | solution.py:22
  14.8 8.2 %collective-permute-start.6 = (f32[64,1024]{1,0:T(8,128)S(1)}, f32[64,1024]{1,0:T(8,128)S(1)}, u32[]{:S(2)}, u32[]{:S(2)}) collective-permute-start(f32[64,1024]{1,0:T(8,128)S(1)} %get-tuple-element.56), channel_id=1, source_target_pairs={{0,12},{1,13},{2,14},{3,15},{4,0},{5,1},{6,2},{7,3},{8,4},{9,5},{1... | collective-permute-start | bytes 786440 | tf_op jit(solution)/shard_map/ppermute | solution.py:22
  23.0 2.4 %collective-permute-start.8 = (f32[2,64,1024]{2,1,0:T(8,128)S(1)}, f32[2,64,1024]{2,1,0:T(8,128)S(1)}, u32[]{:S(2)}, u32[]{:S(2)}) collective-permute-start(f32[2,64,1024]{2,1,0:T(8,128)S(1)} %collective-permute-done.2.side), channel_id=1, source_target_pairs={{0,16},{1,17},{2,18},{3,19},{4,20},{5,21},{6,22},{7,23},{8,24},{9,... | collective-permute-start | bytes 1572872 | tf_op jit(solution)/shard_map/ppermute | solution.py:22
  23.1 13.3 %collective-permute-start.15 = (f32[4,64,768]{2,1,0:T(8,128)S(1)}, f32[4,64,768]{2,1,0:T(8,128)S(1)}, u32[]{:S(2)}, u32[]{:S(2)}) collective-permute-start(f32[4,64,768]{2,1,0:T(8,128)S(1)} %get-tuple-element.67.refs_0_), channel_id=1, source_target_pairs={{0,32},{1,33},{2,34},{3,35},{4,36},{5,37},{6,38},{7,39},{8,40},{9,... | collective-permute-start | bytes 2359304 | tf_op jit(solution)/shard_map/ppermute | solution.py:22
  23.2 2.1 %collective-permute-start.7 = (f32[2,32,1024]{2,1,0:T(8,128)S(1)}, f32[2,32,1024]{2,1,0:T(8,128)S(1)}, u32[]{:S(2)}, u32[]{:S(2)}) collective-permute-start(f32[2,32,1024]{2,1,0:T(8,128)S(1)} %collective-permute-done.1.two), channel_id=1, source_target_pairs={{0,16},{1,17},{2,18},{3,19},{4,20},{5,21},{6,22},{7,23},{8,24},{9,... | collective-permute-start | bytes 786440 | tf_op jit(solution)/shard_map/ppermute | solution.py:22
  25.5 16.1 %collective-permute-start.9 = (f32[256,1024]{1,0:T(8,128)S(1)}, f32[256,1024]{1,0:T(8,128)S(1)}, u32[]{:S(2)}, u32[]{:S(2)}) collective-permute-start(f32[256,1024]{1,0:T(8,128)S(1)} %get-tuple-element.59.refs_0_), channel_id=1, source_target_pairs={{0,4},{1,5},{2,6},{3,7},{4,8},{5,9},{6,10},{7,11},{8,12},{9,13},{1... | collective-permute-start | bytes 3145736 | tf_op jit(solution)/shard_map/ppermute | solution.py:22
  27.1 14.8 %collective-permute-start.12 = (f32[256,1024]{1,0:T(8,128)S(1)}, f32[256,1024]{1,0:T(8,128)S(1)}, u32[]{:S(2)}, u32[]{:S(2)}) collective-permute-start(f32[256,1024]{1,0:T(8,128)S(1)} %get-tuple-element.60.refs_3_), channel_id=1, source_target_pairs={{0,12},{1,13},{2,14},{3,15},{4,0},{5,1},{6,2},{7,3},{8,4},{9,5},{1... | collective-permute-start | bytes 3145736 | tf_op jit(solution)/shard_map/ppermute | solution.py:22
  36.4 13.2 %collective-permute-start.16 = (f32[4,64,768]{2,1,0:T(8,128)S(1)}, f32[4,64,768]{2,1,0:T(8,128)S(1)}, u32[]{:S(2)}, u32[]{:S(2)}) collective-permute-start(f32[4,64,768]{2,1,0:T(8,128)S(1)} %collective-permute-done.15.refs_1_), channel_id=1, source_target_pairs={{0,32},{1,33},{2,34},{3,35},{4,36},{5,37},{6,38},{7,39},{8,40},{9,... | collective-permute-start | bytes 2359304 | tf_op jit(solution)/shard_map/ppermute | solution.py:22
  36.4 16.7 %collective-permute-start.10 = (f32[256,1024]{1,0:T(8,128)S(1)}, f32[256,1024]{1,0:T(8,128)S(1)}, u32[]{:S(2)}, u32[]{:S(2)}) collective-permute-start(f32[256,1024]{1,0:T(8,128)S(1)} %get-tuple-element.59.refs_0_), channel_id=1, source_target_pairs={{0,12},{1,13},{2,14},{3,15},{4,0},{5,1},{6,2},{7,3},{8,4},{9,5},{1... | collective-permute-start | bytes 3145736 | tf_op jit(solution)/shard_map/ppermute | solution.py:22
  39.4 16.0 %collective-permute-start.11 = (f32[256,1024]{1,0:T(8,128)S(1)}, f32[256,1024]{1,0:T(8,128)S(1)}, u32[]{:S(2)}, u32[]{:S(2)}) collective-permute-start(f32[256,1024]{1,0:T(8,128)S(1)} %get-tuple-element.60.refs_3_), channel_id=1, source_target_pairs={{0,4},{1,5},{2,6},{3,7},{4,8},{5,9},{6,10},{7,11},{8,12},{9,13},{1... | collective-permute-start | bytes 3145736 | tf_op jit(solution)/shard_map/ppermute | solution.py:22
  41.6 25.1 %collective-permute-start.13 = (f32[256,1024]{1,0:T(8,128)S(1)}, f32[256,1024]{1,0:T(8,128)S(1)}, u32[]{:S(2)}, u32[]{:S(2)}) collective-permute-start(f32[256,1024]{1,0:T(8,128)S(1)} %collective-permute-done.9.refs_1_), channel_id=1, source_target_pairs={{0,4},{1,5},{2,6},{3,7},{4,8},{5,9},{6,10},{7,11},{8,12},{9,13},{1... | collective-permute-start | bytes 3145736 | tf_op jit(solution)/shard_map/ppermute | solution.py:22
  41.9 24.8 %collective-permute-start.14 = (f32[256,1024]{1,0:T(8,128)S(1)}, f32[256,1024]{1,0:T(8,128)S(1)}, u32[]{:S(2)}, u32[]{:S(2)}) collective-permute-start(f32[256,1024]{1,0:T(8,128)S(1)} %collective-permute-done.12.refs_5_), channel_id=1, source_target_pairs={{0,12},{1,13},{2,14},{3,15},{4,0},{5,1},{6,2},{7,3},{8,4},{9,5},{1... | collective-permute-start | bytes 3145736 | tf_op jit(solution)/shard_map/ppermute | solution.py:22
  49.6 13.2 %collective-permute-start.17 = (f32[4,64,768]{2,1,0:T(8,128)S(1)}, f32[4,64,768]{2,1,0:T(8,128)S(1)}, u32[]{:S(2)}, u32[]{:S(2)}) collective-permute-start(f32[4,64,768]{2,1,0:T(8,128)S(1)} %collective-permute-done.16.refs_2_), channel_id=1, source_target_pairs={{0,32},{1,33},{2,34},{3,35},{4,36},{5,37},{6,38},{7,39},{8,40},{9,... | collective-permute-start | bytes 2359304 | tf_op jit(solution)/shard_map/ppermute | solution.py:22
  67.9 16.1 %collective-permute-start.25 = (f32[1024,256]{1,0:T(8,128)S(1)}, f32[1024,256]{1,0:T(8,128)S(1)}, u32[]{:S(2)}, u32[]{:S(2)}) collective-permute-start(f32[1024,256]{1,0:T(8,128)S(1)} %get-tuple-element.88), channel_id=1, source_target_pairs={{0,3},{1,0},{2,1},{3,2},{4,7},{5,4},{6,5},{7,6},{8,11},{9,8},{10,9... | collective-permute-start | bytes 3145736 | tf_op jit(solution)/shard_map/ppermute | solution.py:22
  68.8 15.4 %collective-permute-start.18 = (f32[4,64,256]{2,1,0:T(8,128)S(1)}, f32[4,64,256]{2,1,0:T(8,128)S(1)}, u32[]{:S(2)}, u32[]{:S(2)}) collective-permute-start(f32[4,64,256]{2,1,0:T(8,128)S(1)} %get-tuple-element.76.refs_0_), channel_id=1, source_target_pairs={{0,32},{1,33},{2,34},{3,35},{4,36},{5,37},{6,38},{7,39},{8,40},{9,... | collective-permute-start | bytes 786440 | tf_op jit(solution)/shard_map/ppermute | solution.py:22
  68.8 23.1 %collective-permute-start.19 = (f32[1024,256]{1,0:T(8,128)S(1)}, f32[1024,256]{1,0:T(8,128)S(1)}, u32[]{:S(2)}, u32[]{:S(2)}) collective-permute-start(f32[1024,256]{1,0:T(8,128)S(1)} %get-tuple-element.77), channel_id=1, source_target_pairs={{0,1},{1,2},{2,3},{3,0},{4,5},{5,6},{6,7},{7,4},{8,9},{9,10},{10,1... | collective-permute-start | bytes 3145736 | tf_op jit(solution)/shard_map/ppermute | solution.py:22
  78.0 25.0 %collective-permute-start.24 = (f32[1024,256]{1,0:T(8,128)S(1)}, f32[1024,256]{1,0:T(8,128)S(1)}, u32[]{:S(2)}, u32[]{:S(2)}) collective-permute-start(f32[1024,256]{1,0:T(8,128)S(1)} %get-tuple-element.86), channel_id=1, source_target_pairs={{0,1},{1,2},{2,3},{3,0},{4,5},{5,6},{6,7},{7,4},{8,9},{9,10},{10,1... | collective-permute-start | bytes 3145736 | tf_op jit(solution)/shard_map/ppermute | solution.py:22
  84.1 18.9 %collective-permute-start.26 = (f32[1024,256]{1,0:T(8,128)S(1)}, f32[1024,256]{1,0:T(8,128)S(1)}, u32[]{:S(2)}, u32[]{:S(2)}) collective-permute-start(f32[1024,256]{1,0:T(8,128)S(1)} %add.14), channel_id=1, source_target_pairs={{0,3},{1,0},{2,1},{3,2},{4,7},{5,4},{6,5},{7,6},{8,11},{9,8},{10,9... | collective-permute-start | bytes 3145736 | tf_op jit(solution)/shard_map/ppermute | solution.py:22
  84.2 7.7 %collective-permute-start.20 = (f32[4,64,256]{2,1,0:T(8,128)S(1)}, f32[4,64,256]{2,1,0:T(8,128)S(1)}, u32[]{:S(2)}, u32[]{:S(2)}) collective-permute-start(f32[4,64,256]{2,1,0:T(8,128)S(1)} %collective-permute-done.18.refs_1_), channel_id=1, source_target_pairs={{0,32},{1,33},{2,34},{3,35},{4,36},{5,37},{6,38},{7,39},{8,40},{9,... | collective-permute-start | bytes 786440 | tf_op jit(solution)/shard_map/ppermute | solution.py:22
  91.9 7.6 %collective-permute-start.21 = (f32[4,64,256]{2,1,0:T(8,128)S(1)}, f32[4,64,256]{2,1,0:T(8,128)S(1)}, u32[]{:S(2)}, u32[]{:S(2)}) collective-permute-start(f32[4,64,256]{2,1,0:T(8,128)S(1)} %collective-permute-done.20.refs_2_), channel_id=1, source_target_pairs={{0,32},{1,33},{2,34},{3,35},{4,36},{5,37},{6,38},{7,39},{8,40},{9,... | collective-permute-start | bytes 786440 | tf_op jit(solution)/shard_map/ppermute | solution.py:22
  91.9 19.6 %collective-permute-start.22 = (f32[1024,256]{1,0:T(8,128)S(1)}, f32[1024,256]{1,0:T(8,128)S(1)}, u32[]{:S(2)}, u32[]{:S(2)}) collective-permute-start(f32[1024,256]{1,0:T(8,128)S(1)} %get-tuple-element.83), channel_id=1, source_target_pairs={{0,3},{1,0},{2,1},{3,2},{4,7},{5,4},{6,5},{7,6},{8,11},{9,8},{10,9... | collective-permute-start | bytes 3145736 | tf_op jit(solution)/shard_map/ppermute | solution.py:22
  92.1 19.4 %collective-permute-start.23 = (f32[1024,256]{1,0:T(8,128)S(1)}, f32[1024,256]{1,0:T(8,128)S(1)}, u32[]{:S(2)}, u32[]{:S(2)}) collective-permute-start(f32[1024,256]{1,0:T(8,128)S(1)} %add.12), channel_id=1, source_target_pairs={{0,1},{1,2},{2,3},{3,0},{4,5},{5,6},{6,7},{7,4},{8,9},{9,10},{10,1... | collective-permute-start | bytes 3145736 | tf_op jit(solution)/shard_map/ppermute | solution.py:22
  103.2 8.2 %collective-permute-start.27 = (f32[1024,256]{1,0:T(8,128)S(1)}, f32[1024,256]{1,0:T(8,128)S(1)}, u32[]{:S(2)}, u32[]{:S(2)}) collective-permute-start(f32[1024,256]{1,0:T(8,128)S(1)} %add_add_fusion), channel_id=1, source_target_pairs={{0,16},{1,17},{2,18},{3,19},{4,20},{5,21},{6,22},{7,23},{8,24},{9,... | collective-permute-start | bytes 3145736 | tf_op jit(solution)/shard_map/ppermute | solution.py:22
